TPU v7x, 32 devices: a whole 2x2x4 slice. The times are simulated.
32 devices in a mesh: dp: 8 (over y, x, core), tok: 4 (over z).
Axes of the slice: x: 2, y: 2, z: 4, core: 2. Of those that a mesh axis runs over, the one named last changes fastest.
Arguments:
- inputs: bfloat16 [4, 256, 2048], P('tok', 'dp'), may hold values from -6 to 6
- cotangent: bfloat16 [4, 256, 2048], P('tok', 'dp'), may hold values from -6 to 6
- norm_gain: float32 [4, 2048], P('tok'), may hold values from 0.5 to 1.5
- router_weight: bfloat16 [4, 2048, 4], P('tok'), may hold values from -0.125 to 0.125
- route_ids: int32 [4, 256, 2], P('tok'), may hold values from 0 to 3, all different within a row; in each aligned block of 256 rows (0 to 255, 256 to 511, ..., all dimensions but the last counted through in order) at most 160 rows name the same one
- w_gate: bfloat16 [4, 4, 2048, 4096], P('tok', None, None, 'dp'), may hold values from -0.125 to 0.125
- w_up: bfloat16 [4, 4, 2048, 4096], P('tok', None, None, 'dp'), may hold values from -0.125 to 0.125
- w_down: bfloat16 [4, 4, 4096, 2048], P('tok', None, 'dp'), may hold values from -0.09375 to 0.09375
Outputs:
- grad_inputs: bfloat16 [4, 256, 2048], P('tok', 'dp')
- grad_gate: bfloat16 [4, 4, 2048, 4096], P('tok', None, None, 'dp')
- grad_up: bfloat16 [4, 4, 2048, 4096], P('tok', None, None, 'dp')
- grad_down: bfloat16 [4, 4, 4096, 2048], P('tok', None, 'dp')
- grad_router: float32 [4, 2048, 4], P('tok')
- grad_gain: float32 [4, 2048], P('tok')
Inputs may be any that keep to these rules, and one draw needn't show every extreme that they name: `route_ids`: for each token the two experts of a sample differ; each expert of a token is chosen by at most 160 of its samples, a bound that some block reaches.
All inputs are finite; a program needn't handle non-finite values.
Results may differ from a plain program's by a relative error of at most 0.0095.
Values may be sent and summed in bfloat16 or wider, within the bound.
No kernel may reach another device: no remote copies, remote signals or barrier semaphores. Data moves between devices by JAX's collectives and lax.ppermute only.
A program may use at most 192 MiB of HBM per device.

v0:
```python
import functools

import jax
import jax.numpy as jnp
from jax import lax
from jax.experimental import pallas as pl
from jax.experimental.pallas import tpu as pltpu
from jax.sharding import PartitionSpec as P

BF16 = jnp.bfloat16
F32 = jnp.float32
MIB = 1024 * 1024


def dot(left, right, dims):
    return lax.dot_general(left, right, (dims, ((), ())), preferred_element_type=F32)


NN = ((1,), (0,))
NT = ((1,), (1,))
TN = ((0,), (0,))


def exchange(value, axis, distance):
    size = lax.axis_size(axis)
    return lax.ppermute(value, axis, [(i, i ^ distance) for i in range(size)])


def gather_chips(rows):
    size = lax.axis_size("dp")
    return [rows] + [exchange(rows, "dp", s) for s in range(2, size, 2)]


def gather_cores(chunks):
    return list(chunks) + [exchange(chunk, "dp", 1) for chunk in chunks]


def after(values):
    return lax.optimization_barrier(values)


def device_of(block, size):
    return 2 * block if block < size // 2 else 2 * block + 1 - size


def assemble(rows, chunks):
    for i, chunk in enumerate(chunks):
        own = chunk.shape[0]
        rows[i * own : (i + 1) * own] = chunk[...]


def head_slice(slot, width):
    return pl.ds(pl.multiple_of(slot * width, width), width)


def hbm(array):
    return pltpu.with_memory_space_constraint(array, pltpu.HBM)


def vmem(array):
    return pltpu.with_memory_space_constraint(array, pltpu.VMEM)


IN_HBM = pl.BlockSpec(memory_space=pltpu.HBM)
IN_VMEM = pl.BlockSpec(memory_space=pltpu.VMEM)
ANYWHERE = pl.BlockSpec(memory_space=pl.ANY)


def heads_kernel(x_hbm, cot_hbm, x_ref, cot_ref, *refs):
    sends, sems = refs[:-1], refs[-1]
    copy_x = pltpu.make_async_copy(x_hbm.at[0], x_ref, sems.at[0])
    copy_cot = pltpu.make_async_copy(cot_hbm.at[0], cot_ref, sems.at[1])
    copy_x.start()
    copy_cot.start()
    copy_x.wait()
    me = lax.axis_index("tok")
    width = sends[0].shape[1]
    for s, send in enumerate(sends):
        send[...] = x_ref[:, head_slice(me ^ (s + 1), width)]
    copy_cot.wait()


def split_heads(x, cotangent):
    _, rows, width = x.shape
    num_tokens = lax.axis_size("tok")
    head = jax.ShapeDtypeStruct((rows, width // num_tokens), BF16)
    return pl.pallas_call(
        heads_kernel,
        in_specs=[IN_HBM] * 2,
        out_shape=(jax.ShapeDtypeStruct((rows, width), BF16),) * 2 + (head,) * (num_tokens - 1),
        scratch_shapes=[pltpu.SemaphoreType.DMA((2,))],
        compiler_params=pltpu.CompilerParams(vmem_limit_bytes=4 * MIB),
        name="split_heads",
    )(hbm(x), hbm(cotangent))


def small_kernel(gain_hbm, router_hbm, route_hbm, gain_ref, router_ref, chosen_ref, routes, sems):
    copies = [
        pltpu.make_async_copy(src, dst, sems.at[i])
        for i, (src, dst) in enumerate(
            [
                (gain_hbm, gain_ref),
                (router_hbm, router_ref),
                (route_hbm, routes),
            ]
        )
    ]
    for copy in copies:
        copy.start()
    for copy in copies:
        copy.wait()
    rows, experts = chosen_ref.shape
    ids = lax.broadcasted_iota(jnp.int32, (experts, rows), 0)
    hit = routes[0:1, :] == ids
    for k in range(1, routes.shape[0]):
        hit = hit | (routes[k : k + 1, :] == ids)
    chosen_ref[...] = hit.astype(F32).T


def small_operands(gain, router_rows, routes):
    experts, all_rows = 8, routes.shape[1]
    return pl.pallas_call(
        small_kernel,
        in_specs=[IN_HBM] * 3,
        out_shape=(
            jax.ShapeDtypeStruct(gain.shape, F32),
            jax.ShapeDtypeStruct(router_rows.shape, BF16),
            jax.ShapeDtypeStruct((all_rows, experts), F32),
        ),
        scratch_shapes=[pltpu.VMEM(routes.shape, jnp.int32), pltpu.SemaphoreType.DMA((3,))],
        compiler_params=pltpu.CompilerParams(vmem_limit_bytes=4 * MIB),
        cost_estimate=pl.CostEstimate(flops=2**36, bytes_accessed=32 * MIB, transcendentals=0),
        name="small_operands",
    )(hbm(gain), hbm(router_rows), hbm(routes))


def norm_kernel(x_ref, gain_ref, *refs):
    heads, (normed_ref, summed_ref) = refs[:-2], refs[-2:]
    me = lax.axis_index("tok")
    width = heads[0].shape[1]
    own = head_slice(me, width)
    summed_ref[:, own] = 2.0 * x_ref[:, own].astype(F32)
    for s, head in enumerate(heads):
        place = head_slice(me ^ (s + 1), width)
        summed_ref[:, place] = x_ref[:, place].astype(F32) + head[...].astype(F32)
    summed = summed_ref[...]
    inv_rms = lax.rsqrt(jnp.mean(summed * summed, axis=1, keepdims=True) + 1e-06)
    normed_ref[...] = (summed * inv_rms * gain_ref[...]).astype(BF16)


def norm_rows(x, gain, heads):
    return pl.pallas_call(
        norm_kernel,
        out_shape=(jax.ShapeDtypeStruct(x.shape, BF16), jax.ShapeDtypeStruct(x.shape, F32)),
        compiler_params=pltpu.CompilerParams(vmem_limit_bytes=4 * MIB),
        name="norm_rows",
    )(x, gain, *heads)


def load_weights(refs, place, experts, sems):
    copies = []
    for i, (e, ref) in enumerate((e, ref) for e in experts for ref in refs):
        hidden = ref.shape[3]
        columns = pl.ds(i * hidden, hidden)
        copies.append(pltpu.make_async_copy(ref.at[0, e], place.at[:, columns], sems.at[i]))
        copies[-1].start()
    return copies


def back_kernel(size, *refs):
    chunks, (down_hbm, gate_hbm, up_hbm, back_ref, weights_ref) = refs[:size], refs[size : size + 5]
    cot, down, down_sems, sems = refs[size + 5 :]
    experts = down.shape[0]
    copies = [
        pltpu.make_async_copy(down_hbm.at[0, e], down.at[e], down_sems.at[e]) for e in range(experts)
    ]
    for copy in copies:
        copy.start()
    loads = load_weights((gate_hbm, up_hbm), weights_ref, range(experts // 2), sems)
    assemble(cot, chunks)
    for e in range(experts):
        copies[e].wait()
        back_ref[e] = dot(cot[...], down[e], NT)
    for load in loads:
        load.wait()


def back_hidden(chunks, w_down, w_gate, w_up):
    size = len(chunks)
    own, width = chunks[0].shape
    _, experts, hidden, _ = w_down.shape
    rows = size * own
    return pl.pallas_call(
        functools.partial(back_kernel, size),
        in_specs=[IN_VMEM] * size + [IN_HBM] * 3,
        out_specs=(IN_VMEM, ANYWHERE),
        out_shape=(
            jax.ShapeDtypeStruct((experts, rows, hidden), F32),
            jax.ShapeDtypeStruct((width, experts // 2 * 2 * hidden), BF16),
        ),
        scratch_shapes=[
            pltpu.VMEM((rows, width), BF16),
            pltpu.VMEM((experts, hidden, width), BF16),
            pltpu.SemaphoreType.DMA((experts,)),
            pltpu.SemaphoreType.DMA((experts // 2 * 2,)),
        ],
        compiler_params=pltpu.CompilerParams(vmem_limit_bytes=16 * MIB),
        cost_estimate=pl.CostEstimate(
            flops=2 * experts * rows * hidden * width,
            bytes_accessed=experts * hidden * (width * 4 + rows * 4) + rows * width * 2,
            transcendentals=0,
        ),
        name="back_hidden",
    )(*chunks, hbm(w_down), hbm(w_gate), hbm(w_up))


def expert_kernel(size, *refs):
    chunks, (first, gate_hbm, up_hbm, back_ref) = refs[:size], refs[size : size + 4]
    chosen_ref, router_ref, gain_ref, grads_out, act_out, sent_out = refs[size + 4 : size + 10]
    kept, (small_out, normed, second, sems) = refs[size + 10 : -4], refs[-4:]
    own, width = chunks[0].shape
    experts = router_ref.shape[0]
    hidden = back_ref.shape[2]
    split = experts // 2
    loads = load_weights((gate_hbm, up_hbm), second, range(split, experts), sems)
    assemble(normed, chunks)
    me = lax.axis_index("dp")
    hits = []
    for i in range(size):
        start = pl.multiple_of((me ^ device_of(i, size)) * own, own)
        hits.append(chosen_ref[pl.ds(start, own), :experts])
    chosen = jnp.concatenate(hits, axis=0)
    prob = jax.nn.sigmoid(dot(normed[...], router_ref[...], NT))
    gates = prob * chosen

    def forward(e):
        if e < split:
            return dot(normed[...], first[:, 2 * e * hidden : 2 * (e + 1) * hidden], NN)
        e -= split
        loads[2 * e].wait()
        loads[2 * e + 1].wait()
        return dot(normed[...], second[:, 2 * e * hidden : 2 * (e + 1) * hidden], NN)

    shares = []
    later = forward(0)
    for e in range(experts):
        pre_gate, pre_up = later[:, :hidden], later[:, hidden:]
        if e + 1 < experts:
            later = forward(e + 1)
        gate = gates[:, e : e + 1]
        back = back_ref[e]
        sigma = jax.nn.sigmoid(pre_gate)
        silu = pre_gate * sigma
        act = silu * pre_up
        shares.append(jnp.sum(act * back, axis=1, keepdims=True))
        scaled = gate * back
        grad_gate = scaled * pre_up * (sigma * (1.0 + pre_gate * (1.0 - sigma)))
        grads_out[:, 2 * e * hidden : (2 * e + 1) * hidden] = grad_gate.astype(BF16)
        grads_out[:, (2 * e + 1) * hidden : (2 * e + 2) * hidden] = (scaled * silu).astype(BF16)
        act_out[:, e * hidden : (e + 1) * hidden] = (gate * act).astype(BF16)
    coef = jnp.concatenate(shares, axis=1) * gates * (1.0 - prob)
    high = coef.astype(BF16).astype(F32)
    middle = (coef - high).astype(BF16).astype(F32)
    low = coef - high - middle
    terms = jnp.concatenate([high, middle, low], axis=1).astype(BF16)
    router = router_ref[...].astype(F32)
    router = jnp.concatenate([router] * 3, axis=0).astype(BF16)
    small = dot(terms, normed[...], TN)
    small_out[:experts] = small[:experts] + small[experts : 2 * experts] + small[2 * experts :]
    step = width // 4
    for c in range(0, width, step):
        here = slice(c, c + step)
        grad = dot(grads_out[:, : 2 * split * hidden], first[here, :], NT)
        grad = grad + dot(grads_out[:, 2 * split * hidden :], second[here, :], NT)
        grad = grad + dot(terms, router[:, here], NN)
        rows_here = normed[:, here].astype(F32)
        gain = jnp.sum(grad * rows_here, axis=0, keepdims=True) / gain_ref[:, here]
        small_out[experts:, here] = jnp.broadcast_to(gain, (8 - experts, step))
        grad = grad.astype(BF16)
        for i in range(size // 2):
            kept[i][:, here] = grad[i * own : (i + 1) * own]
        sent_out[:, here] = grad[size // 2 * own :]


def experts_backward(chunks, first, w_gate, w_up, back, chosen, router_rows, gain):
    size = len(chunks)
    own, width = chunks[0].shape
    experts, rows, hidden = back.shape
    kept = jax.ShapeDtypeStruct((own, width), BF16)
    return pl.pallas_call(
        functools.partial(expert_kernel, size),
        in_specs=[IN_VMEM] * (size + 1) + [IN_HBM] * 2 + [IN_VMEM] * 4,
        out_shape=(
            jax.ShapeDtypeStruct((rows, 2 * experts * hidden), BF16),
            jax.ShapeDtypeStruct((rows, experts * hidden), BF16),
            jax.ShapeDtypeStruct((rows // 2, width), BF16),
        )
        + (kept,) * (size // 2)
        + (jax.ShapeDtypeStruct((8, width), F32),),
        scratch_shapes=[
            pltpu.VMEM((rows, width), BF16),
            pltpu.VMEM((width, 2 * (experts - experts // 2) * hidden), BF16),
            pltpu.SemaphoreType.DMA((2 * (experts - experts // 2),)),
        ],
        compiler_params=pltpu.CompilerParams(vmem_limit_bytes=20 * MIB),
        cost_estimate=pl.CostEstimate(
            flops=8 * experts * rows * hidden * width,
            bytes_accessed=experts * hidden * (width * 4 + rows * 10) + rows * width * 4,
            transcendentals=experts * rows * hidden,
        ),
        name="experts_backward",
    )(*chunks, vmem(first), hbm(w_gate), hbm(w_up), back, chosen, router_rows, gain)


def pair_kernel(count, *refs):
    kept, (arrived_ref, small_ref, other_ref), outs = refs[:count], refs[count : count + 3], refs[count + 3 :]
    own = kept[0].shape[0]
    for i in range(count):
        arrived = arrived_ref[i * own : (i + 1) * own].astype(F32)
        outs[i][...] = (kept[i][...].astype(F32) + arrived).astype(BF16)
    outs[count][...] = small_ref[...] + other_ref[...]


def pair_sum(kept, arrived, small, other):
    return pl.pallas_call(
        functools.partial(pair_kernel, len(kept)),
        out_shape=tuple(jax.ShapeDtypeStruct(k.shape, BF16) for k in kept)
        + (jax.ShapeDtypeStruct(small.shape, F32),),
        compiler_params=pltpu.CompilerParams(vmem_limit_bytes=4 * MIB),
        name="pair_sum",
    )(*kept, arrived, small, other)


SLOTS = 4


def write_out(tiles, buffer, sems):
    copies = []
    for i, (value, destination) in enumerate(tiles):
        slot = i % SLOTS
        if i >= SLOTS:
            copies[i - SLOTS].wait()
        buffer[slot] = value().astype(BF16)
        copies.append(pltpu.make_async_copy(buffer.at[slot], destination, sems.at[slot]))
        copies[-1].start()
    for copy in copies[-SLOTS:]:
        copy.wait()


def gate_up_kernel(*refs):
    chunks, (grads_ref, gate_out, up_out, normed, buffer, sems) = refs[:-6], refs[-6:]
    assemble(normed, chunks)
    width = normed.shape[1]
    hidden = gate_out.shape[3]
    step = buffer.shape[1]
    tiles = []
    for e in range(gate_out.shape[1]):
        for i, out in enumerate((gate_out, up_out)):
            columns = slice((2 * e + i) * hidden, (2 * e + i + 1) * hidden)
            for c in range(0, width, step):
                value = lambda c=c, columns=columns: dot(normed[:, c : c + step], grads_ref[:, columns], TN)
                tiles.append((value, out.at[0, e, pl.ds(c, step)]))
    write_out(tiles, buffer, sems)


def down_kernel(*refs):
    chunks, (act_ref, down_out, cot, buffer, sems) = refs[:-5], refs[-5:]
    assemble(cot, chunks)
    hidden = down_out.shape[2]
    step = buffer.shape[1]
    tiles = []
    for e in range(down_out.shape[1]):
        for c in range(0, hidden, step):
            first = e * hidden + c
            value = lambda first=first: dot(act_ref[:, first : first + step], cot[...], TN)
            tiles.append((value, down_out.at[0, e, pl.ds(c, step)]))
    write_out(tiles, buffer, sems)


def weight_gradients(kernel, chunks, hidden_rows, shapes, step, name):
    width = chunks[0].shape[1]
    rows, columns = hidden_rows.shape
    out_bytes = sum(2 * shape[1] * shape[2] * shape[3] for shape in shapes)
    return pl.pallas_call(
        kernel,
        out_specs=(pl.BlockSpec(memory_space=pltpu.HBM),) * len(shapes),
        out_shape=tuple(jax.ShapeDtypeStruct(shape, BF16) for shape in shapes),
        scratch_shapes=[
            pltpu.VMEM((rows, width), BF16),
            pltpu.VMEM((SLOTS, step, shapes[0][3]), BF16),
            pltpu.SemaphoreType.DMA((SLOTS,)),
        ],
        compiler_params=pltpu.CompilerParams(vmem_limit_bytes=16 * MIB),
        cost_estimate=pl.CostEstimate(
            flops=2 * rows * columns * width,
            bytes_accessed=out_bytes + 2 * rows * (columns + width),
            transcendentals=0,
        ),
        name=name,
    )(*chunks, hidden_rows)


def norm_back_kernel(count, *refs):
    parts, (summed_ref, gain_ref, cot_ref, small_ref, other_ref) = refs[:count], refs[count : count + 5]
    grad_ref, total_ref = refs[count + 5 : count + 7]
    sends = refs[count + 7 :]
    grad_normed = parts[0][...].astype(F32)
    for part in parts[1:]:
        grad_normed = grad_normed + part[...].astype(F32)
    summed = summed_ref[...]
    inv_rms = lax.rsqrt(jnp.mean(summed * summed, axis=1, keepdims=True) + 1e-06)
    scaled = grad_normed * gain_ref[...]
    centre = jnp.mean(scaled * summed, axis=1, keepdims=True)
    grad = inv_rms * scaled - summed * (inv_rms * inv_rms * inv_rms * centre)
    grad_ref[...] = grad + cot_ref[...].astype(F32)
    me = lax.axis_index("tok")
    width = sends[0].shape[1]
    for s, send in enumerate(sends):
        send[...] = grad_ref[:, head_slice(me ^ (s + 1), width)].astype(BF16)
    total_ref[...] = small_ref[...] + other_ref[...]


def norm_backward(parts, summed, gain, cot, small, other):
    rows, width = summed.shape
    num_tokens = lax.axis_size("tok")
    head = jax.ShapeDtypeStruct((rows, width // num_tokens), BF16)
    return pl.pallas_call(
        functools.partial(norm_back_kernel, len(parts)),
        out_shape=(
            jax.ShapeDtypeStruct((rows, width), F32),
            jax.ShapeDtypeStruct(small.shape, F32),
        )
        + (head,) * (num_tokens - 1),
        compiler_params=pltpu.CompilerParams(vmem_limit_bytes=4 * MIB),
        name="norm_backward",
    )(*parts, summed, gain, cot, small, other)


def finish_kernel(grad_ref, small_ref, other_ref, *refs):
    heads, (out_ref, router_out, gain_out) = refs[:-3], refs[-3:]
    me = lax.axis_index("tok")
    width = heads[0].shape[1]
    experts = router_out.shape[0]
    own = head_slice(me, width)
    out_ref[0, :, own] = (2.0 * grad_ref[:, own]).astype(BF16)
    for s, head in enumerate(heads):
        place = head_slice(me ^ (s + 1), width)
        out_ref[0, :, place] = (grad_ref[:, place] + head[...].astype(F32)).astype(BF16)
    router_out[...] = small_ref[:experts] + other_ref[:experts]
    gain_out[...] = small_ref[experts : experts + 1] + other_ref[experts : experts + 1]


def finish(grad_summed, heads, small, other, experts):
    rows, width = grad_summed.shape
    return pl.pallas_call(
        finish_kernel,
        out_shape=(
            jax.ShapeDtypeStruct((1, rows, width), BF16),
            jax.ShapeDtypeStruct((experts, width), F32),
            jax.ShapeDtypeStruct((1, width), F32),
        ),
        compiler_params=pltpu.CompilerParams(vmem_limit_bytes=4 * MIB),
        name="finish",
    )(grad_summed, small, other, *heads)


def shards(inputs, cotangent, norm_gain, router_weight, route_ids, w_gate, w_up, w_down):
    width = inputs.shape[2]
    size = lax.axis_size("dp")
    experts = w_gate.shape[1]

    x, cot, *sends = split_heads(inputs, cotangent)
    heads = [exchange(v, "tok", s + 1) for s, v in enumerate(sends)]
    x, norm_gain = after((x, norm_gain))
    gain, router_rows, chosen = small_operands(norm_gain, router_weight[0].T, route_ids[0].T)
    heads, gain, router_rows, chosen = after((heads, gain, router_rows, chosen))
    far_cots = gather_chips(cot)
    normed, summed = norm_rows(x, gain, heads)
    far_rows = gather_chips(normed)
    cots = gather_cores(far_cots)
    back, weights = back_hidden(cots, w_down, w_gate, w_up)
    far_rows[1:], back = after((far_rows[1:], back))
    rows = gather_cores(far_rows)
    grads, act, sent, *kept, small = experts_backward(
        rows, weights, w_gate, w_up, back, chosen, router_rows, gain
    )
    arrived = exchange(sent, "dp", 1)
    *pairs, small = pair_sum(kept, arrived, small, exchange(small, "dp", 1))
    pairs, grads, small = after((pairs, grads, small))
    parts = pairs[:1] + [exchange(pair, "dp", 2 * s) for s, pair in enumerate(pairs) if s]
    distance = 2
    while 4 * distance < size:
        small = small + exchange(small, "dp", distance)
        distance *= 2
    other = exchange(small, "dp", distance)
    grad_gate, grad_up = weight_gradients(
        gate_up_kernel, rows, grads, (w_gate.shape, w_up.shape), width, "grad_gate_up"
    )
    parts, grad_gate, grad_up, other = after((parts, grad_gate, grad_up, other))
    grad_summed, small, *sends = norm_backward(parts, summed, gain, cot, small, other)
    sends, act, small = after((sends, act, small))
    returned = [exchange(v, "tok", s + 1) for s, v in enumerate(sends)]
    other = exchange(small, "dp", 2 * distance)
    (grad_down,) = weight_gradients(
        down_kernel, cots, act, (w_down.shape,), w_down.shape[2], "grad_down"
    )
    returned, grad_down, other = after((returned, grad_down, other))
    grad_inputs, grad_router, grad_gain = finish(grad_summed, returned, small, other, experts)
    return (
        grad_inputs,
        grad_gate,
        grad_up,
        grad_down,
        grad_router.T[None],
        grad_gain,
    )


def solution(mesh):
    return jax.shard_map(
        shards,
        mesh=mesh,
        in_specs=(
            P("tok", "dp", None),
            P("tok", "dp", None),
            P("tok", None),
            P("tok", None, None),
            P("tok", None, None),
            P("tok", None, None, "dp"),
            P("tok", None, None, "dp"),
            P("tok", None, "dp", None),
        ),
        out_specs=(
            P("tok", "dp", None),
            P("tok", None, None, "dp"),
            P("tok", None, None, "dp"),
            P("tok", None, "dp", None),
            P("tok", None, None),
            P("tok", None),
        ),
        check_vma=False,
    )
```

profile of v0, /device:TPU:0, one launch (start us, length us, event | category | flops | bytes accessed | tf_op | source)
XLA Modules:
  0.0 68.3 jit_solution(7781869699231744477)
XLA Ops:
  0.6 1.0 %split_heads.1 = (bf16[32,2048]{1,0:T(8,128)(2,1)S(1)}, bf16[32,2048]{1,0:T(8,128)(2,1)S(1)}, bf16[32,512]{1,0:T(8,128)(2,1)S(1)}, bf16[32,512]{1,0:T(8,128)(2,1)S(1)}, bf16[32,512]{1,0:T(8,128)(2,1)S(1)}) custom-call(bf16[1,32,2048]{2,1,0:T(8,128)(2,1)} %x_hbm.1, bf16[1,32,2048]{2,1,0:T(8,128)(2,1)} %cot_hbm.1), custom_call_target="tpu_custom_call" | custom-call | tf_op jit(solution)/shard_map/split_heads/pallas_call | solution.py:87
  1.6 3.0 %collective-permute-start.6 = (bf16[32,2048]{1,0:T(8,128)(2,1)S(1)}, bf16[32,2048]{1,0:T(8,128)(2,1)S(1)}, u32[]{:S(2)}, u32[]{:S(2)}) collective-permute-start(bf16[32,2048]{1,0:T(8,128)(2,1)S(1)} %get-tuple-element.90.refs_0_.refs_6_), channel_id=1, source_target_pairs={{0,8},{4,12},{8,0},{12,4},{16,24},{20,28},{24,16},{28,20},{1,9},{5... | collective-permute-start | bytes 393224 | tf_op jit(solution)/shard_map/ppermute | solution.py:26
  4.6 1.5 %collective-permute-start.7 = (bf16[32,2048]{1,0:T(8,128)(2,1)S(1)}, bf16[32,2048]{1,0:T(8,128)(2,1)S(1)}, u32[]{:S(2)}, u32[]{:S(2)}) collective-permute-start(bf16[32,2048]{1,0:T(8,128)(2,1)S(1)} %get-tuple-element.90.refs_0_.refs_6_), channel_id=1, source_target_pairs={{0,16},{4,20},{8,24},{12,28},{16,0},{20,4},{24,8},{28,12},{1,17},{... | collective-permute-start | bytes 393224 | tf_op jit(solution)/shard_map/ppermute | solution.py:26
  6.2 2.0 %collective-permute-start = (bf16[32,512]{1,0:T(8,128)(2,1)S(1)}, bf16[32,512]{1,0:T(8,128)(2,1)S(1)}, u32[]{:S(2)}, u32[]{:S(2)}) collective-permute-start(bf16[32,512]{1,0:T(8,128)(2,1)S(1)} %get-tuple-element.78), channel_id=1, source_target_pairs={{0,1},{1,0},{2,3},{3,2},{4,5},{5,4},{6,7},{7,6},{8,9},{9,8},{10,11... | collective-permute-start | bytes 98312 | tf_op jit(solution)/shard_map/ppermute | solution.py:26
  8.2 2.6 %collective-permute-start.1 = (bf16[32,512]{1,0:T(8,128)(2,1)S(1)}, bf16[32,512]{1,0:T(8,128)(2,1)S(1)}, u32[]{:S(2)}, u32[]{:S(2)}) collective-permute-start(bf16[32,512]{1,0:T(8,128)(2,1)S(1)} %get-tuple-element.79), channel_id=1, source_target_pairs={{0,2},{1,3},{2,0},{3,1},{4,6},{5,7},{6,4},{7,5},{8,10},{9,11},{10,... | collective-permute-start | bytes 98312 | tf_op jit(solution)/shard_map/ppermute | solution.py:26
  10.8 2.5 %collective-permute-done.1.refs_1_ = bf16[32,512]{1,0:T(8,128)(2,1)S(1)} collective-permute-done((bf16[32,512]{1,0:T(8,128)(2,1)S(1)}, bf16[32,512]{1,0:T(8,128)(2,1)S(1)}, u32[]{:S(2)}, u32[]{:S(2)}) %collective-permute-start.1) | collective-permute-done | bytes 32800 | tf_op jit(solution)/shard_map/ppermute | solution.py:26
  13.3 2.2 %collective-permute-start.2 = (bf16[32,512]{1,0:T(8,128)(2,1)S(1)}, bf16[32,512]{1,0:T(8,128)(2,1)S(1)}, u32[]{:S(2)}, u32[]{:S(2)}) collective-permute-start(bf16[32,512]{1,0:T(8,128)(2,1)S(1)} %get-tuple-element.80), channel_id=1, source_target_pairs={{0,3},{1,2},{2,1},{3,0},{4,7},{5,6},{6,5},{7,4},{8,11},{9,10},{10,... | collective-permute-start | bytes 98312 | tf_op jit(solution)/shard_map/ppermute | solution.py:26
  16.1 0.9 %small_operands.1 = (f32[1,2048]{1,0:T(1,128)S(1)}, bf16[4,2048]{1,0:T(4,128)(2,1)S(1)}, f32[256,8]{1,0:T(8,128)S(1)}) custom-call(f32[1,2048]{1,0:T(1,128)} %gain_hbm, bf16[4,2048]{1,0:T(4,128)(2,1)} %bitcast.10, s32[2,256]{1,0:T(2,128)} %bitcast.11), custom_call_target="tpu_custom_call" | custom-call | flops 68719476736 | bytes 33554432 | tf_op jit(solution)/shard_map/small_operands/pallas_call | solution.py:122
  17.0 2.0 %collective-permute-done.2.refs_2_ = bf16[32,512]{1,0:T(8,128)(2,1)S(1)} collective-permute-done((bf16[32,512]{1,0:T(8,128)(2,1)S(1)}, bf16[32,512]{1,0:T(8,128)(2,1)S(1)}, u32[]{:S(2)}, u32[]{:S(2)}) %collective-permute-start.2) | collective-permute-done | bytes 32800 | tf_op jit(solution)/shard_map/ppermute | solution.py:26
  19.1 1.6 %collective-permute-start.3 = (bf16[32,2048]{1,0:T(8,128)(2,1)S(1)}, bf16[32,2048]{1,0:T(8,128)(2,1)S(1)}, u32[]{:S(2)}, u32[]{:S(2)}) collective-permute-start(bf16[32,2048]{1,0:T(8,128)(2,1)S(1)} %get-tuple-element.89.refs_0_), channel_id=1, source_target_pairs={{0,8},{4,12},{8,0},{12,4},{16,24},{20,28},{24,16},{28,20},{1,9},{5... | collective-permute-start | bytes 393224 | tf_op jit(solution)/shard_map/ppermute | solution.py:26
  20.7 1.5 %collective-permute-start.4 = (bf16[32,2048]{1,0:T(8,128)(2,1)S(1)}, bf16[32,2048]{1,0:T(8,128)(2,1)S(1)}, u32[]{:S(2)}, u32[]{:S(2)}) collective-permute-start(bf16[32,2048]{1,0:T(8,128)(2,1)S(1)} %get-tuple-element.89.refs_0_), channel_id=1, source_target_pairs={{0,16},{4,20},{8,24},{12,28},{16,0},{20,4},{24,8},{28,12},{1,17},{... | collective-permute-start | bytes 393224 | tf_op jit(solution)/shard_map/ppermute | solution.py:26
  22.7 6.1 %back_hidden.1 = (f32[4,256,512]{2,1,0:T(8,128)S(1)}, bf16[2048,2048]{1,0:T(8,128)(2,1)S(1)}) custom-call(bf16[32,2048]{1,0:T(8,128)(2,1)S(1)} %get-tuple-element.90.refs_0_.refs_6_, bf16[32,2048]{1,0:T(8,128)(2,1)S(1)} %collective-permute-done.6.refs_1_, bf16[32,2048]{1,0:T(8,128)(2,1)S(1)} %collective-permute-done.7.refs_2_, ...), custom_call_target="tpu_custom_call" | custom-call | flops 2147483648 | bytes 19922944 | tf_op jit(solution)/shard_map/back_hidden/pallas_call | solution.py:193
  28.8 0.6 collective-permute-start.14
  30.9 12.2 %experts_backward.1 = (bf16[256,4096]{1,0:T(8,128)(2,1)S(1)}, bf16[256,2048]{1,0:T(8,128)(2,1)S(1)}, bf16[128,2048]{1,0:T(8,128)(2,1)S(1)}, bf16[32,2048]{1,0:T(...) custom-call(bf16[32,2048]{1,0:T(8,128)(2,1)S(1)} %get-tuple-element., ...), custom_call_target="tpu_custom_call" | custom-call | flops 8589934592 | bytes 24117248 | tf_op jit(solution)/shard_map/experts_backward/pallas_call | solution.py:290
  43.8 1.5 %collective-permute-done.18.refs_6_ = f32[8,2048]{1,0:T(8,128)S(1)} collective-permute-done((f32[8,2048]{1,0:T(8,128)S(1)}, f32[8,2048]{1,0:T(8,128)S(1)}, u32[]{:S(2)}, u32[]{:S(2)}) %collective-permute-start.18) | collective-permute-done | bytes 65568 | tf_op jit(solution)/shard_map/ppermute | solution.py:26
  45.4 1.6 %collective-permute-start.19 = (bf16[32,2048]{1,0:T(8,128)(2,1)S(1)}, bf16[32,2048]{1,0:T(8,128)(2,1)S(1)}, u32[]{:S(2)}, u32[]{:S(2)}) collective-permute-start(bf16[32,2048]{1,0:T(8,128)(2,1)S(1)} %get-tuple-element.112), channel_id=1, source_target_pairs={{0,8},{4,12},{8,0},{12,4},{16,24},{20,28},{24,16},{28,20},{1,9},{5... | collective-permute-start | bytes 393224 | tf_op jit(solution)/shard_map/ppermute | solution.py:26
  46.9 1.5 %collective-permute-start.20 = (bf16[32,2048]{1,0:T(8,128)(2,1)S(1)}, bf16[32,2048]{1,0:T(8,128)(2,1)S(1)}, u32[]{:S(2)}, u32[]{:S(2)}) collective-permute-start(bf16[32,2048]{1,0:T(8,128)(2,1)S(1)} %get-tuple-element.113), channel_id=1, source_target_pairs={{0,16},{4,20},{8,24},{12,28},{16,0},{20,4},{24,8},{28,12},{1,17},{... | collective-permute-start | bytes 393224 | tf_op jit(solution)/shard_map/ppermute | solution.py:26
  48.9 1.5 %collective-permute-start.22 = (f32[8,2048]{1,0:T(8,128)S(1)}, f32[8,2048]{1,0:T(8,128)S(1)}, u32[]{:S(2)}, u32[]{:S(2)}) collective-permute-start(f32[8,2048]{1,0:T(8,128)S(1)} %get-tuple-element.118.refs_7_), channel_id=1, source_target_pairs={{0,8},{4,12},{8,0},{12,4},{16,24},{20,28},{24,16},{28,20},{1,9},{5... | collective-permute-start | bytes 196616 | tf_op jit(solution)/shard_map/ppermute | solution.py:26
  50.4 6.7 %grad_gate_up.1 = (bf16[1,4,2048,512]{3,2,1,0:T(8,128)(2,1)}, bf16[1,4,2048,512]{3,2,1,0:T(8,128)(2,1)}) custom-call(bf16[32,2048]{1,0:T(8,128)(2,1)S(1)} %get-tuple-element.89.refs_0_, bf16[32,2048]{1,0:T(8,128)(2,1)S(1)} %collective-permute-done.3.refs_1_, bf16[32,2048]{1,0:T(8,128)(2,1)S(1)} %collective-permute-done.4.refs_2_, ...), custom_call_target="tpu_custom_call" | custom-call | flops 4294967296 | bytes 19922944 | tf_op jit(solution)/shard_map/grad_gate_up/pallas_call | solution.py:384
  57.5 2.8 %collective-permute-start.24 = (bf16[32,512]{1,0:T(8,128)(2,1)S(1)}, bf16[32,512]{1,0:T(8,128)(2,1)S(1)}, u32[]{:S(2)}, u32[]{:S(2)}) collective-permute-start(bf16[32,512]{1,0:T(8,128)(2,1)S(1)} %get-tuple-element.133), channel_id=1, source_target_pairs={{0,2},{1,3},{2,0},{3,1},{4,6},{5,7},{6,4},{7,5},{8,10},{9,11},{10,... | collective-permute-start | bytes 98312 | tf_op jit(solution)/shard_map/ppermute | solution.py:26
  60.3 1.6 %collective-permute-start.25 = (bf16[32,512]{1,0:T(8,128)(2,1)S(1)}, bf16[32,512]{1,0:T(8,128)(2,1)S(1)}, u32[]{:S(2)}, u32[]{:S(2)}) collective-permute-start(bf16[32,512]{1,0:T(8,128)(2,1)S(1)} %get-tuple-element.134), channel_id=1, source_target_pairs={{0,3},{1,2},{2,1},{3,0},{4,7},{5,6},{6,5},{7,4},{8,11},{9,10},{10,... | collective-permute-start | bytes 98312 | tf_op jit(solution)/shard_map/ppermute | solution.py:26
  61.9 1.5 %collective-permute-start.26 = (f32[8,2048]{1,0:T(8,128)S(1)}, f32[8,2048]{1,0:T(8,128)S(1)}, u32[]{:S(2)}, u32[]{:S(2)}) collective-permute-start(f32[8,2048]{1,0:T(8,128)S(1)} %get-tuple-element.131.small_ref), channel_id=1, source_target_pairs={{0,16},{4,20},{8,24},{12,28},{16,0},{20,4},{24,8},{28,12},{1,17},{... | collective-permute-start | bytes 196616 | tf_op jit(solution)/shard_map/ppermute | solution.py:26
  63.4 4.1 %grad_down.1 = bf16[1,4,512,2048]{3,2,1,0:T(8,128)(2,1)} custom-call(bf16[32,2048]{1,0:T(8,128)(2,1)S(1)} %get-tuple-element.90.refs_0_.refs_6_, bf16[32,2048]{1,0:T(8,128)(2,1)S(1)} %collective-permute-done.6.refs_1_, bf16[32,2048]{1,0:T(8,128)(2,1)S(1)} %collective-permute-done.7.refs_2_, bf16[32,2048]{1,0:T(8,128)(2,1)S(1)} %collective-permute-done.8.refs_3_, ...), custom_call_target="tpu_custom_call" | custom-call | flops 2147483648 | bytes 10485760 | tf_op jit(solution)/shard_map/grad_down/pallas_call | solution.py:384
  67.6 0.7 %finish.1 = (bf16[1,32,2048]{2,1,0:T(8,128)(2,1)}, f32[4,2048]{1,0:T(4,128)}, f32[1,2048]{1,0:T(1,128)}) custom-call(f32[32,2048]{1,0:T(8,128)S(1)} %get-tuple-element.125.grad_ref, f32[8,2048]{1,0:T(8,128)S(1)} %get-tuple-element.131.small_ref, f32[8,2048]{1,0:T(8,128)S(1)} %collective-permute-done.26.other_ref, ...), custom_call_target="tpu_custom_call" | custom-call | tf_op jit(solution)/shard_map/finish/pallas_call | solution.py:455
  (40 shorter events, 4.3 us)
Async XLA Ops:
  1.6 13.9 %collective-permute-start.6 = (bf16[32,2048]{1,0:T(8,128)(2,1)S(1)}, bf16[32,2048]{1,0:T(8,128)(2,1)S(1)}, u32[]{:S(2)}, u32[]{:S(2)}) collective-permute-start(bf16[32,2048]{1,0:T(8,128)(2,1)S(1)} %get-tuple-element.90.refs_0_.refs_6_), channel_id=1, source_target_pairs={{0,8},{4,12},{8,0},{12,4},{16,24},{20,28},{24,16},{28,20},{1,9},{5... | collective-permute-start | bytes 393224 | tf_op jit(solution)/shard_map/ppermute | solution.py:26
  4.6 10.9 %collective-permute-start.7 = (bf16[32,2048]{1,0:T(8,128)(2,1)S(1)}, bf16[32,2048]{1,0:T(8,128)(2,1)S(1)}, u32[]{:S(2)}, u32[]{:S(2)}) collective-permute-start(bf16[32,2048]{1,0:T(8,128)(2,1)S(1)} %get-tuple-element.90.refs_0_.refs_6_), channel_id=1, source_target_pairs={{0,16},{4,20},{8,24},{12,28},{16,0},{20,4},{24,8},{28,12},{1,17},{... | collective-permute-start | bytes 393224 | tf_op jit(solution)/shard_map/ppermute | solution.py:26
  6.1 9.9 %collective-permute-start.8 = (bf16[32,2048]{1,0:T(8,128)(2,1)S(1)}, bf16[32,2048]{1,0:T(8,128)(2,1)S(1)}, u32[]{:S(2)}, u32[]{:S(2)}) collective-permute-start(bf16[32,2048]{1,0:T(8,128)(2,1)S(1)} %get-tuple-element.90.refs_0_.refs_6_), channel_id=1, source_target_pairs={{0,24},{4,28},{8,16},{12,20},{16,8},{20,12},{24,0},{28,4},{1,25},{... | collective-permute-start | bytes 393224 | tf_op jit(solution)/shard_map/ppermute | solution.py:26
  6.2 4.6 %collective-permute-start = (bf16[32,512]{1,0:T(8,128)(2,1)S(1)}, bf16[32,512]{1,0:T(8,128)(2,1)S(1)}, u32[]{:S(2)}, u32[]{:S(2)}) collective-permute-start(bf16[32,512]{1,0:T(8,128)(2,1)S(1)} %get-tuple-element.78), channel_id=1, source_target_pairs={{0,1},{1,0},{2,3},{3,2},{4,5},{5,4},{6,7},{7,6},{8,9},{9,8},{10,11... | collective-permute-start | bytes 98312 | tf_op jit(solution)/shard_map/ppermute | solution.py:26
  8.2 5.1 %collective-permute-start.1 = (bf16[32,512]{1,0:T(8,128)(2,1)S(1)}, bf16[32,512]{1,0:T(8,128)(2,1)S(1)}, u32[]{:S(2)}, u32[]{:S(2)}) collective-permute-start(bf16[32,512]{1,0:T(8,128)(2,1)S(1)} %get-tuple-element.79), channel_id=1, source_target_pairs={{0,2},{1,3},{2,0},{3,1},{4,6},{5,7},{6,4},{7,5},{8,10},{9,11},{10,... | collective-permute-start | bytes 98312 | tf_op jit(solution)/shard_map/ppermute | solution.py:26
  10.8 9.9 %collective-permute-start.9 = (bf16[32,2048]{1,0:T(8,128)(2,1)S(1)}, bf16[32,2048]{1,0:T(8,128)(2,1)S(1)}, u32[]{:S(2)}, u32[]{:S(2)}) collective-permute-start(bf16[32,2048]{1,0:T(8,128)(2,1)S(1)} %get-tuple-element.90.refs_0_.refs_6_), channel_id=1, source_target_pairs={{0,4},{4,0},{8,12},{12,8},{16,20},{20,16},{24,28},{28,24},{1,5},{5... | collective-permute-start | bytes 393224 | tf_op jit(solution)/shard_map/ppermute | solution.py:26
  13.3 5.7 %collective-permute-start.2 = (bf16[32,512]{1,0:T(8,128)(2,1)S(1)}, bf16[32,512]{1,0:T(8,128)(2,1)S(1)}, u32[]{:S(2)}, u32[]{:S(2)}) collective-permute-start(bf16[32,512]{1,0:T(8,128)(2,1)S(1)} %get-tuple-element.80), channel_id=1, source_target_pairs={{0,3},{1,2},{2,1},{3,0},{4,7},{5,6},{6,5},{7,4},{8,11},{9,10},{10,... | collective-permute-start | bytes 98312 | tf_op jit(solution)/shard_map/ppermute | solution.py:26
  15.5 6.7 %collective-permute-start.10 = (bf16[32,2048]{1,0:T(8,128)(2,1)S(1)}, bf16[32,2048]{1,0:T(8,128)(2,1)S(1)}, u32[]{:S(2)}, u32[]{:S(2)}) collective-permute-start(bf16[32,2048]{1,0:T(8,128)(2,1)S(1)} %collective-permute-done.6.refs_1_), channel_id=1, source_target_pairs={{0,4},{4,0},{8,12},{12,8},{16,20},{20,16},{24,28},{28,24},{1,5},{5... | collective-permute-start | bytes 393224 | tf_op jit(solution)/shard_map/ppermute | solution.py:26
  15.5 7.2 %collective-permute-start.11 = (bf16[32,2048]{1,0:T(8,128)(2,1)S(1)}, bf16[32,2048]{1,0:T(8,128)(2,1)S(1)}, u32[]{:S(2)}, u32[]{:S(2)}) collective-permute-start(bf16[32,2048]{1,0:T(8,128)(2,1)S(1)} %collective-permute-done.7.refs_2_), channel_id=1, source_target_pairs={{0,4},{4,0},{8,12},{12,8},{16,20},{20,16},{24,28},{28,24},{1,5},{5... | collective-permute-start | bytes 393224 | tf_op jit(solution)/shard_map/ppermute | solution.py:26
  16.0 6.7 %collective-permute-start.12 = (bf16[32,2048]{1,0:T(8,128)(2,1)S(1)}, bf16[32,2048]{1,0:T(8,128)(2,1)S(1)}, u32[]{:S(2)}, u32[]{:S(2)}) collective-permute-start(bf16[32,2048]{1,0:T(8,128)(2,1)S(1)} %collective-permute-done.8.refs_3_), channel_id=1, source_target_pairs={{0,4},{4,0},{8,12},{12,8},{16,20},{20,16},{24,28},{28,24},{1,5},{5... | collective-permute-start | bytes 393224 | tf_op jit(solution)/shard_map/ppermute | solution.py:26
  19.1 9.7 %collective-permute-start.3 = (bf16[32,2048]{1,0:T(8,128)(2,1)S(1)}, bf16[32,2048]{1,0:T(8,128)(2,1)S(1)}, u32[]{:S(2)}, u32[]{:S(2)}) collective-permute-start(bf16[32,2048]{1,0:T(8,128)(2,1)S(1)} %get-tuple-element.89.refs_0_), channel_id=1, source_target_pairs={{0,8},{4,12},{8,0},{12,4},{16,24},{20,28},{24,16},{28,20},{1,9},{5... | collective-permute-start | bytes 393224 | tf_op jit(solution)/shard_map/ppermute | solution.py:26
  20.7 8.1 %collective-permute-start.4 = (bf16[32,2048]{1,0:T(8,128)(2,1)S(1)}, bf16[32,2048]{1,0:T(8,128)(2,1)S(1)}, u32[]{:S(2)}, u32[]{:S(2)}) collective-permute-start(bf16[32,2048]{1,0:T(8,128)(2,1)S(1)} %get-tuple-element.89.refs_0_), channel_id=1, source_target_pairs={{0,16},{4,20},{8,24},{12,28},{16,0},{20,4},{24,8},{28,12},{1,17},{... | collective-permute-start | bytes 393224 | tf_op jit(solution)/shard_map/ppermute | solution.py:26
  22.2 6.6 %collective-permute-start.5 = (bf16[32,2048]{1,0:T(8,128)(2,1)S(1)}, bf16[32,2048]{1,0:T(8,128)(2,1)S(1)}, u32[]{:S(2)}, u32[]{:S(2)}) collective-permute-start(bf16[32,2048]{1,0:T(8,128)(2,1)S(1)} %get-tuple-element.89.refs_0_), channel_id=1, source_target_pairs={{0,24},{4,28},{8,16},{12,20},{16,8},{20,12},{24,0},{28,4},{1,25},{... | collective-permute-start | bytes 393224 | tf_op jit(solution)/shard_map/ppermute | solution.py:26
  22.7 7.2 %collective-permute-start.13 = (bf16[32,2048]{1,0:T(8,128)(2,1)S(1)}, bf16[32,2048]{1,0:T(8,128)(2,1)S(1)}, u32[]{:S(2)}, u32[]{:S(2)}) collective-permute-start(bf16[32,2048]{1,0:T(8,128)(2,1)S(1)} %get-tuple-element.89.refs_0_), channel_id=1, source_target_pairs={{0,4},{4,0},{8,12},{12,8},{16,20},{20,16},{24,28},{28,24},{1,5},{5... | collective-permute-start | bytes 393224 | tf_op jit(solution)/shard_map/ppermute | solution.py:26
  43.2 2.1 %collective-permute-start.17 = (bf16[128,2048]{1,0:T(8,128)(2,1)S(1)}, bf16[128,2048]{1,0:T(8,128)(2,1)S(1)}, u32[]{:S(2)}, u32[]{:S(2)}) collective-permute-start(bf16[128,2048]{1,0:T(8,128)(2,1)S(1)} %get-tuple-element.103), channel_id=1, source_target_pairs={{0,4},{4,0},{8,12},{12,8},{16,20},{20,16},{24,28},{28,24},{1,5},{5... | collective-permute-start | bytes 1572872 | tf_op jit(solution)/shard_map/ppermute | solution.py:26
  43.6 1.7 %collective-permute-start.18 = (f32[8,2048]{1,0:T(8,128)S(1)}, f32[8,2048]{1,0:T(8,128)S(1)}, u32[]{:S(2)}, u32[]{:S(2)}) collective-permute-start(f32[8,2048]{1,0:T(8,128)S(1)} %get-tuple-element.104.refs_5_), channel_id=1, source_target_pairs={{0,4},{4,0},{8,12},{12,8},{16,20},{20,16},{24,28},{28,24},{1,5},{5... | collective-permute-start | bytes 196616 | tf_op jit(solution)/shard_map/ppermute | solution.py:26
  45.4 11.8 %collective-permute-start.19 = (bf16[32,2048]{1,0:T(8,128)(2,1)S(1)}, bf16[32,2048]{1,0:T(8,128)(2,1)S(1)}, u32[]{:S(2)}, u32[]{:S(2)}) collective-permute-start(bf16[32,2048]{1,0:T(8,128)(2,1)S(1)} %get-tuple-element.112), channel_id=1, source_target_pairs={{0,8},{4,12},{8,0},{12,4},{16,24},{20,28},{24,16},{28,20},{1,9},{5... | collective-permute-start | bytes 393224 | tf_op jit(solution)/shard_map/ppermute | solution.py:26
  46.9 10.2 %collective-permute-start.20 = (bf16[32,2048]{1,0:T(8,128)(2,1)S(1)}, bf16[32,2048]{1,0:T(8,128)(2,1)S(1)}, u32[]{:S(2)}, u32[]{:S(2)}) collective-permute-start(bf16[32,2048]{1,0:T(8,128)(2,1)S(1)} %get-tuple-element.113), channel_id=1, source_target_pairs={{0,16},{4,20},{8,24},{12,28},{16,0},{20,4},{24,8},{28,12},{1,17},{... | collective-permute-start | bytes 393224 | tf_op jit(solution)/shard_map/ppermute | solution.py:26
  48.5 8.7 %collective-permute-start.21 = (bf16[32,2048]{1,0:T(8,128)(2,1)S(1)}, bf16[32,2048]{1,0:T(8,128)(2,1)S(1)}, u32[]{:S(2)}, u32[]{:S(2)}) collective-permute-start(bf16[32,2048]{1,0:T(8,128)(2,1)S(1)} %get-tuple-element.114), channel_id=1, source_target_pairs={{0,24},{4,28},{8,16},{12,20},{16,8},{20,12},{24,0},{28,4},{1,25},{... | collective-permute-start | bytes 393224 | tf_op jit(solution)/shard_map/ppermute | solution.py:26
  48.9 8.2 %collective-permute-start.22 = (f32[8,2048]{1,0:T(8,128)S(1)}, f32[8,2048]{1,0:T(8,128)S(1)}, u32[]{:S(2)}, u32[]{:S(2)}) collective-permute-start(f32[8,2048]{1,0:T(8,128)S(1)} %get-tuple-element.118.refs_7_), channel_id=1, source_target_pairs={{0,8},{4,12},{8,0},{12,4},{16,24},{20,28},{24,16},{28,20},{1,9},{5... | collective-permute-start | bytes 196616 | tf_op jit(solution)/shard_map/ppermute | solution.py:26
  57.4 10.1 %collective-permute-start.23 = (bf16[32,512]{1,0:T(8,128)(2,1)S(1)}, bf16[32,512]{1,0:T(8,128)(2,1)S(1)}, u32[]{:S(2)}, u32[]{:S(2)}) collective-permute-start(bf16[32,512]{1,0:T(8,128)(2,1)S(1)} %get-tuple-element.132), channel_id=1, source_target_pairs={{0,1},{1,0},{2,3},{3,2},{4,5},{5,4},{6,7},{7,6},{8,9},{9,8},{10,11... | collective-permute-start | bytes 98312 | tf_op jit(solution)/shard_map/ppermute | solution.py:26
  57.5 10.0 %collective-permute-start.24 = (bf16[32,512]{1,0:T(8,128)(2,1)S(1)}, bf16[32,512]{1,0:T(8,128)(2,1)S(1)}, u32[]{:S(2)}, u32[]{:S(2)}) collective-permute-start(bf16[32,512]{1,0:T(8,128)(2,1)S(1)} %get-tuple-element.133), channel_id=1, source_target_pairs={{0,2},{1,3},{2,0},{3,1},{4,6},{5,7},{6,4},{7,5},{8,10},{9,11},{10,... | collective-permute-start | bytes 98312 | tf_op jit(solution)/shard_map/ppermute | solution.py:26
  60.3 7.3 %collective-permute-start.25 = (bf16[32,512]{1,0:T(8,128)(2,1)S(1)}, bf16[32,512]{1,0:T(8,128)(2,1)S(1)}, u32[]{:S(2)}, u32[]{:S(2)}) collective-permute-start(bf16[32,512]{1,0:T(8,128)(2,1)S(1)} %get-tuple-element.134), channel_id=1, source_target_pairs={{0,3},{1,2},{2,1},{3,0},{4,7},{5,6},{6,5},{7,4},{8,11},{9,10},{10,... | collective-permute-start | bytes 98312 | tf_op jit(solution)/shard_map/ppermute | solution.py:26
  61.9 5.7 %collective-permute-start.26 = (f32[8,2048]{1,0:T(8,128)S(1)}, f32[8,2048]{1,0:T(8,128)S(1)}, u32[]{:S(2)}, u32[]{:S(2)}) collective-permute-start(f32[8,2048]{1,0:T(8,128)S(1)} %get-tuple-element.131.small_ref), channel_id=1, source_target_pairs={{0,16},{4,20},{8,24},{12,28},{16,0},{20,4},{24,8},{28,12},{1,17},{... | collective-permute-start | bytes 196616 | tf_op jit(solution)/shard_map/ppermute | solution.py:26
  (3 other events, 4.4 us)
where the time goes:
time: 68.5 us; the launch traced here: 68.3 us
  Pallas kernels  32.2 us (47%)
  starting transfers between devices  28.2 us (41%)
  waiting for transfers between devices  7.06 us (10%)
  between operations  0.82 us (1%)
    ppermute x27, starting transfers between devices, exchange(): return lax.ppermute(value, axis, [(i, i ^ distance) for i in range(size)])  28.2 us
    pallas_call x1, Pallas kernels, experts_backward(): pl.pallas_call(functools.partial(expert_kernel, size), in_specs=[IN_VMEM]...  12.2 us
    pallas_call x2, Pallas kernels, weight_gradients(): pl.pallas_call(kernel, out_specs=(pl.BlockSpec(memory_space=pltpu.HBM),)...  10.8 us
    ppermute x27, waiting for transfers between devices, exchange(): return lax.ppermute(value, axis, [(i, i ^ distance) for i in range(size)])  7.06 us
    pallas_call x1, Pallas kernels, back_hidden(): pl.pallas_call(functools.partial(back_kernel, size), in_specs=[IN_VMEM] *...  6.08 us
  transfers between devices with their start and end apart: 27, of which 6 were waited for; matrix products, arithmetic and copies ran while one was open for 0% of the time, Pallas kernels for 26%

commit v1 on v0

--- a/solution.py
+++ b/solution.py
@@ -44,9 +44,10 @@
 
 
 def assemble(rows, chunks):
-    for i, chunk in enumerate(chunks):
-        own = chunk.shape[0]
-        rows[i * own : (i + 1) * own] = chunk[...]
+    first = 0
+    for chunk in chunks:
+        rows[first : first + chunk.shape[0]] = chunk[...]
+        first += chunk.shape[0]
 
 
 def head_slice(slot, width):
@@ -66,35 +67,100 @@
 ANYWHERE = pl.BlockSpec(memory_space=pl.ANY)
 
 
-def heads_kernel(x_hbm, cot_hbm, x_ref, cot_ref, *refs):
-    sends, sems = refs[:-1], refs[-1]
+def head_plan(num_tokens):
+    held, stages, bit = [(0, d) for d in range(1, num_tokens)], [], 1
+    while bit < num_tokens:
+        sent = [item for item in held if item[1] & bit]
+        received = [(source ^ bit, target ^ bit) for source, target in sent]
+        held = [item for item in held if not item[1] & bit] + received
+        stages.append((bit, sent, received))
+        bit *= 2
+    first = stages[0][1]
+    return first, [(0, d) for d in range(1, num_tokens) if (0, d) not in first], stages
+
+
+def pick(item, lists):
+    for i, items in enumerate(lists):
+        if item in items:
+            return i, items.index(item)
+
+
+def pack_kernel(picks, *refs):
+    for k, (i, j) in enumerate(picks):
+        refs[-1][k] = refs[i][j]
+
+
+def pack_heads(arrays, picks):
+    return pl.pallas_call(
+        functools.partial(pack_kernel, picks),
+        out_shape=jax.ShapeDtypeStruct((len(picks),) + arrays[0].shape[1:], BF16),
+        compiler_params=pltpu.CompilerParams(vmem_limit_bytes=4 * MIB),
+        name="pack_heads",
+    )(*arrays)
+
+
+def first_stage(first, kept):
+    _, kept_items, stages = head_plan(lax.axis_size("tok"))
+    bit, _, received = stages[0]
+    return [kept, exchange(first, "tok", bit)], [kept_items, received]
+
+
+def other_stages(arrays, lists):
+    for bit, sent, received in head_plan(lax.axis_size("tok"))[2][1:]:
+        payload = pack_heads(arrays, [pick(item, lists) for item in sent])
+        arrays = arrays + [exchange(payload, "tok", bit)]
+        lists = lists + [received]
+    return arrays, lists
+
+
+def heads_kernel(x_hbm, cot_hbm, x_ref, cot_ref, first_ref, kept_ref, sems):
     copy_x = pltpu.make_async_copy(x_hbm.at[0], x_ref, sems.at[0])
     copy_cot = pltpu.make_async_copy(cot_hbm.at[0], cot_ref, sems.at[1])
     copy_x.start()
     copy_cot.start()
     copy_x.wait()
+    store_heads(x_ref, first_ref, kept_ref)
+    copy_cot.wait()
+
+
+def store_heads(rows_ref, first_ref, kept_ref):
+    width = first_ref.shape[2]
+    first, kept, _ = head_plan(rows_ref.shape[1] // width)
     me = lax.axis_index("tok")
-    width = sends[0].shape[1]
-    for s, send in enumerate(sends):
-        send[...] = x_ref[:, head_slice(me ^ (s + 1), width)]
-    copy_cot.wait()
+    for ref, items in ((first_ref, first), (kept_ref, kept)):
+        for k, (_, d) in enumerate(items):
+            ref[k] = rows_ref[:, head_slice(me ^ d, width)].astype(BF16)
+
+
+def head_shapes(rows, width):
+    num_tokens = lax.axis_size("tok")
+    first, kept, _ = head_plan(num_tokens)
+    return tuple(
+        jax.ShapeDtypeStruct((len(items), rows, width // num_tokens), BF16) for items in (first, kept)
+    )
 
 
 def split_heads(x, cotangent):
     _, rows, width = x.shape
-    num_tokens = lax.axis_size("tok")
-    head = jax.ShapeDtypeStruct((rows, width // num_tokens), BF16)
     return pl.pallas_call(
         heads_kernel,
         in_specs=[IN_HBM] * 2,
-        out_shape=(jax.ShapeDtypeStruct((rows, width), BF16),) * 2 + (head,) * (num_tokens - 1),
+        out_shape=(jax.ShapeDtypeStruct((rows, width), BF16),) * 2 + head_shapes(rows, width),
         scratch_shapes=[pltpu.SemaphoreType.DMA((2,))],
         compiler_params=pltpu.CompilerParams(vmem_limit_bytes=4 * MIB),
         name="split_heads",
     )(hbm(x), hbm(cotangent))
 
 
-def small_kernel(gain_hbm, router_hbm, route_hbm, gain_ref, router_ref, chosen_ref, routes, sems):
+def from_tokens(arrays, lists):
+    num_tokens = lax.axis_size("tok")
+    return tuple((d,) + pick((d, 0), lists) for d in range(1, num_tokens))
+
+
+def small_kernel(gain_hbm, router_hbm, route_hbm, down_hbm, *refs):
+    gain_ref, router_ref, chosen_ref, down_ref, routes, sems, down_sem = refs
+    load = pltpu.make_async_copy(down_hbm.at[0, pl.ds(0, down_ref.shape[0])], down_ref, down_sem)
+    load.start()
     copies = [
         pltpu.make_async_copy(src, dst, sems.at[i])
         for i, (src, dst) in enumerate(
@@ -115,46 +181,67 @@
     for k in range(1, routes.shape[0]):
         hit = hit | (routes[k : k + 1, :] == ids)
     chosen_ref[...] = hit.astype(F32).T
-
-
-def small_operands(gain, router_rows, routes):
+    load.wait()
+
+
+def small_operands(gain, router_rows, routes, w_down):
     experts, all_rows = 8, routes.shape[1]
     return pl.pallas_call(
         small_kernel,
-        in_specs=[IN_HBM] * 3,
+        in_specs=[IN_HBM] * 4,
+        out_specs=(IN_VMEM,) * 3 + (ANYWHERE,),
         out_shape=(
             jax.ShapeDtypeStruct(gain.shape, F32),
             jax.ShapeDtypeStruct(router_rows.shape, BF16),
             jax.ShapeDtypeStruct((all_rows, experts), F32),
-        ),
-        scratch_shapes=[pltpu.VMEM(routes.shape, jnp.int32), pltpu.SemaphoreType.DMA((3,))],
+            jax.ShapeDtypeStruct((w_down.shape[1] // 2,) + w_down.shape[2:], BF16),
+        ),
+        scratch_shapes=[
+            pltpu.VMEM(routes.shape, jnp.int32),
+            pltpu.SemaphoreType.DMA((3,)),
+            pltpu.SemaphoreType.DMA(()),
+        ],
         compiler_params=pltpu.CompilerParams(vmem_limit_bytes=4 * MIB),
         cost_estimate=pl.CostEstimate(flops=2**36, bytes_accessed=32 * MIB, transcendentals=0),
         name="small_operands",
-    )(hbm(gain), hbm(router_rows), hbm(routes))
-
-
-def norm_kernel(x_ref, gain_ref, *refs):
+    )(hbm(gain), hbm(router_rows), hbm(routes), hbm(w_down))
+
+
+def norm_kernel(places, x_ref, gain_ref, *refs):
     heads, (normed_ref, summed_ref) = refs[:-2], refs[-2:]
     me = lax.axis_index("tok")
-    width = heads[0].shape[1]
+    width = heads[0].shape[2]
     own = head_slice(me, width)
     summed_ref[:, own] = 2.0 * x_ref[:, own].astype(F32)
-    for s, head in enumerate(heads):
-        place = head_slice(me ^ (s + 1), width)
-        summed_ref[:, place] = x_ref[:, place].astype(F32) + head[...].astype(F32)
+    for d, i, j in places:
+        place = head_slice(me ^ d, width)
+        summed_ref[:, place] = x_ref[:, place].astype(F32) + heads[i][j].astype(F32)
     summed = summed_ref[...]
     inv_rms = lax.rsqrt(jnp.mean(summed * summed, axis=1, keepdims=True) + 1e-06)
     normed_ref[...] = (summed * inv_rms * gain_ref[...]).astype(BF16)
 
 
-def norm_rows(x, gain, heads):
-    return pl.pallas_call(
-        norm_kernel,
+def norm_rows(x, gain, heads, places):
+    return pl.pallas_call(
+        functools.partial(norm_kernel, places),
         out_shape=(jax.ShapeDtypeStruct(x.shape, BF16), jax.ShapeDtypeStruct(x.shape, F32)),
         compiler_params=pltpu.CompilerParams(vmem_limit_bytes=4 * MIB),
         name="norm_rows",
     )(x, gain, *heads)
+
+
+def join_kernel(*refs):
+    assemble(refs[-1], refs[:-1])
+
+
+def join_rows(chunks):
+    rows, width = sum(chunk.shape[0] for chunk in chunks), chunks[0].shape[1]
+    return pl.pallas_call(
+        join_kernel,
+        out_shape=jax.ShapeDtypeStruct((rows, width), BF16),
+        compiler_params=pltpu.CompilerParams(vmem_limit_bytes=4 * MIB),
+        name="join_rows",
+    )(*chunks)
 
 
 def load_weights(refs, place, experts, sems):
@@ -167,32 +254,35 @@
     return copies
 
 
-def back_kernel(size, *refs):
-    chunks, (down_hbm, gate_hbm, up_hbm, back_ref, weights_ref) = refs[:size], refs[size : size + 5]
-    cot, down, down_sems, sems = refs[size + 5 :]
-    experts = down.shape[0]
+def back_kernel(count, *refs):
+    chunks, (first, down_hbm, gate_hbm, up_hbm, back_ref, weights_ref) = refs[:count], refs[count : count + 6]
+    cot, second, down_sems, sems = refs[count + 6 :]
+    split = first.shape[0]
+    experts = split + second.shape[0]
     copies = [
-        pltpu.make_async_copy(down_hbm.at[0, e], down.at[e], down_sems.at[e]) for e in range(experts)
+        pltpu.make_async_copy(down_hbm.at[0, split + e], second.at[e], down_sems.at[e])
+        for e in range(experts - split)
     ]
     for copy in copies:
         copy.start()
     loads = load_weights((gate_hbm, up_hbm), weights_ref, range(experts // 2), sems)
     assemble(cot, chunks)
-    for e in range(experts):
-        copies[e].wait()
-        back_ref[e] = dot(cot[...], down[e], NT)
+    for e in range(split):
+        back_ref[e] = dot(cot[...], first[e], NT)
+    for e, copy in enumerate(copies):
+        copy.wait()
+        back_ref[split + e] = dot(cot[...], second[e], NT)
     for load in loads:
         load.wait()
 
 
-def back_hidden(chunks, w_down, w_gate, w_up):
-    size = len(chunks)
-    own, width = chunks[0].shape
-    _, experts, hidden, _ = w_down.shape
-    rows = size * own
-    return pl.pallas_call(
-        functools.partial(back_kernel, size),
-        in_specs=[IN_VMEM] * size + [IN_HBM] * 3,
+def back_hidden(chunks, first, w_down, w_gate, w_up):
+    _, experts, hidden, width = w_down.shape
+    rows = sum(chunk.shape[0] for chunk in chunks)
+    rest = experts - first.shape[0]
+    return pl.pallas_call(
+        functools.partial(back_kernel, len(chunks)),
+        in_specs=[IN_VMEM] * (len(chunks) + 1) + [IN_HBM] * 3,
         out_specs=(IN_VMEM, ANYWHERE),
         out_shape=(
             jax.ShapeDtypeStruct((experts, rows, hidden), F32),
@@ -200,18 +290,18 @@
         ),
         scratch_shapes=[
             pltpu.VMEM((rows, width), BF16),
-            pltpu.VMEM((experts, hidden, width), BF16),
-            pltpu.SemaphoreType.DMA((experts,)),
+            pltpu.VMEM((rest, hidden, width), BF16),
+            pltpu.SemaphoreType.DMA((rest,)),
             pltpu.SemaphoreType.DMA((experts // 2 * 2,)),
         ],
         compiler_params=pltpu.CompilerParams(vmem_limit_bytes=16 * MIB),
         cost_estimate=pl.CostEstimate(
-            flops=2 * experts * rows * hidden * width,
-            bytes_accessed=experts * hidden * (width * 4 + rows * 4) + rows * width * 2,
+            flops=0,
+            bytes_accessed=0,
             transcendentals=0,
         ),
         name="back_hidden",
-    )(*chunks, hbm(w_down), hbm(w_gate), hbm(w_up))
+    )(*chunks, vmem(first), hbm(w_down), hbm(w_gate), hbm(w_up))
 
 
 def expert_kernel(size, *refs):
@@ -267,6 +357,7 @@
     router = jnp.concatenate([router] * 3, axis=0).astype(BF16)
     small = dot(terms, normed[...], TN)
     small_out[:experts] = small[:experts] + small[experts : 2 * experts] + small[2 * experts :]
+    half = size // 2 * own
     step = width // 4
     for c in range(0, width, step):
         here = slice(c, c + step)
@@ -279,7 +370,9 @@
         grad = grad.astype(BF16)
         for i in range(size // 2):
             kept[i][:, here] = grad[i * own : (i + 1) * own]
-        sent_out[:, here] = grad[size // 2 * own :]
+        sent_out[:half, here] = grad[half:]
+    core = me % 2
+    sent_out[half:] = two_terms(small_out[:, head_slice(1 - core, width // 2)])
 
 
 def experts_backward(chunks, first, w_gate, w_up, back, chosen, router_rows, gain):
@@ -293,7 +386,7 @@
         out_shape=(
             jax.ShapeDtypeStruct((rows, 2 * experts * hidden), BF16),
             jax.ShapeDtypeStruct((rows, experts * hidden), BF16),
-            jax.ShapeDtypeStruct((rows // 2, width), BF16),
+            jax.ShapeDtypeStruct((rows // 2 + 8, width), BF16),
         )
         + (kept,) * (size // 2)
         + (jax.ShapeDtypeStruct((8, width), F32),),
@@ -312,23 +405,37 @@
     )(*chunks, vmem(first), hbm(w_gate), hbm(w_up), back, chosen, router_rows, gain)
 
 
+def two_terms(small):
+    high = small.astype(BF16)
+    low = (small - high.astype(F32)).astype(BF16)
+    return jnp.concatenate([high, low], axis=1)
+
+
+def one_term(terms):
+    half = terms.shape[1] // 2
+    return terms[:, :half].astype(F32) + terms[:, half:].astype(F32)
+
+
 def pair_kernel(count, *refs):
-    kept, (arrived_ref, small_ref, other_ref), outs = refs[:count], refs[count : count + 3], refs[count + 3 :]
-    own = kept[0].shape[0]
+    kept, (arrived_ref, small_ref), outs = refs[:count], refs[count : count + 2], refs[count + 2 :]
+    own, width = kept[0].shape
+    core = lax.axis_index("dp") % 2
+    mine = small_ref[:, head_slice(core, width // 2)]
+    small = two_terms(mine + one_term(arrived_ref[count * own :]))
     for i in range(count):
         arrived = arrived_ref[i * own : (i + 1) * own].astype(F32)
-        outs[i][...] = (kept[i][...].astype(F32) + arrived).astype(BF16)
-    outs[count][...] = small_ref[...] + other_ref[...]
-
-
-def pair_sum(kept, arrived, small, other):
+        outs[i][:own] = (kept[i][...].astype(F32) + arrived).astype(BF16)
+        outs[i][own:] = small
+
+
+def pair_sum(kept, arrived, small):
+    own, width = kept[0].shape
     return pl.pallas_call(
         functools.partial(pair_kernel, len(kept)),
-        out_shape=tuple(jax.ShapeDtypeStruct(k.shape, BF16) for k in kept)
-        + (jax.ShapeDtypeStruct(small.shape, F32),),
+        out_shape=(jax.ShapeDtypeStruct((own + 8, width), BF16),) * len(kept),
         compiler_params=pltpu.CompilerParams(vmem_limit_bytes=4 * MIB),
         name="pair_sum",
-    )(*kept, arrived, small, other)
+    )(*kept, arrived, small)
 
 
 SLOTS = 4
@@ -363,97 +470,107 @@
     write_out(tiles, buffer, sems)
 
 
-def down_kernel(*refs):
-    chunks, (act_ref, down_out, cot, buffer, sems) = refs[:-5], refs[-5:]
+def down_kernel(experts, *refs):
+    cot, buffer, sems = refs[-3:]
+    down_out, (*chunks, act_ref) = refs[-4], refs[: -5 if experts[0] else -4]
     assemble(cot, chunks)
     hidden = down_out.shape[2]
-    step = buffer.shape[1]
     tiles = []
-    for e in range(down_out.shape[1]):
-        for c in range(0, hidden, step):
-            first = e * hidden + c
-            value = lambda first=first: dot(act_ref[:, first : first + step], cot[...], TN)
-            tiles.append((value, down_out.at[0, e, pl.ds(c, step)]))
+    for e in experts:
+        value = lambda e=e: dot(act_ref[:, e * hidden : (e + 1) * hidden], cot[...], TN)
+        tiles.append((value, down_out.at[0, e]))
     write_out(tiles, buffer, sems)
 
 
-def weight_gradients(kernel, chunks, hidden_rows, shapes, step, name):
+def weight_gradients(kernel, chunks, hidden_rows, shapes, name, share=1.0, started=None):
     width = chunks[0].shape[1]
     rows, columns = hidden_rows.shape
     out_bytes = sum(2 * shape[1] * shape[2] * shape[3] for shape in shapes)
+    operands = (*chunks, hidden_rows) + (() if started is None else (started,))
     return pl.pallas_call(
         kernel,
-        out_specs=(pl.BlockSpec(memory_space=pltpu.HBM),) * len(shapes),
+        in_specs=[IN_VMEM] * (len(chunks) + 1) + [IN_HBM] * (started is not None),
+        out_specs=(IN_HBM,) * len(shapes),
         out_shape=tuple(jax.ShapeDtypeStruct(shape, BF16) for shape in shapes),
+        input_output_aliases={} if started is None else {len(operands) - 1: 0},
         scratch_shapes=[
             pltpu.VMEM((rows, width), BF16),
-            pltpu.VMEM((SLOTS, step, shapes[0][3]), BF16),
+            pltpu.VMEM((SLOTS,) + shapes[0][2:], BF16),
             pltpu.SemaphoreType.DMA((SLOTS,)),
         ],
         compiler_params=pltpu.CompilerParams(vmem_limit_bytes=16 * MIB),
         cost_estimate=pl.CostEstimate(
-            flops=2 * rows * columns * width,
-            bytes_accessed=out_bytes + 2 * rows * (columns + width),
+            flops=int(share * 2 * rows * columns * width),
+            bytes_accessed=int(share * out_bytes) + 2 * rows * (columns + width),
             transcendentals=0,
         ),
         name=name,
-    )(*chunks, hidden_rows)
+    )(*operands)
 
 
 def norm_back_kernel(count, *refs):
-    parts, (summed_ref, gain_ref, cot_ref, small_ref, other_ref) = refs[:count], refs[count : count + 5]
-    grad_ref, total_ref = refs[count + 5 : count + 7]
-    sends = refs[count + 7 :]
-    grad_normed = parts[0][...].astype(F32)
+    parts, (summed_ref, gain_ref, cot_ref) = refs[:count], refs[count : count + 3]
+    grad_ref, small_out, *sends = refs[count + 3 :]
+    own = summed_ref.shape[0]
+    grad_normed = parts[0][:own].astype(F32)
     for part in parts[1:]:
-        grad_normed = grad_normed + part[...].astype(F32)
+        grad_normed = grad_normed + part[:own].astype(F32)
     summed = summed_ref[...]
     inv_rms = lax.rsqrt(jnp.mean(summed * summed, axis=1, keepdims=True) + 1e-06)
     scaled = grad_normed * gain_ref[...]
     centre = jnp.mean(scaled * summed, axis=1, keepdims=True)
     grad = inv_rms * scaled - summed * (inv_rms * inv_rms * inv_rms * centre)
     grad_ref[...] = grad + cot_ref[...].astype(F32)
-    me = lax.axis_index("tok")
-    width = sends[0].shape[1]
+    head = sends[0].shape[2]
     for s, send in enumerate(sends):
-        send[...] = grad_ref[:, head_slice(me ^ (s + 1), width)].astype(BF16)
-    total_ref[...] = small_ref[...] + other_ref[...]
-
-
-def norm_backward(parts, summed, gain, cot, small, other):
+        place = head_slice(lax.axis_index("tok") ^ (s + 1), head)
+        send[0] = grad_ref[:, place].astype(BF16)
+    me = lax.axis_index("dp") // 2
+    smalls = jnp.stack([one_term(part[own:]) for part in parts])
+    small = jnp.zeros(smalls.shape[1:], F32)
+    for chip in range(count):
+        for i in range(count):
+            small = small + jnp.where((me ^ i) == chip, smalls[i], 0.0)
+    small_out[...] = small
+
+
+def norm_backward(parts, summed, gain, cot):
     rows, width = summed.shape
     num_tokens = lax.axis_size("tok")
-    head = jax.ShapeDtypeStruct((rows, width // num_tokens), BF16)
+    head = jax.ShapeDtypeStruct((1, rows, width // num_tokens), BF16)
     return pl.pallas_call(
         functools.partial(norm_back_kernel, len(parts)),
         out_shape=(
             jax.ShapeDtypeStruct((rows, width), F32),
-            jax.ShapeDtypeStruct(small.shape, F32),
+            jax.ShapeDtypeStruct((8, width // 2), F32),
         )
         + (head,) * (num_tokens - 1),
         compiler_params=pltpu.CompilerParams(vmem_limit_bytes=4 * MIB),
         name="norm_backward",
-    )(*parts, summed, gain, cot, small, other)
-
-
-def finish_kernel(grad_ref, small_ref, other_ref, *refs):
+    )(*parts, summed, gain, cot)
+
+
+def finish_kernel(places, grad_ref, small_ref, other_ref, *refs):
     heads, (out_ref, router_out, gain_out) = refs[:-3], refs[-3:]
+    core = lax.axis_index("dp") % 2
+    experts, columns = router_out.shape
+    for ref, c in ((small_ref, core), (other_ref, 1 - core)):
+        place = head_slice(c, columns // 2)
+        router_out[:, place] = ref[:experts]
+        gain_out[:, place] = ref[experts : experts + 1]
     me = lax.axis_index("tok")
-    width = heads[0].shape[1]
-    experts = router_out.shape[0]
+    width = heads[0].shape[2]
     own = head_slice(me, width)
     out_ref[0, :, own] = (2.0 * grad_ref[:, own]).astype(BF16)
-    for s, head in enumerate(heads):
-        place = head_slice(me ^ (s + 1), width)
-        out_ref[0, :, place] = (grad_ref[:, place] + head[...].astype(F32)).astype(BF16)
-    router_out[...] = small_ref[:experts] + other_ref[:experts]
-    gain_out[...] = small_ref[experts : experts + 1] + other_ref[experts : experts + 1]
-
-
-def finish(grad_summed, heads, small, other, experts):
+    for d, i, j in places:
+        place = head_slice(me ^ d, width)
+        out_ref[0, :, place] = (grad_ref[:, place] + heads[i][j].astype(F32)).astype(BF16)
+
+
+def finish(grad_summed, heads, places, small, other, experts):
     rows, width = grad_summed.shape
     return pl.pallas_call(
-        finish_kernel,
+        functools.partial(finish_kernel, places),
         out_shape=(
             jax.ShapeDtypeStruct((1, rows, width), BF16),
             jax.ShapeDtypeStruct((experts, width), F32),
@@ -469,43 +586,58 @@
     size = lax.axis_size("dp")
     experts = w_gate.shape[1]
 
-    x, cot, *sends = split_heads(inputs, cotangent)
-    heads = [exchange(v, "tok", s + 1) for s, v in enumerate(sends)]
-    x, norm_gain = after((x, norm_gain))
-    gain, router_rows, chosen = small_operands(norm_gain, router_weight[0].T, route_ids[0].T)
-    heads, gain, router_rows, chosen = after((heads, gain, router_rows, chosen))
-    far_cots = gather_chips(cot)
-    normed, summed = norm_rows(x, gain, heads)
+    x, cot, first, kept = split_heads(inputs, cotangent)
+    heads, items = first_stage(first, kept)
+    heads, items = other_stages(heads, items)
+    cots, distance = [cot], 2
+    while distance < size:
+        cots += [exchange(chunk, "dp", distance) for chunk in cots]
+        distance *= 2
+    norm_gain, heads[1] = after((norm_gain, heads[1]))
+    gain, router_rows, chosen, down = small_operands(
+        norm_gain, router_weight[0].T, route_ids[0].T, w_down
+    )
+    heads, gain, router_rows, chosen, down = after((heads, gain, router_rows, chosen, down))
+    places = from_tokens(heads, items)
+    normed, summed = norm_rows(x, gain, heads, places)
     far_rows = gather_chips(normed)
-    cots = gather_cores(far_cots)
-    back, weights = back_hidden(cots, w_down, w_gate, w_up)
+    cots, summed = after((cots, summed))
+    cots = gather_cores([join_rows(cots)])
+    back, weights = back_hidden(cots, down, w_down, w_gate, w_up)
     far_rows[1:], back = after((far_rows[1:], back))
     rows = gather_cores(far_rows)
     grads, act, sent, *kept, small = experts_backward(
         rows, weights, w_gate, w_up, back, chosen, router_rows, gain
     )
+    sent, act = after((sent, act))
     arrived = exchange(sent, "dp", 1)
-    *pairs, small = pair_sum(kept, arrived, small, exchange(small, "dp", 1))
-    pairs, grads, small = after((pairs, grads, small))
-    parts = pairs[:1] + [exchange(pair, "dp", 2 * s) for s, pair in enumerate(pairs) if s]
-    distance = 2
-    while 4 * distance < size:
-        small = small + exchange(small, "dp", distance)
-        distance *= 2
-    other = exchange(small, "dp", distance)
+    (grad_down,) = weight_gradients(
+        functools.partial(down_kernel, range(1)), cots, act, (w_down.shape,), "grad_down_0", 1 / experts
+    )
+    arrived, grad_down, grads = after((arrived, grad_down, grads))
+    pairs = pair_sum(kept, arrived, small)
+    pairs, grads = after((pairs, grads))
+    parts = [pairs[0]] + [exchange(pair, "dp", 2 * s) for s, pair in enumerate(pairs) if s]
     grad_gate, grad_up = weight_gradients(
-        gate_up_kernel, rows, grads, (w_gate.shape, w_up.shape), width, "grad_gate_up"
-    )
-    parts, grad_gate, grad_up, other = after((parts, grad_gate, grad_up, other))
-    grad_summed, small, *sends = norm_backward(parts, summed, gain, cot, small, other)
+        gate_up_kernel, rows, grads, (w_gate.shape, w_up.shape), "grad_gate_up"
+    )
+    parts, grad_gate, grad_up = after((parts, grad_gate, grad_up))
+    grad_summed, small, *sends = norm_backward(parts, summed, gain, cot)
     sends, act, small = after((sends, act, small))
-    returned = [exchange(v, "tok", s + 1) for s, v in enumerate(sends)]
-    other = exchange(small, "dp", 2 * distance)
+    other = exchange(small, "dp", 1)
+    returned = [exchange(send, "tok", s + 1) for s, send in enumerate(sends)]
     (grad_down,) = weight_gradients(
-        down_kernel, cots, act, (w_down.shape,), w_down.shape[2], "grad_down"
+        functools.partial(down_kernel, range(1, experts)),
+        cots,
+        act,
+        (w_down.shape,),
+        "grad_down",
+        1 - 1 / experts,
+        grad_down,
     )
     returned, grad_down, other = after((returned, grad_down, other))
-    grad_inputs, grad_router, grad_gain = finish(grad_summed, returned, small, other, experts)
+    places = tuple((s + 1, s, 0) for s in range(len(returned)))
+    grad_inputs, grad_router, grad_gain = finish(grad_summed, returned, places, small, other, experts)
     return (
         grad_inputs,
         grad_gate,

time: 68.5 us -> 62.2 us (0.908)
  starting transfers between devices: 28.2 us -> 22.6 us
  waiting for transfers between devices: 7.06 us -> 5.01 us
  Pallas kernels: 32.2 us -> 33.5 us
    ppermute x27 -> x21, starting transfers between devices: 28.2 us -> 22.6 us  [exchange(): return lax.ppermute(value, axis, [(i, i ^ distance) for i in range(size)])]
    ppermute x27 -> x21, waiting for transfers between devices: 7.06 us -> 5.01 us  [exchange(): return lax.ppermute(value, axis, [(i, i ^ distance) for i in range(size)])]
    pallas_call x7 -> x10, Pallas kernels: 18.8 us -> 20.6 us  [the longest x3 12.3 us: weight_gradients(): pl.pallas_call(kernel, in_specs=[IN_VMEM] * (len(chunks) + 1) + [IN_HBM]...]
  transfers between devices with their start and end apart: 27 -> 21, of which waited for: 6 -> 8; matrix products, arithmetic and copies ran while one was open for 0% -> 0% of each run, Pallas kernels for 26% -> 32%
where the time goes in v1:
time: 62.2 us; the launch traced here: 61.9 us
  Pallas kernels  33.5 us (54%)
  starting transfers between devices  22.6 us (36%)
  waiting for transfers between devices  5.01 us (8%)
  between operations  0.8 us (1%)
    ppermute x21, starting transfers between devices, exchange(): return lax.ppermute(value, axis, [(i, i ^ distance) for i in range(size)])  22.6 us
    pallas_call x3, Pallas kernels, weight_gradients(): pl.pallas_call(kernel, in_specs=[IN_VMEM] * (len(chunks) + 1) + [IN_HBM]...  12.3 us
    pallas_call x1, Pallas kernels, experts_backward(): pl.pallas_call(functools.partial(expert_kernel, size), in_specs=[IN_VMEM]...  11.7 us
    pallas_call x1, Pallas kernels, back_hidden(): pl.pallas_call(functools.partial(back_kernel, len(chunks)), in_specs=[IN_...  5.04 us
    ppermute x21, waiting for transfers between devices, exchange(): return lax.ppermute(value, axis, [(i, i ^ distance) for i in range(size)])  5.01 us
    pallas_call x1, Pallas kernels, small_operands(): pl.pallas_call(small_kernel, in_specs=[IN_HBM] * 4, out_specs=(IN_VMEM,)...  2.26 us
  transfers between devices with their start and end apart: 21, of which 8 were waited for; matrix products, arithmetic and copies ran while one was open for 0% of the time, Pallas kernels for 32%

profile of v1, /device:TPU:0, one launch (start us, length us, event | category | flops | bytes accessed | tf_op | source)
XLA Modules:
  0.0 61.9 jit_solution(13532730891226394981)
XLA Ops:
  0.6 1.0 %split_heads.1 = (bf16[32,2048]{1,0:T(8,128)(2,1)S(1)}, bf16[32,2048]{1,0:T(8,128)(2,1)S(1)}, bf16[2,32,512]{2,1,0:T(8,128)(2,1)S(1)}, bf16[1,32,512]{2,1,0:T(8,128)(2,1)S(1)}) custom-call(bf16[1,32,2048]{2,1,0:T(8,128)(2,1)} %x_hbm.1, bf16[1,32,2048]{2,1,0:T(8,128)(2,1)} %cot_hbm.1), custom_call_target="tpu_custom_call" | custom-call | tf_op jit(solution)/shard_map/split_heads/pallas_call | solution.py:145
  1.6 3.0 %collective-permute-start.5 = (bf16[32,2048]{1,0:T(8,128)(2,1)S(1)}, bf16[32,2048]{1,0:T(8,128)(2,1)S(1)}, u32[]{:S(2)}, u32[]{:S(2)}) collective-permute-start(bf16[32,2048]{1,0:T(8,128)(2,1)S(1)} %get-tuple-element.100.refs_0_.refs_6_), channel_id=1, source_target_pairs={{0,8},{4,12},{8,0},{12,4},{16,24},{20,28},{24,16},{28,20},{1,9},{5... | collective-permute-start | bytes 393224 | tf_op jit(solution)/shard_map/ppermute | solution.py:26
  4.6 1.6 %collective-permute-start = (bf16[2,32,512]{2,1,0:T(8,128)(2,1)S(1)}, bf16[2,32,512]{2,1,0:T(8,128)(2,1)S(1)}, u32[]{:S(2)}, u32[]{:S(2)}) collective-permute-start(bf16[2,32,512]{2,1,0:T(8,128)(2,1)S(1)} %get-tuple-element.86), channel_id=1, source_target_pairs={{0,1},{1,0},{2,3},{3,2},{4,5},{5,4},{6,7},{7,6},{8,9},{9,8},{10,11... | collective-permute-start | bytes 196616 | tf_op jit(solution)/shard_map/ppermute | solution.py:26
  6.2 1.5 %collective-permute-start.6 = (bf16[32,2048]{1,0:T(8,128)(2,1)S(1)}, bf16[32,2048]{1,0:T(8,128)(2,1)S(1)}, u32[]{:S(2)}, u32[]{:S(2)}) collective-permute-start(bf16[32,2048]{1,0:T(8,128)(2,1)S(1)} %get-tuple-element.100.refs_0_.refs_6_), channel_id=1, source_target_pairs={{0,16},{4,20},{8,24},{12,28},{16,0},{20,4},{24,8},{28,12},{1,17},{... | collective-permute-start | bytes 393224 | tf_op jit(solution)/shard_map/ppermute | solution.py:26
  7.7 1.2 %collective-permute-done.refs_1_ = bf16[2,32,512]{2,1,0:T(8,128)(2,1)S(1)} collective-permute-done((bf16[2,32,512]{2,1,0:T(8,128)(2,1)S(1)}, bf16[2,32,512]{2,1,0:T(8,128)(2,1)S(1)}, u32[]{:S(2)}, u32[]{:S(2)}) %collective-permute-start) | collective-permute-done | bytes 65568 | tf_op jit(solution)/shard_map/ppermute | solution.py:26
  8.9 2.6 %collective-permute-start.1 = (bf16[2,32,512]{2,1,0:T(8,128)(2,1)S(1)}, bf16[2,32,512]{2,1,0:T(8,128)(2,1)S(1)}, u32[]{:S(2)}, u32[]{:S(2)}) collective-permute-start(bf16[2,32,512]{2,1,0:T(8,128)(2,1)S(1)} %pack_heads.1), channel_id=1, source_target_pairs={{0,2},{1,3},{2,0},{3,1},{4,6},{5,7},{6,4},{7,5},{8,10},{9,11},{10,... | collective-permute-start | bytes 196616 | tf_op jit(solution)/shard_map/ppermute | solution.py:26
  11.5 1.5 %collective-permute-start.7 = (bf16[32,2048]{1,0:T(8,128)(2,1)S(1)}, bf16[32,2048]{1,0:T(8,128)(2,1)S(1)}, u32[]{:S(2)}, u32[]{:S(2)}) collective-permute-start(bf16[32,2048]{1,0:T(8,128)(2,1)S(1)} %collective-permute-done.5.refs_1_), channel_id=1, source_target_pairs={{0,16},{4,20},{8,24},{12,28},{16,0},{20,4},{24,8},{28,12},{1,17},{... | collective-permute-start | bytes 393224 | tf_op jit(solution)/shard_map/ppermute | solution.py:26
  13.0 2.3 %small_operands.1 = (f32[1,2048]{1,0:T(1,128)S(1)}, bf16[4,2048]{1,0:T(4,128)(2,1)S(1)}, f32[256,8]{1,0:T(8,128)S(1)}, bf16[2,512,2048]{2,1,0:T(8,128)(2,1)S(1)}) custom-call(f32[1,2048]{1,0:T(1,128)} %gain_hbm, bf16[4,2048]{1,0:T(4,128)(2,1)} %bitcast.10, s32[2,256]{1,0:T(2,128)} %bitcast.11, bf16[1,4,512,2048]{3,2,1,0:T(8,128)(2,1)} %refs_3_.1), custom_call_target="tpu_custom_call" | custom-call | flops 68719476736 | bytes 33554432 | tf_op jit(solution)/shard_map/small_operands/pallas_call | solution.py:189
  15.5 1.0 %collective-permute-done.7.refs_3_ = bf16[32,2048]{1,0:T(8,128)(2,1)S(1)} collective-permute-done((bf16[32,2048]{1,0:T(8,128)(2,1)S(1)}, bf16[32,2048]{1,0:T(8,128)(2,1)S(1)}, u32[]{:S(2)}, u32[]{:S(2)}) %collective-permute-start.7) | collective-permute-done | bytes 131104 | tf_op jit(solution)/shard_map/ppermute | solution.py:26
  16.6 1.6 %collective-permute-start.4 = (bf16[32,2048]{1,0:T(8,128)(2,1)S(1)}, bf16[32,2048]{1,0:T(8,128)(2,1)S(1)}, u32[]{:S(2)}, u32[]{:S(2)}) collective-permute-start(bf16[32,2048]{1,0:T(8,128)(2,1)S(1)} %get-tuple-element.97.refs_0_), channel_id=1, source_target_pairs={{0,24},{4,28},{8,16},{12,20},{16,8},{20,12},{24,0},{28,4},{1,25},{... | collective-permute-start | bytes 393224 | tf_op jit(solution)/shard_map/ppermute | solution.py:26
  18.6 1.5 %collective-permute-start.2 = (bf16[32,2048]{1,0:T(8,128)(2,1)S(1)}, bf16[32,2048]{1,0:T(8,128)(2,1)S(1)}, u32[]{:S(2)}, u32[]{:S(2)}) collective-permute-start(bf16[32,2048]{1,0:T(8,128)(2,1)S(1)} %get-tuple-element.97.refs_0_), channel_id=1, source_target_pairs={{0,8},{4,12},{8,0},{12,4},{16,24},{20,28},{24,16},{28,20},{1,9},{5... | collective-permute-start | bytes 393224 | tf_op jit(solution)/shard_map/ppermute | solution.py:26
  20.1 5.0 %back_hidden.1 = (f32[4,256,512]{2,1,0:T(8,128)S(1)}, bf16[2048,2048]{1,0:T(8,128)(2,1)S(1)}) custom-call(bf16[128,2048]{1,0:T(8,128)(2,1)S(1)} %join_rows.1.refs_0_, bf16[128,2048]{1,0:T(8,128)(2,1)S(1)} %collective-permute-done.8.refs_1_, bf16[2,512,2048]{2,1,0:T(8,128)(2,1)S(1)} %get-tuple-element.104.refs_2_, bf16[1,4,512,2048]{3,2,1,0:T(8,128)(2,1)} %refs_3_.1, ...), custom_call_target="tpu_custom_call" | custom-call | tf_op jit(solution)/shard_map/back_hidden/pallas_call | solution.py:283
  25.2 1.0 %collective-permute-done.3.refs_2_ = bf16[32,2048]{1,0:T(8,128)(2,1)S(1)} collective-permute-done((bf16[32,2048]{1,0:T(8,128)(2,1)S(1)}, bf16[32,2048]{1,0:T(8,128)(2,1)S(1)}, u32[]{:S(2)}, u32[]{:S(2)}) %collective-permute-start.3) | collective-permute-done | bytes 131104 | tf_op jit(solution)/shard_map/ppermute | solution.py:26
  26.8 0.8 %collective-permute-done.10.refs_5_ = bf16[32,2048]{1,0:T(8,128)(2,1)S(1)} collective-permute-done((bf16[32,2048]{1,0:T(8,128)(2,1)S(1)}, bf16[32,2048]{1,0:T(8,128)(2,1)S(1)}, u32[]{:S(2)}, u32[]{:S(2)}) %collective-permute-start.10) | collective-permute-done | bytes 131104 | tf_op jit(solution)/shard_map/ppermute | solution.py:26
  28.2 11.7 %experts_backward.1 = (bf16[256,4096]{1,0:T(8,128)(2,1)S(1)}, bf16[256,2048]{1,0:T(8,128)(2,1)S(1)}, bf16[136,2048]{1,0:T(8,128)(2,1)S(1)}, bf16[32,2048]{1,0:T(...) custom-call(bf16[32,2048]{1,0:T(8,128)(2,1)S(1)} %get-tuple-element., ...), custom_call_target="tpu_custom_call" | custom-call | flops 8589934592 | bytes 24117248 | tf_op jit(solution)/shard_map/experts_backward/pallas_call | solution.py:383
  40.1 2.1 %grad_down_0.1.refs_3_ = bf16[1,4,512,2048]{3,2,1,0:T(8,128)(2,1)} custom-call(bf16[128,2048]{1,0:T(8,128)(2,1)S(1)} %join_rows.1.refs_0_, bf16[128,2048]{1,0:T(8,128)(2,1)S(1)} %collective-permute-done.8.refs_1_, bf16[256,2048]{1,0:T(8,128)(2,1)S(1)} %get-tuple-element.150.refs_2_), custom_call_target="tpu_custom_call" | custom-call | flops 536870912 | bytes 4194304 | tf_op jit(solution)/shard_map/grad_down_0/pallas_call | solution.py:490
  42.9 1.4 %collective-permute-start.15 = (bf16[40,2048]{1,0:T(8,128)(2,1)S(1)}, bf16[40,2048]{1,0:T(8,128)(2,1)S(1)}, u32[]{:S(2)}, u32[]{:S(2)}) collective-permute-start(bf16[40,2048]{1,0:T(8,128)(2,1)S(1)} %get-tuple-element.131), channel_id=1, source_target_pairs={{0,16},{4,20},{8,24},{12,28},{16,0},{20,4},{24,8},{28,12},{1,17},{... | collective-permute-start | bytes 491528 | tf_op jit(solution)/shard_map/ppermute | solution.py:26
  44.4 1.5 %collective-permute-start.16 = (bf16[40,2048]{1,0:T(8,128)(2,1)S(1)}, bf16[40,2048]{1,0:T(8,128)(2,1)S(1)}, u32[]{:S(2)}, u32[]{:S(2)}) collective-permute-start(bf16[40,2048]{1,0:T(8,128)(2,1)S(1)} %get-tuple-element.132), channel_id=1, source_target_pairs={{0,24},{4,28},{8,16},{12,20},{16,8},{20,12},{24,0},{28,4},{1,25},{... | collective-permute-start | bytes 491528 | tf_op jit(solution)/shard_map/ppermute | solution.py:26
  45.9 6.7 %grad_gate_up.1 = (bf16[1,4,2048,512]{3,2,1,0:T(8,128)(2,1)}, bf16[1,4,2048,512]{3,2,1,0:T(8,128)(2,1)}) custom-call(bf16[32,2048]{1,0:T(8,128)(2,1)S(1)} %get-tuple-element.97.refs_0_, bf16[32,2048]{1,0:T(8,128)(2,1)S(1)} %collective-permute-done.2.refs_1_, bf16[32,2048]{1,0:T(8,128)(2,1)S(1)} %collective-permute-done.3.refs_2_, ...), custom_call_target="tpu_custom_call" | custom-call | flops 4294967296 | bytes 19922944 | tf_op jit(solution)/shard_map/grad_gate_up/pallas_call | solution.py:490
  52.9 1.6 %collective-permute-start.17 = (bf16[1,32,512]{2,1,0:T(8,128)(2,1)S(1)}, bf16[1,32,512]{2,1,0:T(8,128)(2,1)S(1)}, u32[]{:S(2)}, u32[]{:S(2)}) collective-permute-start(bf16[1,32,512]{2,1,0:T(8,128)(2,1)S(1)} %get-tuple-element.147), channel_id=1, source_target_pairs={{0,1},{1,0},{2,3},{3,2},{4,5},{5,4},{6,7},{7,6},{8,9},{9,8},{10,11... | collective-permute-start | bytes 98312 | tf_op jit(solution)/shard_map/ppermute | solution.py:26
  54.5 1.0 %collective-permute-start.18 = (bf16[1,32,512]{2,1,0:T(8,128)(2,1)S(1)}, bf16[1,32,512]{2,1,0:T(8,128)(2,1)S(1)}, u32[]{:S(2)}, u32[]{:S(2)}) collective-permute-start(bf16[1,32,512]{2,1,0:T(8,128)(2,1)S(1)} %get-tuple-element.148), channel_id=1, source_target_pairs={{0,2},{1,3},{2,0},{3,1},{4,6},{5,7},{6,4},{7,5},{8,10},{9,11},{10,... | collective-permute-start | bytes 98312 | tf_op jit(solution)/shard_map/ppermute | solution.py:26
  55.5 1.8 %collective-permute-start.19 = (bf16[1,32,512]{2,1,0:T(8,128)(2,1)S(1)}, bf16[1,32,512]{2,1,0:T(8,128)(2,1)S(1)}, u32[]{:S(2)}, u32[]{:S(2)}) collective-permute-start(bf16[1,32,512]{2,1,0:T(8,128)(2,1)S(1)} %get-tuple-element.149), channel_id=1, source_target_pairs={{0,3},{1,2},{2,1},{3,0},{4,7},{5,6},{6,5},{7,4},{8,11},{9,10},{10,... | collective-permute-start | bytes 98312 | tf_op jit(solution)/shard_map/ppermute | solution.py:26
  57.3 3.5 %grad_down.1 = bf16[1,4,512,2048]{3,2,1,0:T(8,128)(2,1)} custom-call(bf16[128,2048]{1,0:T(8,128)(2,1)S(1)} %join_rows.1.refs_0_, bf16[128,2048]{1,0:T(8,128)(2,1)S(1)} %collective-permute-done.8.refs_1_, bf16[256,2048]{1,0:T(8,128)(2,1)S(1)} %get-tuple-element.150.refs_2_, bf16[1,4,512,2048]{3,2,1,0:T(8,128)(2,1)} %grad_down_0.1.refs_3_), custom_call_target="tpu_custom_call", output_to_operand_aliasing={{}: (3, {})} | custom-call | flops 1610612736 | bytes 8388608 | tf_op jit(solution)/shard_map/grad_down/pallas_call | solution.py:490
  61.2 0.7 %finish.1 = (bf16[1,32,2048]{2,1,0:T(8,128)(2,1)}, f32[4,2048]{1,0:T(4,128)}, f32[1,2048]{1,0:T(1,128)}) custom-call(f32[32,2048]{1,0:T(8,128)S(1)} %get-tuple-element.141.grad_ref, f32[8,1024]{1,0:T(8,128)S(1)} %get-tuple-element.146.small_ref, f32[8,1024]{1,0:T(8,128)S(1)} %collective-permute-done.20.other_ref, ...), custom_call_target="tpu_custom_call" | custom-call | tf_op jit(solution)/shard_map/finish/pallas_call | solution.py:572
  (31 shorter events, 3.5 us)
Async XLA Ops:
  1.6 9.9 %collective-permute-start.5 = (bf16[32,2048]{1,0:T(8,128)(2,1)S(1)}, bf16[32,2048]{1,0:T(8,128)(2,1)S(1)}, u32[]{:S(2)}, u32[]{:S(2)}) collective-permute-start(bf16[32,2048]{1,0:T(8,128)(2,1)S(1)} %get-tuple-element.100.refs_0_.refs_6_), channel_id=1, source_target_pairs={{0,8},{4,12},{8,0},{12,4},{16,24},{20,28},{24,16},{28,20},{1,9},{5... | collective-permute-start | bytes 393224 | tf_op jit(solution)/shard_map/ppermute | solution.py:26
  4.6 4.3 %collective-permute-start = (bf16[2,32,512]{2,1,0:T(8,128)(2,1)S(1)}, bf16[2,32,512]{2,1,0:T(8,128)(2,1)S(1)}, u32[]{:S(2)}, u32[]{:S(2)}) collective-permute-start(bf16[2,32,512]{2,1,0:T(8,128)(2,1)S(1)} %get-tuple-element.86), channel_id=1, source_target_pairs={{0,1},{1,0},{2,3},{3,2},{4,5},{5,4},{6,7},{7,6},{8,9},{9,8},{10,11... | collective-permute-start | bytes 196616 | tf_op jit(solution)/shard_map/ppermute | solution.py:26
  6.2 9.3 %collective-permute-start.6 = (bf16[32,2048]{1,0:T(8,128)(2,1)S(1)}, bf16[32,2048]{1,0:T(8,128)(2,1)S(1)}, u32[]{:S(2)}, u32[]{:S(2)}) collective-permute-start(bf16[32,2048]{1,0:T(8,128)(2,1)S(1)} %get-tuple-element.100.refs_0_.refs_6_), channel_id=1, source_target_pairs={{0,16},{4,20},{8,24},{12,28},{16,0},{20,4},{24,8},{28,12},{1,17},{... | collective-permute-start | bytes 393224 | tf_op jit(solution)/shard_map/ppermute | solution.py:26
  8.9 6.4 %collective-permute-start.1 = (bf16[2,32,512]{2,1,0:T(8,128)(2,1)S(1)}, bf16[2,32,512]{2,1,0:T(8,128)(2,1)S(1)}, u32[]{:S(2)}, u32[]{:S(2)}) collective-permute-start(bf16[2,32,512]{2,1,0:T(8,128)(2,1)S(1)} %pack_heads.1), channel_id=1, source_target_pairs={{0,2},{1,3},{2,0},{3,1},{4,6},{5,7},{6,4},{7,5},{8,10},{9,11},{10,... | collective-permute-start | bytes 196616 | tf_op jit(solution)/shard_map/ppermute | solution.py:26
  11.5 5.0 %collective-permute-start.7 = (bf16[32,2048]{1,0:T(8,128)(2,1)S(1)}, bf16[32,2048]{1,0:T(8,128)(2,1)S(1)}, u32[]{:S(2)}, u32[]{:S(2)}) collective-permute-start(bf16[32,2048]{1,0:T(8,128)(2,1)S(1)} %collective-permute-done.5.refs_1_), channel_id=1, source_target_pairs={{0,16},{4,20},{8,24},{12,28},{16,0},{20,4},{24,8},{28,12},{1,17},{... | collective-permute-start | bytes 393224 | tf_op jit(solution)/shard_map/ppermute | solution.py:26
  16.5 3.6 %collective-permute-start.8 = (bf16[128,2048]{1,0:T(8,128)(2,1)S(1)}, bf16[128,2048]{1,0:T(8,128)(2,1)S(1)}, u32[]{:S(2)}, u32[]{:S(2)}) collective-permute-start(bf16[128,2048]{1,0:T(8,128)(2,1)S(1)} %join_rows.1.refs_0_), channel_id=1, source_target_pairs={{0,4},{4,0},{8,12},{12,8},{16,20},{20,16},{24,28},{28,24},{1,5},{5... | collective-permute-start | bytes 1572872 | tf_op jit(solution)/shard_map/ppermute | solution.py:26
  16.6 8.6 %collective-permute-start.4 = (bf16[32,2048]{1,0:T(8,128)(2,1)S(1)}, bf16[32,2048]{1,0:T(8,128)(2,1)S(1)}, u32[]{:S(2)}, u32[]{:S(2)}) collective-permute-start(bf16[32,2048]{1,0:T(8,128)(2,1)S(1)} %get-tuple-element.97.refs_0_), channel_id=1, source_target_pairs={{0,24},{4,28},{8,16},{12,20},{16,8},{20,12},{24,0},{28,4},{1,25},{... | collective-permute-start | bytes 393224 | tf_op jit(solution)/shard_map/ppermute | solution.py:26
  18.1 8.1 %collective-permute-start.3 = (bf16[32,2048]{1,0:T(8,128)(2,1)S(1)}, bf16[32,2048]{1,0:T(8,128)(2,1)S(1)}, u32[]{:S(2)}, u32[]{:S(2)}) collective-permute-start(bf16[32,2048]{1,0:T(8,128)(2,1)S(1)} %get-tuple-element.97.refs_0_), channel_id=1, source_target_pairs={{0,16},{4,20},{8,24},{12,28},{16,0},{20,4},{24,8},{28,12},{1,17},{... | collective-permute-start | bytes 393224 | tf_op jit(solution)/shard_map/ppermute | solution.py:26
  18.6 7.7 %collective-permute-start.2 = (bf16[32,2048]{1,0:T(8,128)(2,1)S(1)}, bf16[32,2048]{1,0:T(8,128)(2,1)S(1)}, u32[]{:S(2)}, u32[]{:S(2)}) collective-permute-start(bf16[32,2048]{1,0:T(8,128)(2,1)S(1)} %get-tuple-element.97.refs_0_), channel_id=1, source_target_pairs={{0,8},{4,12},{8,0},{12,4},{16,24},{20,28},{24,16},{28,20},{1,9},{5... | collective-permute-start | bytes 393224 | tf_op jit(solution)/shard_map/ppermute | solution.py:26
  20.1 6.7 %collective-permute-start.9 = (bf16[32,2048]{1,0:T(8,128)(2,1)S(1)}, bf16[32,2048]{1,0:T(8,128)(2,1)S(1)}, u32[]{:S(2)}, u32[]{:S(2)}) collective-permute-start(bf16[32,2048]{1,0:T(8,128)(2,1)S(1)} %get-tuple-element.97.refs_0_), channel_id=1, source_target_pairs={{0,4},{4,0},{8,12},{12,8},{16,20},{20,16},{24,28},{28,24},{1,5},{5... | collective-permute-start | bytes 393224 | tf_op jit(solution)/shard_map/ppermute | solution.py:26
  26.3 1.3 %collective-permute-start.10 = (bf16[32,2048]{1,0:T(8,128)(2,1)S(1)}, bf16[32,2048]{1,0:T(8,128)(2,1)S(1)}, u32[]{:S(2)}, u32[]{:S(2)}) collective-permute-start(bf16[32,2048]{1,0:T(8,128)(2,1)S(1)} %collective-permute-done.2.refs_1_), channel_id=1, source_target_pairs={{0,4},{4,0},{8,12},{12,8},{16,20},{20,16},{24,28},{28,24},{1,5},{5... | collective-permute-start | bytes 393224 | tf_op jit(solution)/shard_map/ppermute | solution.py:26
  26.3 1.5 %collective-permute-start.11 = (bf16[32,2048]{1,0:T(8,128)(2,1)S(1)}, bf16[32,2048]{1,0:T(8,128)(2,1)S(1)}, u32[]{:S(2)}, u32[]{:S(2)}) collective-permute-start(bf16[32,2048]{1,0:T(8,128)(2,1)S(1)} %collective-permute-done.3.refs_2_), channel_id=1, source_target_pairs={{0,4},{4,0},{8,12},{12,8},{16,20},{20,16},{24,28},{28,24},{1,5},{5... | collective-permute-start | bytes 393224 | tf_op jit(solution)/shard_map/ppermute | solution.py:26
  26.8 1.3 %collective-permute-start.12 = (bf16[32,2048]{1,0:T(8,128)(2,1)S(1)}, bf16[32,2048]{1,0:T(8,128)(2,1)S(1)}, u32[]{:S(2)}, u32[]{:S(2)}) collective-permute-start(bf16[32,2048]{1,0:T(8,128)(2,1)S(1)} %collective-permute-done.4.refs_3_), channel_id=1, source_target_pairs={{0,4},{4,0},{8,12},{12,8},{16,20},{20,16},{24,28},{28,24},{1,5},{5... | collective-permute-start | bytes 393224 | tf_op jit(solution)/shard_map/ppermute | solution.py:26
  39.8 2.3 %collective-permute-start.13 = (bf16[136,2048]{1,0:T(8,128)(2,1)S(1)}, bf16[136,2048]{1,0:T(8,128)(2,1)S(1)}, u32[]{:S(2)}, u32[]{:S(2)}) collective-permute-start(bf16[136,2048]{1,0:T(8,128)(2,1)S(1)} %get-tuple-element.119), channel_id=1, source_target_pairs={{0,4},{4,0},{8,12},{12,8},{16,20},{20,16},{24,28},{28,24},{1,5},{5... | collective-permute-start | bytes 1671176 | tf_op jit(solution)/shard_map/ppermute | solution.py:26
  42.3 10.3 %collective-permute-start.14 = (bf16[40,2048]{1,0:T(8,128)(2,1)S(1)}, bf16[40,2048]{1,0:T(8,128)(2,1)S(1)}, u32[]{:S(2)}, u32[]{:S(2)}) collective-permute-start(bf16[40,2048]{1,0:T(8,128)(2,1)S(1)} %get-tuple-element.130), channel_id=1, source_target_pairs={{0,8},{4,12},{8,0},{12,4},{16,24},{20,28},{24,16},{28,20},{1,9},{5... | collective-permute-start | bytes 491528 | tf_op jit(solution)/shard_map/ppermute | solution.py:26
  42.9 9.7 %collective-permute-start.15 = (bf16[40,2048]{1,0:T(8,128)(2,1)S(1)}, bf16[40,2048]{1,0:T(8,128)(2,1)S(1)}, u32[]{:S(2)}, u32[]{:S(2)}) collective-permute-start(bf16[40,2048]{1,0:T(8,128)(2,1)S(1)} %get-tuple-element.131), channel_id=1, source_target_pairs={{0,16},{4,20},{8,24},{12,28},{16,0},{20,4},{24,8},{28,12},{1,17},{... | collective-permute-start | bytes 491528 | tf_op jit(solution)/shard_map/ppermute | solution.py:26
  44.4 8.3 %collective-permute-start.16 = (bf16[40,2048]{1,0:T(8,128)(2,1)S(1)}, bf16[40,2048]{1,0:T(8,128)(2,1)S(1)}, u32[]{:S(2)}, u32[]{:S(2)}) collective-permute-start(bf16[40,2048]{1,0:T(8,128)(2,1)S(1)} %get-tuple-element.132), channel_id=1, source_target_pairs={{0,24},{4,28},{8,16},{12,20},{16,8},{20,12},{24,0},{28,4},{1,25},{... | collective-permute-start | bytes 491528 | tf_op jit(solution)/shard_map/ppermute | solution.py:26
  52.9 7.9 %collective-permute-start.17 = (bf16[1,32,512]{2,1,0:T(8,128)(2,1)S(1)}, bf16[1,32,512]{2,1,0:T(8,128)(2,1)S(1)}, u32[]{:S(2)}, u32[]{:S(2)}) collective-permute-start(bf16[1,32,512]{2,1,0:T(8,128)(2,1)S(1)} %get-tuple-element.147), channel_id=1, source_target_pairs={{0,1},{1,0},{2,3},{3,2},{4,5},{5,4},{6,7},{7,6},{8,9},{9,8},{10,11... | collective-permute-start | bytes 98312 | tf_op jit(solution)/shard_map/ppermute | solution.py:26
  54.5 6.3 %collective-permute-start.18 = (bf16[1,32,512]{2,1,0:T(8,128)(2,1)S(1)}, bf16[1,32,512]{2,1,0:T(8,128)(2,1)S(1)}, u32[]{:S(2)}, u32[]{:S(2)}) collective-permute-start(bf16[1,32,512]{2,1,0:T(8,128)(2,1)S(1)} %get-tuple-element.148), channel_id=1, source_target_pairs={{0,2},{1,3},{2,0},{3,1},{4,6},{5,7},{6,4},{7,5},{8,10},{9,11},{10,... | collective-permute-start | bytes 98312 | tf_op jit(solution)/shard_map/ppermute | solution.py:26
  55.5 5.7 %collective-permute-start.19 = (bf16[1,32,512]{2,1,0:T(8,128)(2,1)S(1)}, bf16[1,32,512]{2,1,0:T(8,128)(2,1)S(1)}, u32[]{:S(2)}, u32[]{:S(2)}) collective-permute-start(bf16[1,32,512]{2,1,0:T(8,128)(2,1)S(1)} %get-tuple-element.149), channel_id=1, source_target_pairs={{0,3},{1,2},{2,1},{3,0},{4,7},{5,6},{6,5},{7,4},{8,11},{9,10},{10,... | collective-permute-start | bytes 98312 | tf_op jit(solution)/shard_map/ppermute | solution.py:26
  57.3 3.9 %collective-permute-start.20 = (f32[8,1024]{1,0:T(8,128)S(1)}, f32[8,1024]{1,0:T(8,128)S(1)}, u32[]{:S(2)}, u32[]{:S(2)}) collective-permute-start(f32[8,1024]{1,0:T(8,128)S(1)} %get-tuple-element.146.small_ref), channel_id=1, source_target_pairs={{0,4},{4,0},{8,12},{12,8},{16,20},{20,16},{24,28},{28,24},{1,5},{5... | collective-permute-start | bytes 98312 | tf_op jit(solution)/shard_map/ppermute | solution.py:26

commit v2 on v1

--- a/solution.py
+++ b/solution.py
@@ -1,4 +1,5 @@
 import functools
+import math
 
 import jax
 import jax.numpy as jnp
@@ -439,71 +440,80 @@
 
 
 SLOTS = 4
-
-
-def write_out(tiles, buffer, sems):
+DOWN_MIDDLE = 2
+
+
+def write_out(tiles, buffers, sems):
     copies = []
     for i, (value, destination) in enumerate(tiles):
         slot = i % SLOTS
         if i >= SLOTS:
             copies[i - SLOTS].wait()
-        buffer[slot] = value().astype(BF16)
-        copies.append(pltpu.make_async_copy(buffer.at[slot], destination, sems.at[slot]))
+        rows, columns = destination.shape
+        buffer = next(ref for ref in buffers if ref.shape[2] == columns and ref.shape[1] >= rows)
+        place = buffer.at[slot, pl.ds(0, rows)]
+        place[...] = value().astype(BF16)
+        copies.append(pltpu.make_async_copy(place, destination, sems.at[slot]))
         copies[-1].start()
     for copy in copies[-SLOTS:]:
         copy.wait()
 
 
-def gate_up_kernel(*refs):
-    chunks, (grads_ref, gate_out, up_out, normed, buffer, sems) = refs[:-6], refs[-6:]
-    assemble(normed, chunks)
-    width = normed.shape[1]
-    hidden = gate_out.shape[3]
-    step = buffer.shape[1]
+def weight_kernel(counts, down_experts, *refs):
+    normed_chunks, refs = refs[: counts[0]], refs[counts[0] :]
+    cot_chunks, refs = refs[: counts[1]], refs[counts[1] :]
+    buffers, sems = refs[-3:-1], refs[-1]
     tiles = []
-    for e in range(gate_out.shape[1]):
-        for i, out in enumerate((gate_out, up_out)):
-            columns = slice((2 * e + i) * hidden, (2 * e + i + 1) * hidden)
-            for c in range(0, width, step):
-                value = lambda c=c, columns=columns: dot(normed[:, c : c + step], grads_ref[:, columns], TN)
-                tiles.append((value, out.at[0, e, pl.ds(c, step)]))
-    write_out(tiles, buffer, sems)
-
-
-def down_kernel(experts, *refs):
-    cot, buffer, sems = refs[-3:]
-    down_out, (*chunks, act_ref) = refs[-4], refs[: -5 if experts[0] else -4]
-    assemble(cot, chunks)
+    if counts[0]:
+        grads_ref, act_ref = refs[:2]
+        gate_out, up_out, down_out, normed, cot = refs[-8:-3]
+        assemble(normed, normed_chunks)
+        hidden = gate_out.shape[3]
+        for e in range(gate_out.shape[1]):
+            for i, out in enumerate((gate_out, up_out)):
+                first = (2 * e + i) * hidden
+                columns = slice(first, first + hidden)
+                value = lambda columns=columns: dot(normed[...], grads_ref[:, columns], TN)
+                tiles.append((value, out.at[0, e]))
+    else:
+        act_ref = refs[0]
+        down_out, cot = refs[-5:-3]
+    assemble(cot, cot_chunks)
     hidden = down_out.shape[2]
-    tiles = []
-    for e in experts:
-        value = lambda e=e: dot(act_ref[:, e * hidden : (e + 1) * hidden], cot[...], TN)
-        tiles.append((value, down_out.at[0, e]))
-    write_out(tiles, buffer, sems)
-
-
-def weight_gradients(kernel, chunks, hidden_rows, shapes, name, share=1.0, started=None):
-    width = chunks[0].shape[1]
-    rows, columns = hidden_rows.shape
-    out_bytes = sum(2 * shape[1] * shape[2] * shape[3] for shape in shapes)
-    operands = (*chunks, hidden_rows) + (() if started is None else (started,))
-    return pl.pallas_call(
-        kernel,
-        in_specs=[IN_VMEM] * (len(chunks) + 1) + [IN_HBM] * (started is not None),
+    for e in down_experts:
+        parts = 2 if e == down_experts[-1] else 1
+        step = hidden // parts
+        for first in range(0, hidden, step):
+            columns = slice(e * hidden + first, e * hidden + first + step)
+            value = lambda columns=columns: dot(act_ref[:, columns], cot[...], TN)
+            tiles.append((value, down_out.at[0, e, pl.ds(first, step)]))
+    write_out(tiles, buffers, sems)
+
+
+def weight_gradients(cot_chunks, act, down_shape, down_experts, name, started=None, gate_up=None):
+    width = cot_chunks[0].shape[1]
+    rows = act.shape[0]
+    normed_chunks, grads, shapes = gate_up or ([], None, [])
+    operands = [*normed_chunks, *cot_chunks, *([grads] if gate_up else []), act]
+    specs = [IN_VMEM] * len(operands)
+    if started is not None:
+        operands, specs = operands + [started], specs + [IN_HBM]
+    shapes = [*shapes, down_shape]
+    tile = down_shape[2] * width
+    flops = 2 * rows * (tile * len(down_experts) + sum(math.prod(shape) for shape in shapes[:-1]))
+    slot = (down_shape[2], width)
+    return pl.pallas_call(
+        functools.partial(weight_kernel, (len(normed_chunks), len(cot_chunks)), down_experts),
+        in_specs=specs,
         out_specs=(IN_HBM,) * len(shapes),
         out_shape=tuple(jax.ShapeDtypeStruct(shape, BF16) for shape in shapes),
-        input_output_aliases={} if started is None else {len(operands) - 1: 0},
-        scratch_shapes=[
-            pltpu.VMEM((rows, width), BF16),
-            pltpu.VMEM((SLOTS,) + shapes[0][2:], BF16),
-            pltpu.SemaphoreType.DMA((SLOTS,)),
-        ],
-        compiler_params=pltpu.CompilerParams(vmem_limit_bytes=16 * MIB),
-        cost_estimate=pl.CostEstimate(
-            flops=int(share * 2 * rows * columns * width),
-            bytes_accessed=int(share * out_bytes) + 2 * rows * (columns + width),
-            transcendentals=0,
-        ),
+        input_output_aliases={} if started is None else {len(operands) - 1: len(shapes) - 1},
+        scratch_shapes=[pltpu.VMEM((rows, width), BF16)] * (2 if gate_up else 1)
+        + [pltpu.VMEM((SLOTS,) + (slot[::-1] if gate_up else (16, 128)), BF16)]
+        + [pltpu.VMEM((SLOTS,) + slot, BF16)]
+        + [pltpu.SemaphoreType.DMA((SLOTS,))],
+        compiler_params=pltpu.CompilerParams(vmem_limit_bytes=24 * MIB),
+        cost_estimate=pl.CostEstimate(flops=flops, bytes_accessed=flops // rows, transcendentals=0),
         name=name,
     )(*operands)
 
@@ -589,10 +599,7 @@
     x, cot, first, kept = split_heads(inputs, cotangent)
     heads, items = first_stage(first, kept)
     heads, items = other_stages(heads, items)
-    cots, distance = [cot], 2
-    while distance < size:
-        cots += [exchange(chunk, "dp", distance) for chunk in cots]
-        distance *= 2
+    cots = gather_chips(cot)
     norm_gain, heads[1] = after((norm_gain, heads[1]))
     gain, router_rows, chosen, down = small_operands(
         norm_gain, router_weight[0].T, route_ids[0].T, w_down
@@ -611,32 +618,30 @@
     )
     sent, act = after((sent, act))
     arrived = exchange(sent, "dp", 1)
-    (grad_down,) = weight_gradients(
-        functools.partial(down_kernel, range(1)), cots, act, (w_down.shape,), "grad_down_0", 1 / experts
-    )
+    (grad_down,) = weight_gradients(cots, act, w_down.shape, range(1), "grad_down_0")
     arrived, grad_down, grads = after((arrived, grad_down, grads))
     pairs = pair_sum(kept, arrived, small)
     pairs, grads = after((pairs, grads))
-    parts = [pairs[0]] + [exchange(pair, "dp", 2 * s) for s, pair in enumerate(pairs) if s]
-    grad_gate, grad_up = weight_gradients(
-        gate_up_kernel, rows, grads, (w_gate.shape, w_up.shape), "grad_gate_up"
+    far = [exchange(pairs[s], "dp", 2 * s) for s in reversed(range(1, size // 2))]
+    grad_gate, grad_up, grad_down = weight_gradients(
+        cots,
+        act,
+        w_down.shape,
+        range(1, DOWN_MIDDLE),
+        "grad_gate_up",
+        grad_down,
+        (rows, grads, (w_gate.shape, w_up.shape)),
     )
-    parts, grad_gate, grad_up = after((parts, grad_gate, grad_up))
-    grad_summed, small, *sends = norm_backward(parts, summed, gain, cot)
+    far, grad_gate, grad_up, grad_down = after((far, grad_gate, grad_up, grad_down))
+    grad_summed, small, *sends = norm_backward([pairs[0]] + far[::-1], summed, gain, cot)
     sends, act, small = after((sends, act, small))
     other = exchange(small, "dp", 1)
-    returned = [exchange(send, "tok", s + 1) for s, send in enumerate(sends)]
+    returned = [exchange(send, "tok", s + 1) for s, send in reversed(list(enumerate(sends)))]
     (grad_down,) = weight_gradients(
-        functools.partial(down_kernel, range(1, experts)),
-        cots,
-        act,
-        (w_down.shape,),
-        "grad_down",
-        1 - 1 / experts,
-        grad_down,
+        cots, act, w_down.shape, range(DOWN_MIDDLE, experts), "grad_down", grad_down
     )
     returned, grad_down, other = after((returned, grad_down, other))
-    places = tuple((s + 1, s, 0) for s in range(len(returned)))
+    places = tuple((len(returned) - s, s, 0) for s in range(len(returned)))
     grad_inputs, grad_router, grad_gain = finish(grad_summed, returned, places, small, other, experts)
     return (
         grad_inputs,

time: 62.2 us -> 59.4 us (0.955)
  waiting for transfers between devices: 5.01 us -> 3.5 us
  starting transfers between devices: 22.6 us -> 21.6 us
    ppermute x21, waiting for transfers between devices: 5.01 us -> 3.5 us  [exchange(): return lax.ppermute(value, axis, [(i, i ^ distance) for i in range(size)])]
    ppermute x21, starting transfers between devices: 22.6 us -> 21.6 us  [exchange(): return lax.ppermute(value, axis, [(i, i ^ distance) for i in range(size)])]
  transfers between devices with their start and end apart: 21 -> 21, of which waited for: 8 -> 6; matrix products, arithmetic and copies ran while one was open for 0% -> 0% of each run, Pallas kernels for 32% -> 33%
where the time goes in v2:
time: 59.4 us; the launch traced here: 59.1 us
  Pallas kernels  33.1 us (56%)
  starting transfers between devices  21.6 us (36%)
  waiting for transfers between devices  3.5 us (6%)
  between operations  0.82 us (1%)
    ppermute x21, starting transfers between devices, exchange(): return lax.ppermute(value, axis, [(i, i ^ distance) for i in range(size)])  21.6 us
    pallas_call x3, Pallas kernels, weight_gradients(): pl.pallas_call(functools.partial(weight_kernel, (len(normed_chunks), len(...  11.9 us
    pallas_call x1, Pallas kernels, experts_backward(): pl.pallas_call(functools.partial(expert_kernel, size), in_specs=[IN_VMEM]...  11.6 us
    pallas_call x1, Pallas kernels, back_hidden(): pl.pallas_call(functools.partial(back_kernel, len(chunks)), in_specs=[IN_...  5.04 us
    ppermute x21, waiting for transfers between devices, exchange(): return lax.ppermute(value, axis, [(i, i ^ distance) for i in range(size)])  3.5 us
    pallas_call x1, Pallas kernels, small_operands(): pl.pallas_call(small_kernel, in_specs=[IN_HBM] * 4, out_specs=(IN_VMEM,)...  2.26 us
  transfers between devices with their start and end apart: 21, of which 6 were waited for; matrix products, arithmetic and copies ran while one was open for 0% of the time, Pallas kernels for 33%

profile of v2, /device:TPU:0, one launch (start us, length us, event | category | flops | bytes accessed | tf_op | source)
XLA Modules:
  0.0 59.1 jit_solution(17165450331386842802)
XLA Ops:
  0.6 1.0 %split_heads.1 = (bf16[32,2048]{1,0:T(8,128)(2,1)S(1)}, bf16[32,2048]{1,0:T(8,128)(2,1)S(1)}, bf16[2,32,512]{2,1,0:T(8,128)(2,1)S(1)}, bf16[1,32,512]{2,1,0:T(8,128)(2,1)S(1)}) custom-call(bf16[1,32,2048]{2,1,0:T(8,128)(2,1)} %x_hbm.1, bf16[1,32,2048]{2,1,0:T(8,128)(2,1)} %cot_hbm.1), custom_call_target="tpu_custom_call" | custom-call | tf_op jit(solution)/shard_map/split_heads/pallas_call | solution.py:146
  1.6 3.1 %collective-permute-start = (bf16[2,32,512]{2,1,0:T(8,128)(2,1)S(1)}, bf16[2,32,512]{2,1,0:T(8,128)(2,1)S(1)}, u32[]{:S(2)}, u32[]{:S(2)}) collective-permute-start(bf16[2,32,512]{2,1,0:T(8,128)(2,1)S(1)} %get-tuple-element.87), channel_id=1, source_target_pairs={{0,1},{1,0},{2,3},{3,2},{4,5},{5,4},{6,7},{7,6},{8,9},{9,8},{10,11... | collective-permute-start | bytes 196616 | tf_op jit(solution)/shard_map/ppermute | solution.py:27
  4.7 2.4 %collective-permute-start.7 = (bf16[32,2048]{1,0:T(8,128)(2,1)S(1)}, bf16[32,2048]{1,0:T(8,128)(2,1)S(1)}, u32[]{:S(2)}, u32[]{:S(2)}) collective-permute-start(bf16[32,2048]{1,0:T(8,128)(2,1)S(1)} %get-tuple-element.101.refs_0_.refs_6_), channel_id=1, source_target_pairs={{0,24},{4,28},{8,16},{12,20},{16,8},{20,12},{24,0},{28,4},{1,25},{... | collective-permute-start | bytes 393224 | tf_op jit(solution)/shard_map/ppermute | solution.py:27
  7.7 0.5 collective-permute-start.5
  8.2 2.7 %collective-permute-start.1 = (bf16[2,32,512]{2,1,0:T(8,128)(2,1)S(1)}, bf16[2,32,512]{2,1,0:T(8,128)(2,1)S(1)}, u32[]{:S(2)}, u32[]{:S(2)}) collective-permute-start(bf16[2,32,512]{2,1,0:T(8,128)(2,1)S(1)} %pack_heads.1), channel_id=1, source_target_pairs={{0,2},{1,3},{2,0},{3,1},{4,6},{5,7},{6,4},{7,5},{8,10},{9,11},{10,... | collective-permute-start | bytes 196616 | tf_op jit(solution)/shard_map/ppermute | solution.py:27
  10.9 2.3 %small_operands.1 = (f32[1,2048]{1,0:T(1,128)S(1)}, bf16[4,2048]{1,0:T(4,128)(2,1)S(1)}, f32[256,8]{1,0:T(8,128)S(1)}, bf16[2,512,2048]{2,1,0:T(8,128)(2,1)S(1)}) custom-call(f32[1,2048]{1,0:T(1,128)} %gain_hbm, bf16[4,2048]{1,0:T(4,128)(2,1)} %bitcast.10, s32[2,256]{1,0:T(2,128)} %bitcast.11, bf16[1,4,512,2048]{3,2,1,0:T(8,128)(2,1)} %refs_3_.1), custom_call_target="tpu_custom_call" | custom-call | flops 68719476736 | bytes 33554432 | tf_op jit(solution)/shard_map/small_operands/pallas_call | solution.py:190
  13.1 1.0 %collective-permute-done.1.refs_2_ = bf16[2,32,512]{2,1,0:T(8,128)(2,1)S(1)} collective-permute-done((bf16[2,32,512]{2,1,0:T(8,128)(2,1)S(1)}, bf16[2,32,512]{2,1,0:T(8,128)(2,1)S(1)}, u32[]{:S(2)}, u32[]{:S(2)}) %collective-permute-start.1) | collective-permute-done | bytes 65568 | tf_op jit(solution)/shard_map/ppermute | solution.py:27
  14.5 2.5 %collective-permute-start.4 = (bf16[32,2048]{1,0:T(8,128)(2,1)S(1)}, bf16[32,2048]{1,0:T(8,128)(2,1)S(1)}, u32[]{:S(2)}, u32[]{:S(2)}) collective-permute-start(bf16[32,2048]{1,0:T(8,128)(2,1)S(1)} %get-tuple-element.98.refs_0_), channel_id=1, source_target_pairs={{0,24},{4,28},{8,16},{12,20},{16,8},{20,12},{24,0},{28,4},{1,25},{... | collective-permute-start | bytes 393224 | tf_op jit(solution)/shard_map/ppermute | solution.py:27
  17.0 0.5 collective-permute-start.3
  17.5 0.5 collective-permute-start.2
  18.0 5.0 %back_hidden.1 = (f32[4,256,512]{2,1,0:T(8,128)S(1)}, bf16[2048,2048]{1,0:T(8,128)(2,1)S(1)}) custom-call(bf16[128,2048]{1,0:T(8,128)(2,1)S(1)} %join_rows.1.refs_0_.refs_8_, bf16[128,2048]{1,0:T(8,128)(2,1)S(1)} %collective-permute-done.8.refs_1_.refs_9_, bf16[2,512,2048]{2,1,0:T(8,128)(2,1)S(1)} %get-tuple-element.105.refs_2_, ...), custom_call_target="tpu_custom_call" | custom-call | tf_op jit(solution)/shard_map/back_hidden/pallas_call | solution.py:284
  23.1 1.0 %collective-permute-done.3.refs_2_ = bf16[32,2048]{1,0:T(8,128)(2,1)S(1)} collective-permute-done((bf16[32,2048]{1,0:T(8,128)(2,1)S(1)}, bf16[32,2048]{1,0:T(8,128)(2,1)S(1)}, u32[]{:S(2)}, u32[]{:S(2)}) %collective-permute-start.3) | collective-permute-done | bytes 131104 | tf_op jit(solution)/shard_map/ppermute | solution.py:27
  24.2 0.5 collective-permute-start.11
  24.7 0.8 %collective-permute-done.10.refs_5_ = bf16[32,2048]{1,0:T(8,128)(2,1)S(1)} collective-permute-done((bf16[32,2048]{1,0:T(8,128)(2,1)S(1)}, bf16[32,2048]{1,0:T(8,128)(2,1)S(1)}, u32[]{:S(2)}, u32[]{:S(2)}) %collective-permute-start.10) | collective-permute-done | bytes 131104 | tf_op jit(solution)/shard_map/ppermute | solution.py:27
  26.0 11.6 %experts_backward.1 = (bf16[256,4096]{1,0:T(8,128)(2,1)S(1)}, bf16[256,2048]{1,0:T(8,128)(2,1)S(1)}, bf16[136,2048]{1,0:T(8,128)(2,1)S(1)}, bf16[32,2048]{1,0:T(...) custom-call(bf16[32,2048]{1,0:T(8,128)(2,1)S(1)} %get-tuple-element., ...), custom_call_target="tpu_custom_call" | custom-call | flops 8589934592 | bytes 24117248 | tf_op jit(solution)/shard_map/experts_backward/pallas_call | solution.py:384
  37.9 1.8 %grad_down_0.1.refs_12_ = bf16[1,4,512,2048]{3,2,1,0:T(8,128)(2,1)} custom-call(bf16[128,2048]{1,0:T(8,128)(2,1)S(1)} %join_rows.1.refs_0_.refs_8_, bf16[128,2048]{1,0:T(8,128)(2,1)S(1)} %collective-permute-done.8.refs_1_.refs_9_, bf16[256,2048]{1,0:T(8,128)(2,1)S(1)} %get-tuple-element.152.refs_2_.refs_11_), custom_call_target="tpu_custom_call" | custom-call | flops 536870912 | bytes 2097152 | tf_op jit(solution)/shard_map/grad_down_0/pallas_call | solution.py:505
  39.9 1.8 %collective-permute-start.14 = (bf16[40,2048]{1,0:T(8,128)(2,1)S(1)}, bf16[40,2048]{1,0:T(8,128)(2,1)S(1)}, u32[]{:S(2)}, u32[]{:S(2)}) collective-permute-start(bf16[40,2048]{1,0:T(8,128)(2,1)S(1)} %get-tuple-element.131), channel_id=1, source_target_pairs={{0,24},{4,28},{8,16},{12,20},{16,8},{20,12},{24,0},{28,4},{1,25},{... | collective-permute-start | bytes 491528 | tf_op jit(solution)/shard_map/ppermute | solution.py:27
  41.7 1.2 %collective-permute-start.15 = (bf16[40,2048]{1,0:T(8,128)(2,1)S(1)}, bf16[40,2048]{1,0:T(8,128)(2,1)S(1)}, u32[]{:S(2)}, u32[]{:S(2)}) collective-permute-start(bf16[40,2048]{1,0:T(8,128)(2,1)S(1)} %get-tuple-element.132), channel_id=1, source_target_pairs={{0,16},{4,20},{8,24},{12,28},{16,0},{20,4},{24,8},{28,12},{1,17},{... | collective-permute-start | bytes 491528 | tf_op jit(solution)/shard_map/ppermute | solution.py:27
  42.9 0.5 collective-permute-start.16
  43.5 7.3 %grad_gate_up.1 = (bf16[1,4,2048,512]{3,2,1,0:T(8,128)(2,1)}, bf16[1,4,2048,512]{3,2,1,0:T(8,128)(2,1)}, bf16[1,4,512,2048]{3,2,1,0:T(8,128)(2,1)}) custom-call(bf16[32,2048]{1,0:T(8,128)(2,1)S(1)} %get-tuple-element.98.refs_0_, bf16[32,2048]{1,0:T(8,128)(2,1)S(1)} %collective-permute-done.2.refs_1_, ...), custom_call_target="tpu_custom_call", output_to_operand_aliasing={{2}: (12, {})} | custom-call | flops 4831838208 | bytes 18874368 | tf_op jit(solution)/shard_map/grad_gate_up/pallas_call | solution.py:505
  51.1 2.1 %collective-permute-start.17 = (bf16[1,32,512]{2,1,0:T(8,128)(2,1)S(1)}, bf16[1,32,512]{2,1,0:T(8,128)(2,1)S(1)}, u32[]{:S(2)}, u32[]{:S(2)}) collective-permute-start(bf16[1,32,512]{2,1,0:T(8,128)(2,1)S(1)} %get-tuple-element.149), channel_id=1, source_target_pairs={{0,3},{1,2},{2,1},{3,0},{4,7},{5,6},{6,5},{7,4},{8,11},{9,10},{10,... | collective-permute-start | bytes 98312 | tf_op jit(solution)/shard_map/ppermute | solution.py:27
  53.2 2.4 %collective-permute-start.19 = (bf16[1,32,512]{2,1,0:T(8,128)(2,1)S(1)}, bf16[1,32,512]{2,1,0:T(8,128)(2,1)S(1)}, u32[]{:S(2)}, u32[]{:S(2)}) collective-permute-start(bf16[1,32,512]{2,1,0:T(8,128)(2,1)S(1)} %get-tuple-element.151), channel_id=1, source_target_pairs={{0,1},{1,0},{2,3},{3,2},{4,5},{5,4},{6,7},{7,6},{8,9},{9,8},{10,11... | collective-permute-start | bytes 98312 | tf_op jit(solution)/shard_map/ppermute | solution.py:27
  55.5 2.8 %grad_down.1 = bf16[1,4,512,2048]{3,2,1,0:T(8,128)(2,1)} custom-call(bf16[128,2048]{1,0:T(8,128)(2,1)S(1)} %join_rows.1.refs_0_.refs_8_, bf16[128,2048]{1,0:T(8,128)(2,1)S(1)} %collective-permute-done.8.refs_1_.refs_9_, bf16[256,2048]{1,0:T(8,128)(2,1)S(1)} %get-tuple-element.152.refs_2_.refs_11_, ...), custom_call_target="tpu_custom_call", output_to_operand_aliasing={{}: (3, {})} | custom-call | flops 1073741824 | bytes 4194304 | tf_op jit(solution)/shard_map/grad_down/pallas_call | solution.py:505
  58.4 0.7 %finish.1 = (bf16[1,32,2048]{2,1,0:T(8,128)(2,1)}, f32[4,2048]{1,0:T(4,128)}, f32[1,2048]{1,0:T(1,128)}) custom-call(f32[32,2048]{1,0:T(8,128)S(1)} %get-tuple-element.143.grad_ref, f32[8,1024]{1,0:T(8,128)S(1)} %get-tuple-element.148.small_ref, f32[8,1024]{1,0:T(8,128)S(1)} %collective-permute-done.20.other_ref, ...), custom_call_target="tpu_custom_call" | custom-call | tf_op jit(solution)/shard_map/finish/pallas_call | solution.py:582
  (31 shorter events, 2.1 us)
Async XLA Ops:
  1.6 6.6 %collective-permute-start = (bf16[2,32,512]{2,1,0:T(8,128)(2,1)S(1)}, bf16[2,32,512]{2,1,0:T(8,128)(2,1)S(1)}, u32[]{:S(2)}, u32[]{:S(2)}) collective-permute-start(bf16[2,32,512]{2,1,0:T(8,128)(2,1)S(1)} %get-tuple-element.87), channel_id=1, source_target_pairs={{0,1},{1,0},{2,3},{3,2},{4,5},{5,4},{6,7},{7,6},{8,9},{9,8},{10,11... | collective-permute-start | bytes 196616 | tf_op jit(solution)/shard_map/ppermute | solution.py:27
  4.7 9.6 %collective-permute-start.7 = (bf16[32,2048]{1,0:T(8,128)(2,1)S(1)}, bf16[32,2048]{1,0:T(8,128)(2,1)S(1)}, u32[]{:S(2)}, u32[]{:S(2)}) collective-permute-start(bf16[32,2048]{1,0:T(8,128)(2,1)S(1)} %get-tuple-element.101.refs_0_.refs_6_), channel_id=1, source_target_pairs={{0,24},{4,28},{8,16},{12,20},{16,8},{20,12},{24,0},{28,4},{1,25},{... | collective-permute-start | bytes 393224 | tf_op jit(solution)/shard_map/ppermute | solution.py:27
  7.2 7.2 %collective-permute-start.6 = (bf16[32,2048]{1,0:T(8,128)(2,1)S(1)}, bf16[32,2048]{1,0:T(8,128)(2,1)S(1)}, u32[]{:S(2)}, u32[]{:S(2)}) collective-permute-start(bf16[32,2048]{1,0:T(8,128)(2,1)S(1)} %get-tuple-element.101.refs_0_.refs_6_), channel_id=1, source_target_pairs={{0,16},{4,20},{8,24},{12,28},{16,0},{20,4},{24,8},{28,12},{1,17},{... | collective-permute-start | bytes 393224 | tf_op jit(solution)/shard_map/ppermute | solution.py:27
  7.7 6.7 %collective-permute-start.5 = (bf16[32,2048]{1,0:T(8,128)(2,1)S(1)}, bf16[32,2048]{1,0:T(8,128)(2,1)S(1)}, u32[]{:S(2)}, u32[]{:S(2)}) collective-permute-start(bf16[32,2048]{1,0:T(8,128)(2,1)S(1)} %get-tuple-element.101.refs_0_.refs_6_), channel_id=1, source_target_pairs={{0,8},{4,12},{8,0},{12,4},{16,24},{20,28},{24,16},{28,20},{1,9},{5... | collective-permute-start | bytes 393224 | tf_op jit(solution)/shard_map/ppermute | solution.py:27
  8.2 5.9 %collective-permute-start.1 = (bf16[2,32,512]{2,1,0:T(8,128)(2,1)S(1)}, bf16[2,32,512]{2,1,0:T(8,128)(2,1)S(1)}, u32[]{:S(2)}, u32[]{:S(2)}) collective-permute-start(bf16[2,32,512]{2,1,0:T(8,128)(2,1)S(1)} %pack_heads.1), channel_id=1, source_target_pairs={{0,2},{1,3},{2,0},{3,1},{4,6},{5,7},{6,4},{7,5},{8,10},{9,11},{10,... | collective-permute-start | bytes 196616 | tf_op jit(solution)/shard_map/ppermute | solution.py:27
  14.4 3.6 %collective-permute-start.8 = (bf16[128,2048]{1,0:T(8,128)(2,1)S(1)}, bf16[128,2048]{1,0:T(8,128)(2,1)S(1)}, u32[]{:S(2)}, u32[]{:S(2)}) collective-permute-start(bf16[128,2048]{1,0:T(8,128)(2,1)S(1)} %join_rows.1.refs_0_.refs_8_), channel_id=1, source_target_pairs={{0,4},{4,0},{8,12},{12,8},{16,20},{20,16},{24,28},{28,24},{1,5},{5... | collective-permute-start | bytes 1572872 | tf_op jit(solution)/shard_map/ppermute | solution.py:27
  14.5 8.6 %collective-permute-start.4 = (bf16[32,2048]{1,0:T(8,128)(2,1)S(1)}, bf16[32,2048]{1,0:T(8,128)(2,1)S(1)}, u32[]{:S(2)}, u32[]{:S(2)}) collective-permute-start(bf16[32,2048]{1,0:T(8,128)(2,1)S(1)} %get-tuple-element.98.refs_0_), channel_id=1, source_target_pairs={{0,24},{4,28},{8,16},{12,20},{16,8},{20,12},{24,0},{28,4},{1,25},{... | collective-permute-start | bytes 393224 | tf_op jit(solution)/shard_map/ppermute | solution.py:27
  17.0 7.1 %collective-permute-start.3 = (bf16[32,2048]{1,0:T(8,128)(2,1)S(1)}, bf16[32,2048]{1,0:T(8,128)(2,1)S(1)}, u32[]{:S(2)}, u32[]{:S(2)}) collective-permute-start(bf16[32,2048]{1,0:T(8,128)(2,1)S(1)} %get-tuple-element.98.refs_0_), channel_id=1, source_target_pairs={{0,16},{4,20},{8,24},{12,28},{16,0},{20,4},{24,8},{28,12},{1,17},{... | collective-permute-start | bytes 393224 | tf_op jit(solution)/shard_map/ppermute | solution.py:27
  17.5 6.7 %collective-permute-start.2 = (bf16[32,2048]{1,0:T(8,128)(2,1)S(1)}, bf16[32,2048]{1,0:T(8,128)(2,1)S(1)}, u32[]{:S(2)}, u32[]{:S(2)}) collective-permute-start(bf16[32,2048]{1,0:T(8,128)(2,1)S(1)} %get-tuple-element.98.refs_0_), channel_id=1, source_target_pairs={{0,8},{4,12},{8,0},{12,4},{16,24},{20,28},{24,16},{28,20},{1,9},{5... | collective-permute-start | bytes 393224 | tf_op jit(solution)/shard_map/ppermute | solution.py:27
  18.0 6.7 %collective-permute-start.9 = (bf16[32,2048]{1,0:T(8,128)(2,1)S(1)}, bf16[32,2048]{1,0:T(8,128)(2,1)S(1)}, u32[]{:S(2)}, u32[]{:S(2)}) collective-permute-start(bf16[32,2048]{1,0:T(8,128)(2,1)S(1)} %get-tuple-element.98.refs_0_), channel_id=1, source_target_pairs={{0,4},{4,0},{8,12},{12,8},{16,20},{20,16},{24,28},{28,24},{1,5},{5... | collective-permute-start | bytes 393224 | tf_op jit(solution)/shard_map/ppermute | solution.py:27
  24.2 1.3 %collective-permute-start.10 = (bf16[32,2048]{1,0:T(8,128)(2,1)S(1)}, bf16[32,2048]{1,0:T(8,128)(2,1)S(1)}, u32[]{:S(2)}, u32[]{:S(2)}) collective-permute-start(bf16[32,2048]{1,0:T(8,128)(2,1)S(1)} %collective-permute-done.2.refs_1_), channel_id=1, source_target_pairs={{0,4},{4,0},{8,12},{12,8},{16,20},{20,16},{24,28},{28,24},{1,5},{5... | collective-permute-start | bytes 393224 | tf_op jit(solution)/shard_map/ppermute | solution.py:27
  24.2 1.5 %collective-permute-start.11 = (bf16[32,2048]{1,0:T(8,128)(2,1)S(1)}, bf16[32,2048]{1,0:T(8,128)(2,1)S(1)}, u32[]{:S(2)}, u32[]{:S(2)}) collective-permute-start(bf16[32,2048]{1,0:T(8,128)(2,1)S(1)} %collective-permute-done.3.refs_2_), channel_id=1, source_target_pairs={{0,4},{4,0},{8,12},{12,8},{16,20},{20,16},{24,28},{28,24},{1,5},{5... | collective-permute-start | bytes 393224 | tf_op jit(solution)/shard_map/ppermute | solution.py:27
  24.7 1.3 %collective-permute-start.12 = (bf16[32,2048]{1,0:T(8,128)(2,1)S(1)}, bf16[32,2048]{1,0:T(8,128)(2,1)S(1)}, u32[]{:S(2)}, u32[]{:S(2)}) collective-permute-start(bf16[32,2048]{1,0:T(8,128)(2,1)S(1)} %collective-permute-done.4.refs_3_), channel_id=1, source_target_pairs={{0,4},{4,0},{8,12},{12,8},{16,20},{20,16},{24,28},{28,24},{1,5},{5... | collective-permute-start | bytes 393224 | tf_op jit(solution)/shard_map/ppermute | solution.py:27
  37.7 2.1 %collective-permute-start.13 = (bf16[136,2048]{1,0:T(8,128)(2,1)S(1)}, bf16[136,2048]{1,0:T(8,128)(2,1)S(1)}, u32[]{:S(2)}, u32[]{:S(2)}) collective-permute-start(bf16[136,2048]{1,0:T(8,128)(2,1)S(1)} %get-tuple-element.120), channel_id=1, source_target_pairs={{0,4},{4,0},{8,12},{12,8},{16,20},{20,16},{24,28},{28,24},{1,5},{5... | collective-permute-start | bytes 1671176 | tf_op jit(solution)/shard_map/ppermute | solution.py:27
  39.9 10.9 %collective-permute-start.14 = (bf16[40,2048]{1,0:T(8,128)(2,1)S(1)}, bf16[40,2048]{1,0:T(8,128)(2,1)S(1)}, u32[]{:S(2)}, u32[]{:S(2)}) collective-permute-start(bf16[40,2048]{1,0:T(8,128)(2,1)S(1)} %get-tuple-element.131), channel_id=1, source_target_pairs={{0,24},{4,28},{8,16},{12,20},{16,8},{20,12},{24,0},{28,4},{1,25},{... | collective-permute-start | bytes 491528 | tf_op jit(solution)/shard_map/ppermute | solution.py:27
  41.7 9.1 %collective-permute-start.15 = (bf16[40,2048]{1,0:T(8,128)(2,1)S(1)}, bf16[40,2048]{1,0:T(8,128)(2,1)S(1)}, u32[]{:S(2)}, u32[]{:S(2)}) collective-permute-start(bf16[40,2048]{1,0:T(8,128)(2,1)S(1)} %get-tuple-element.132), channel_id=1, source_target_pairs={{0,16},{4,20},{8,24},{12,28},{16,0},{20,4},{24,8},{28,12},{1,17},{... | collective-permute-start | bytes 491528 | tf_op jit(solution)/shard_map/ppermute | solution.py:27
  42.9 7.9 %collective-permute-start.16 = (bf16[40,2048]{1,0:T(8,128)(2,1)S(1)}, bf16[40,2048]{1,0:T(8,128)(2,1)S(1)}, u32[]{:S(2)}, u32[]{:S(2)}) collective-permute-start(bf16[40,2048]{1,0:T(8,128)(2,1)S(1)} %get-tuple-element.133), channel_id=1, source_target_pairs={{0,8},{4,12},{8,0},{12,4},{16,24},{20,28},{24,16},{28,20},{1,9},{5... | collective-permute-start | bytes 491528 | tf_op jit(solution)/shard_map/ppermute | solution.py:27
  51.1 7.3 %collective-permute-start.17 = (bf16[1,32,512]{2,1,0:T(8,128)(2,1)S(1)}, bf16[1,32,512]{2,1,0:T(8,128)(2,1)S(1)}, u32[]{:S(2)}, u32[]{:S(2)}) collective-permute-start(bf16[1,32,512]{2,1,0:T(8,128)(2,1)S(1)} %get-tuple-element.149), channel_id=1, source_target_pairs={{0,3},{1,2},{2,1},{3,0},{4,7},{5,6},{6,5},{7,4},{8,11},{9,10},{10,... | collective-permute-start | bytes 98312 | tf_op jit(solution)/shard_map/ppermute | solution.py:27
  53.2 5.2 %collective-permute-start.18 = (bf16[1,32,512]{2,1,0:T(8,128)(2,1)S(1)}, bf16[1,32,512]{2,1,0:T(8,128)(2,1)S(1)}, u32[]{:S(2)}, u32[]{:S(2)}) collective-permute-start(bf16[1,32,512]{2,1,0:T(8,128)(2,1)S(1)} %get-tuple-element.150), channel_id=1, source_target_pairs={{0,2},{1,3},{2,0},{3,1},{4,6},{5,7},{6,4},{7,5},{8,10},{9,11},{10,... | collective-permute-start | bytes 98312 | tf_op jit(solution)/shard_map/ppermute | solution.py:27
  53.2 5.2 %collective-permute-start.19 = (bf16[1,32,512]{2,1,0:T(8,128)(2,1)S(1)}, bf16[1,32,512]{2,1,0:T(8,128)(2,1)S(1)}, u32[]{:S(2)}, u32[]{:S(2)}) collective-permute-start(bf16[1,32,512]{2,1,0:T(8,128)(2,1)S(1)} %get-tuple-element.151), channel_id=1, source_target_pairs={{0,1},{1,0},{2,3},{3,2},{4,5},{5,4},{6,7},{7,6},{8,9},{9,8},{10,11... | collective-permute-start | bytes 98312 | tf_op jit(solution)/shard_map/ppermute | solution.py:27
  55.5 2.8 %collective-permute-start.20 = (f32[8,1024]{1,0:T(8,128)S(1)}, f32[8,1024]{1,0:T(8,128)S(1)}, u32[]{:S(2)}, u32[]{:S(2)}) collective-permute-start(f32[8,1024]{1,0:T(8,128)S(1)} %get-tuple-element.148.small_ref), channel_id=1, source_target_pairs={{0,4},{4,0},{8,12},{12,8},{16,20},{20,16},{24,28},{28,24},{1,5},{5... | collective-permute-start | bytes 98312 | tf_op jit(solution)/shard_map/ppermute | solution.py:27

commit v3 on v2

--- a/solution.py
+++ b/solution.py
@@ -195,7 +195,7 @@
             jax.ShapeDtypeStruct(gain.shape, F32),
             jax.ShapeDtypeStruct(router_rows.shape, BF16),
             jax.ShapeDtypeStruct((all_rows, experts), F32),
-            jax.ShapeDtypeStruct((w_down.shape[1] // 2,) + w_down.shape[2:], BF16),
+            jax.ShapeDtypeStruct((w_down.shape[1] - 1,) + w_down.shape[2:], BF16),
         ),
         scratch_shapes=[
             pltpu.VMEM(routes.shape, jnp.int32),
@@ -245,19 +245,38 @@
     )(*chunks)
 
 
-def load_weights(refs, place, experts, sems):
+def load_weights(refs, place, experts, sems, start=0):
     copies = []
     for i, (e, ref) in enumerate((e, ref) for e in experts for ref in refs):
         hidden = ref.shape[3]
-        columns = pl.ds(i * hidden, hidden)
+        columns = pl.ds((2 * start + i) * hidden, hidden)
         copies.append(pltpu.make_async_copy(ref.at[0, e], place.at[:, columns], sems.at[i]))
         copies[-1].start()
     return copies
 
 
+def load_kernel(gate_hbm, up_hbm, weights_ref, sems):
+    for load in load_weights((gate_hbm, up_hbm), weights_ref, range(1), sems):
+        load.wait()
+
+
+def load_first(w_gate, w_up):
+    _, experts, width, hidden = w_gate.shape
+    return pl.pallas_call(
+        load_kernel,
+        in_specs=[IN_HBM] * 2,
+        out_specs=ANYWHERE,
+        out_shape=jax.ShapeDtypeStruct((width, experts // 2 * 2 * hidden), BF16),
+        scratch_shapes=[pltpu.SemaphoreType.DMA((2,))],
+        compiler_params=pltpu.CompilerParams(vmem_limit_bytes=1 * MIB),
+        cost_estimate=pl.CostEstimate(flops=2**36, bytes_accessed=4 * width * hidden, transcendentals=0),
+        name="load_first",
+    )(hbm(w_gate), hbm(w_up))
+
+
 def back_kernel(count, *refs):
-    chunks, (first, down_hbm, gate_hbm, up_hbm, back_ref, weights_ref) = refs[:count], refs[count : count + 6]
-    cot, second, down_sems, sems = refs[count + 6 :]
+    chunks, (first, down_hbm, gate_hbm, up_hbm, _, back_ref, weights_ref) = refs[:count], refs[count : count + 7]
+    cot, second, down_sems, sems = refs[count + 7 :]
     split = first.shape[0]
     experts = split + second.shape[0]
     copies = [
@@ -266,7 +285,7 @@
     ]
     for copy in copies:
         copy.start()
-    loads = load_weights((gate_hbm, up_hbm), weights_ref, range(experts // 2), sems)
+    loads = load_weights((gate_hbm, up_hbm), weights_ref, range(1, experts // 2), sems, 1)
     assemble(cot, chunks)
     for e in range(split):
         back_ref[e] = dot(cot[...], first[e], NT)
@@ -277,13 +296,14 @@
         load.wait()
 
 
-def back_hidden(chunks, first, w_down, w_gate, w_up):
+def back_hidden(chunks, first, w_down, w_gate, w_up, weights):
     _, experts, hidden, width = w_down.shape
     rows = sum(chunk.shape[0] for chunk in chunks)
     rest = experts - first.shape[0]
     return pl.pallas_call(
         functools.partial(back_kernel, len(chunks)),
-        in_specs=[IN_VMEM] * (len(chunks) + 1) + [IN_HBM] * 3,
+        in_specs=[IN_VMEM] * (len(chunks) + 1) + [IN_HBM] * 3 + [ANYWHERE],
+        input_output_aliases={len(chunks) + 4: 1},
         out_specs=(IN_VMEM, ANYWHERE),
         out_shape=(
             jax.ShapeDtypeStruct((experts, rows, hidden), F32),
@@ -293,7 +313,7 @@
             pltpu.VMEM((rows, width), BF16),
             pltpu.VMEM((rest, hidden, width), BF16),
             pltpu.SemaphoreType.DMA((rest,)),
-            pltpu.SemaphoreType.DMA((experts // 2 * 2,)),
+            pltpu.SemaphoreType.DMA(((experts // 2 - 1) * 2,)),
         ],
         compiler_params=pltpu.CompilerParams(vmem_limit_bytes=16 * MIB),
         cost_estimate=pl.CostEstimate(
@@ -302,13 +322,13 @@
             transcendentals=0,
         ),
         name="back_hidden",
-    )(*chunks, vmem(first), hbm(w_down), hbm(w_gate), hbm(w_up))
+    )(*chunks, vmem(first), hbm(w_down), hbm(w_gate), hbm(w_up), weights)
 
 
 def expert_kernel(size, *refs):
     chunks, (first, gate_hbm, up_hbm, back_ref) = refs[:size], refs[size : size + 4]
     chosen_ref, router_ref, gain_ref, grads_out, act_out, sent_out = refs[size + 4 : size + 10]
-    kept, (small_out, normed, second, sems) = refs[size + 10 : -4], refs[-4:]
+    kept, (small_out, normed, total, second, sems) = refs[size + 10 : -5], refs[-5:]
     own, width = chunks[0].shape
     experts = router_ref.shape[0]
     hidden = back_ref.shape[2]
@@ -349,6 +369,8 @@
         grads_out[:, 2 * e * hidden : (2 * e + 1) * hidden] = grad_gate.astype(BF16)
         grads_out[:, (2 * e + 1) * hidden : (2 * e + 2) * hidden] = (scaled * silu).astype(BF16)
         act_out[:, e * hidden : (e + 1) * hidden] = (gate * act).astype(BF16)
+        if e == experts - 2:
+            total[...] = dot(grads_out[:, : 2 * split * hidden], first[...], NT)
     coef = jnp.concatenate(shares, axis=1) * gates * (1.0 - prob)
     high = coef.astype(BF16).astype(F32)
     middle = (coef - high).astype(BF16).astype(F32)
@@ -362,8 +384,7 @@
     step = width // 4
     for c in range(0, width, step):
         here = slice(c, c + step)
-        grad = dot(grads_out[:, : 2 * split * hidden], first[here, :], NT)
-        grad = grad + dot(grads_out[:, 2 * split * hidden :], second[here, :], NT)
+        grad = total[:, here] + dot(grads_out[:, 2 * split * hidden :], second[here, :], NT)
         grad = grad + dot(terms, router[:, here], NN)
         rows_here = normed[:, here].astype(F32)
         gain = jnp.sum(grad * rows_here, axis=0, keepdims=True) / gain_ref[:, here]
@@ -393,6 +414,7 @@
         + (jax.ShapeDtypeStruct((8, width), F32),),
         scratch_shapes=[
             pltpu.VMEM((rows, width), BF16),
+            pltpu.VMEM((rows, width), F32),
             pltpu.VMEM((width, 2 * (experts - experts // 2) * hidden), BF16),
             pltpu.SemaphoreType.DMA((2 * (experts - experts // 2),)),
         ],
@@ -608,11 +630,16 @@
     places = from_tokens(heads, items)
     normed, summed = norm_rows(x, gain, heads, places)
     far_rows = gather_chips(normed)
-    cots, summed = after((cots, summed))
-    cots = gather_cores([join_rows(cots)])
-    back, weights = back_hidden(cots, down, w_down, w_gate, w_up)
+    own_other = exchange(far_rows[0], "dp", 1)
+    cots, own_other = after((cots, own_other))
+    mine = join_rows(cots)
+    w_gate_first, mine = after((w_gate, mine))
+    weights = load_first(w_gate_first, w_up)
+    other_cots, weights = after((exchange(mine, "dp", 1), weights))
+    cots = [mine, other_cots]
+    back, weights = back_hidden(cots, down, w_down, w_gate, w_up, weights)
     far_rows[1:], back = after((far_rows[1:], back))
-    rows = gather_cores(far_rows)
+    rows = far_rows + [own_other] + [exchange(chunk, "dp", 1) for chunk in far_rows[1:]]
     grads, act, sent, *kept, small = experts_backward(
         rows, weights, w_gate, w_up, back, chosen, router_rows, gain
     )

time: 59.4 us -> 58.9 us (level)
  waiting for transfers between devices: 3.5 us -> 2.53 us
    pallas_call x0 -> x1, Pallas kernels: none -> 2.24 us  [load_first(): pl.pallas_call(load_kernel, in_specs=[IN_HBM] * 2, out_specs=ANYWHERE, ou...]
    pallas_call x1, Pallas kernels: 5.04 us -> 3.04 us  [back_hidden(): pl.pallas_call(functools.partial(back_kernel, len(chunks)), in_specs=[IN_...]
    ppermute x21, waiting for transfers between devices: 3.5 us -> 2.53 us  [exchange(): return lax.ppermute(value, axis, [(i, i ^ distance) for i in range(size)])]
    pallas_call x1, Pallas kernels: 2.26 us -> 2.85 us  [small_operands(): pl.pallas_call(small_kernel, in_specs=[IN_HBM] * 4, out_specs=(IN_VMEM,)...]
  transfers between devices with their start and end apart: 21 -> 21, of which waited for: 6 -> 6; matrix products, arithmetic and copies ran while one was open for 0% -> 0% of each run, Pallas kernels for 33% -> 35%
where the time goes in v3:
time: 58.9 us; the launch traced here: 58.7 us
  Pallas kernels  33.6 us (57%)
  starting transfers between devices  21.7 us (37%)
  waiting for transfers between devices  2.53 us (4%)
  between operations  0.81 us (1%)
    ppermute x21, starting transfers between devices, exchange(): return lax.ppermute(value, axis, [(i, i ^ distance) for i in range(size)])  21.7 us
    pallas_call x3, Pallas kernels, weight_gradients(): pl.pallas_call(functools.partial(weight_kernel, (len(normed_chunks), len(...  11.9 us
    pallas_call x1, Pallas kernels, experts_backward(): pl.pallas_call(functools.partial(expert_kernel, size), in_specs=[IN_VMEM]...  11.3 us
    pallas_call x1, Pallas kernels, back_hidden(): pl.pallas_call(functools.partial(back_kernel, len(chunks)), in_specs=[IN_...  3.04 us
    pallas_call x1, Pallas kernels, small_operands(): pl.pallas_call(small_kernel, in_specs=[IN_HBM] * 4, out_specs=(IN_VMEM,)...  2.85 us
    ppermute x21, waiting for transfers between devices, exchange(): return lax.ppermute(value, axis, [(i, i ^ distance) for i in range(size)])  2.53 us
    pallas_call x1, Pallas kernels, load_first(): pl.pallas_call(load_kernel, in_specs=[IN_HBM] * 2, out_specs=ANYWHERE, ou...  2.24 us
  transfers between devices with their start and end apart: 21, of which 6 were waited for; matrix products, arithmetic and copies ran while one was open for 0% of the time, Pallas kernels for 35%

profile of v3, /device:TPU:0, one launch (start us, length us, event | category | flops | bytes accessed | tf_op | source)
XLA Modules:
  0.0 58.7 jit_solution(10086234886757268460)
XLA Ops:
  0.6 1.0 %split_heads.1 = (bf16[32,2048]{1,0:T(8,128)(2,1)S(1)}, bf16[32,2048]{1,0:T(8,128)(2,1)S(1)}, bf16[2,32,512]{2,1,0:T(8,128)(2,1)S(1)}, bf16[1,32,512]{2,1,0:T(8,128)(2,1)S(1)}) custom-call(bf16[1,32,2048]{2,1,0:T(8,128)(2,1)} %x_hbm.1, bf16[1,32,2048]{2,1,0:T(8,128)(2,1)} %cot_hbm.1), custom_call_target="tpu_custom_call" | custom-call | tf_op jit(solution)/shard_map/split_heads/pallas_call | solution.py:146
  1.6 3.1 %collective-permute-start = (bf16[2,32,512]{2,1,0:T(8,128)(2,1)S(1)}, bf16[2,32,512]{2,1,0:T(8,128)(2,1)S(1)}, u32[]{:S(2)}, u32[]{:S(2)}) collective-permute-start(bf16[2,32,512]{2,1,0:T(8,128)(2,1)S(1)} %get-tuple-element.91), channel_id=1, source_target_pairs={{0,1},{1,0},{2,3},{3,2},{4,5},{5,4},{6,7},{7,6},{8,9},{9,8},{10,11... | collective-permute-start | bytes 196616 | tf_op jit(solution)/shard_map/ppermute | solution.py:27
  4.7 2.4 %collective-permute-start.7 = (bf16[32,2048]{1,0:T(8,128)(2,1)S(1)}, bf16[32,2048]{1,0:T(8,128)(2,1)S(1)}, u32[]{:S(2)}, u32[]{:S(2)}) collective-permute-start(bf16[32,2048]{1,0:T(8,128)(2,1)S(1)} %get-tuple-element.104.refs_0_.refs_6_), channel_id=1, source_target_pairs={{0,24},{4,28},{8,16},{12,20},{16,8},{20,12},{24,0},{28,4},{1,25},{... | collective-permute-start | bytes 393224 | tf_op jit(solution)/shard_map/ppermute | solution.py:27
  7.7 0.5 collective-permute-start.5
  8.2 2.7 %collective-permute-start.1 = (bf16[2,32,512]{2,1,0:T(8,128)(2,1)S(1)}, bf16[2,32,512]{2,1,0:T(8,128)(2,1)S(1)}, u32[]{:S(2)}, u32[]{:S(2)}) collective-permute-start(bf16[2,32,512]{2,1,0:T(8,128)(2,1)S(1)} %pack_heads.1), channel_id=1, source_target_pairs={{0,2},{1,3},{2,0},{3,1},{4,6},{5,7},{6,4},{7,5},{8,10},{9,11},{10,... | collective-permute-start | bytes 196616 | tf_op jit(solution)/shard_map/ppermute | solution.py:27
  10.9 2.9 %small_operands.1 = (f32[1,2048]{1,0:T(1,128)S(1)}, bf16[4,2048]{1,0:T(4,128)(2,1)S(1)}, f32[256,8]{1,0:T(8,128)S(1)}, bf16[3,512,2048]{2,1,0:T(8,128)(2,1)S(1)}) custom-call(f32[1,2048]{1,0:T(1,128)} %gain_hbm, bf16[4,2048]{1,0:T(4,128)(2,1)} %bitcast.10, s32[2,256]{1,0:T(2,128)} %bitcast.11, bf16[1,4,512,2048]{3,2,1,0:T(8,128)(2,1)} %refs_3_.1), custom_call_target="tpu_custom_call" | custom-call | flops 68719476736 | bytes 33554432 | tf_op jit(solution)/shard_map/small_operands/pallas_call | solution.py:190
  14.4 2.5 %collective-permute-start.4 = (bf16[32,2048]{1,0:T(8,128)(2,1)S(1)}, bf16[32,2048]{1,0:T(8,128)(2,1)S(1)}, u32[]{:S(2)}, u32[]{:S(2)}) collective-permute-start(bf16[32,2048]{1,0:T(8,128)(2,1)S(1)} %get-tuple-element.102.refs_0_), channel_id=1, source_target_pairs={{0,24},{4,28},{8,16},{12,20},{16,8},{20,12},{24,0},{28,4},{1,25},{... | collective-permute-start | bytes 393224 | tf_op jit(solution)/shard_map/ppermute | solution.py:27
  16.9 0.5 collective-permute-start.3
  17.4 0.5 collective-permute-start.2
  18.1 2.2 %load_first.1.refs_6_ = bf16[2048,2048]{1,0:T(8,128)(2,1)S(1)} custom-call(bf16[1,4,2048,512]{3,2,1,0:T(8,128)(2,1)} %refs_9_.1, bf16[1,4,2048,512]{3,2,1,0:T(8,128)(2,1)} %refs_10_.1), custom_call_target="tpu_custom_call" | custom-call | flops 68719476736 | bytes 4194304 | tf_op jit(solution)/shard_map/load_first/pallas_call | solution.py:265
  20.3 3.0 %back_hidden.1 = (f32[4,256,512]{2,1,0:T(8,128)S(1)}, bf16[2048,2048]{1,0:T(8,128)(2,1)S(1)}) custom-call(bf16[128,2048]{1,0:T(8,128)(2,1)S(1)} %join_rows.1.refs_0_.refs_8_, bf16[128,2048]{1,0:T(8,128)(2,1)S(1)} %collective-permute-done.9.refs_1_.refs_9_, bf16[3,512,2048]{2,1,0:T(8,128)(2,1)S(1)} %get-tuple-element.111.refs_2_, ...), custom_call_target="tpu_custom_call", output_to_operand_aliasing={{1}: (6, {})} | custom-call | tf_op jit(solution)/shard_map/back_hidden/pallas_call | solution.py:303
  23.4 0.6 %collective-permute-done.3.refs_2_ = bf16[32,2048]{1,0:T(8,128)(2,1)S(1)} collective-permute-done((bf16[32,2048]{1,0:T(8,128)(2,1)S(1)}, bf16[32,2048]{1,0:T(8,128)(2,1)S(1)}, u32[]{:S(2)}, u32[]{:S(2)}) %collective-permute-start.3) | collective-permute-done | bytes 131104 | tf_op jit(solution)/shard_map/ppermute | solution.py:27
  24.1 0.5 collective-permute-start.11
  24.6 0.8 %collective-permute-done.10.refs_5_ = bf16[32,2048]{1,0:T(8,128)(2,1)S(1)} collective-permute-done((bf16[32,2048]{1,0:T(8,128)(2,1)S(1)}, bf16[32,2048]{1,0:T(8,128)(2,1)S(1)}, u32[]{:S(2)}, u32[]{:S(2)}) %collective-permute-start.10) | collective-permute-done | bytes 131104 | tf_op jit(solution)/shard_map/ppermute | solution.py:27
  26.0 11.3 %experts_backward.1 = (bf16[256,4096]{1,0:T(8,128)(2,1)S(1)}, bf16[256,2048]{1,0:T(8,128)(2,1)S(1)}, bf16[136,2048]{1,0:T(8,128)(2,1)S(1)}, bf16[32,2048]{1,0:T(...) custom-call(bf16[32,2048]{1,0:T(8,128)(2,1)S(1)} %get-tuple-element., ...), custom_call_target="tpu_custom_call" | custom-call | flops 8589934592 | bytes 24117248 | tf_op jit(solution)/shard_map/experts_backward/pallas_call | solution.py:405
  37.5 1.8 %grad_down_0.1.refs_12_ = bf16[1,4,512,2048]{3,2,1,0:T(8,128)(2,1)} custom-call(bf16[128,2048]{1,0:T(8,128)(2,1)S(1)} %join_rows.1.refs_0_.refs_8_, bf16[128,2048]{1,0:T(8,128)(2,1)S(1)} %collective-permute-done.9.refs_1_.refs_9_, bf16[256,2048]{1,0:T(8,128)(2,1)S(1)} %get-tuple-element.160.refs_2_.refs_11_), custom_call_target="tpu_custom_call" | custom-call | flops 536870912 | bytes 2097152 | tf_op jit(solution)/shard_map/grad_down_0/pallas_call | solution.py:527
  39.5 2.2 %collective-permute-start.14 = (bf16[40,2048]{1,0:T(8,128)(2,1)S(1)}, bf16[40,2048]{1,0:T(8,128)(2,1)S(1)}, u32[]{:S(2)}, u32[]{:S(2)}) collective-permute-start(bf16[40,2048]{1,0:T(8,128)(2,1)S(1)} %get-tuple-element.139), channel_id=1, source_target_pairs={{0,24},{4,28},{8,16},{12,20},{16,8},{20,12},{24,0},{28,4},{1,25},{... | collective-permute-start | bytes 491528 | tf_op jit(solution)/shard_map/ppermute | solution.py:27
  41.7 0.8 %collective-permute-start.15 = (bf16[40,2048]{1,0:T(8,128)(2,1)S(1)}, bf16[40,2048]{1,0:T(8,128)(2,1)S(1)}, u32[]{:S(2)}, u32[]{:S(2)}) collective-permute-start(bf16[40,2048]{1,0:T(8,128)(2,1)S(1)} %get-tuple-element.140), channel_id=1, source_target_pairs={{0,16},{4,20},{8,24},{12,28},{16,0},{20,4},{24,8},{28,12},{1,17},{... | collective-permute-start | bytes 491528 | tf_op jit(solution)/shard_map/ppermute | solution.py:27
  42.5 0.5 collective-permute-start.16
  43.0 7.3 %grad_gate_up.1 = (bf16[1,4,2048,512]{3,2,1,0:T(8,128)(2,1)}, bf16[1,4,2048,512]{3,2,1,0:T(8,128)(2,1)}, bf16[1,4,512,2048]{3,2,1,0:T(8,128)(2,1)}) custom-call(bf16[32,2048]{1,0:T(8,128)(2,1)S(1)} %get-tuple-element.102.refs_0_, bf16[32,2048]{1,0:T(8,128)(2,1)S(1)} %collective-permute-done.2.refs_1_, ...), custom_call_target="tpu_custom_call", output_to_operand_aliasing={{2}: (12, {})} | custom-call | flops 4831838208 | bytes 18874368 | tf_op jit(solution)/shard_map/grad_gate_up/pallas_call | solution.py:527
  50.7 2.1 %collective-permute-start.17 = (bf16[1,32,512]{2,1,0:T(8,128)(2,1)S(1)}, bf16[1,32,512]{2,1,0:T(8,128)(2,1)S(1)}, u32[]{:S(2)}, u32[]{:S(2)}) collective-permute-start(bf16[1,32,512]{2,1,0:T(8,128)(2,1)S(1)} %get-tuple-element.157), channel_id=1, source_target_pairs={{0,3},{1,2},{2,1},{3,0},{4,7},{5,6},{6,5},{7,4},{8,11},{9,10},{10,... | collective-permute-start | bytes 98312 | tf_op jit(solution)/shard_map/ppermute | solution.py:27
  52.8 2.3 %collective-permute-start.19 = (bf16[1,32,512]{2,1,0:T(8,128)(2,1)S(1)}, bf16[1,32,512]{2,1,0:T(8,128)(2,1)S(1)}, u32[]{:S(2)}, u32[]{:S(2)}) collective-permute-start(bf16[1,32,512]{2,1,0:T(8,128)(2,1)S(1)} %get-tuple-element.159), channel_id=1, source_target_pairs={{0,1},{1,0},{2,3},{3,2},{4,5},{5,4},{6,7},{7,6},{8,9},{9,8},{10,11... | collective-permute-start | bytes 98312 | tf_op jit(solution)/shard_map/ppermute | solution.py:27
  55.1 2.8 %grad_down.1 = bf16[1,4,512,2048]{3,2,1,0:T(8,128)(2,1)} custom-call(bf16[128,2048]{1,0:T(8,128)(2,1)S(1)} %join_rows.1.refs_0_.refs_8_, bf16[128,2048]{1,0:T(8,128)(2,1)S(1)} %collective-permute-done.9.refs_1_.refs_9_, bf16[256,2048]{1,0:T(8,128)(2,1)S(1)} %get-tuple-element.160.refs_2_.refs_11_, ...), custom_call_target="tpu_custom_call", output_to_operand_aliasing={{}: (3, {})} | custom-call | flops 1073741824 | bytes 4194304 | tf_op jit(solution)/shard_map/grad_down/pallas_call | solution.py:527
  57.9 0.7 %finish.1 = (bf16[1,32,2048]{2,1,0:T(8,128)(2,1)}, f32[4,2048]{1,0:T(4,128)}, f32[1,2048]{1,0:T(1,128)}) custom-call(f32[32,2048]{1,0:T(8,128)S(1)} %get-tuple-element.151.grad_ref, f32[8,1024]{1,0:T(8,128)S(1)} %get-tuple-element.156.small_ref, f32[8,1024]{1,0:T(8,128)S(1)} %collective-permute-done.20.other_ref, ...), custom_call_target="tpu_custom_call" | custom-call | tf_op jit(solution)/shard_map/finish/pallas_call | solution.py:604
  (32 shorter events, 2.5 us)
Async XLA Ops:
  1.6 6.6 %collective-permute-start = (bf16[2,32,512]{2,1,0:T(8,128)(2,1)S(1)}, bf16[2,32,512]{2,1,0:T(8,128)(2,1)S(1)}, u32[]{:S(2)}, u32[]{:S(2)}) collective-permute-start(bf16[2,32,512]{2,1,0:T(8,128)(2,1)S(1)} %get-tuple-element.91), channel_id=1, source_target_pairs={{0,1},{1,0},{2,3},{3,2},{4,5},{5,4},{6,7},{7,6},{8,9},{9,8},{10,11... | collective-permute-start | bytes 196616 | tf_op jit(solution)/shard_map/ppermute | solution.py:27
  4.7 12.2 %collective-permute-start.7 = (bf16[32,2048]{1,0:T(8,128)(2,1)S(1)}, bf16[32,2048]{1,0:T(8,128)(2,1)S(1)}, u32[]{:S(2)}, u32[]{:S(2)}) collective-permute-start(bf16[32,2048]{1,0:T(8,128)(2,1)S(1)} %get-tuple-element.104.refs_0_.refs_6_), channel_id=1, source_target_pairs={{0,24},{4,28},{8,16},{12,20},{16,8},{20,12},{24,0},{28,4},{1,25},{... | collective-permute-start | bytes 393224 | tf_op jit(solution)/shard_map/ppermute | solution.py:27
  7.2 10.3 %collective-permute-start.6 = (bf16[32,2048]{1,0:T(8,128)(2,1)S(1)}, bf16[32,2048]{1,0:T(8,128)(2,1)S(1)}, u32[]{:S(2)}, u32[]{:S(2)}) collective-permute-start(bf16[32,2048]{1,0:T(8,128)(2,1)S(1)} %get-tuple-element.104.refs_0_.refs_6_), channel_id=1, source_target_pairs={{0,16},{4,20},{8,24},{12,28},{16,0},{20,4},{24,8},{28,12},{1,17},{... | collective-permute-start | bytes 393224 | tf_op jit(solution)/shard_map/ppermute | solution.py:27
  7.7 10.3 %collective-permute-start.5 = (bf16[32,2048]{1,0:T(8,128)(2,1)S(1)}, bf16[32,2048]{1,0:T(8,128)(2,1)S(1)}, u32[]{:S(2)}, u32[]{:S(2)}) collective-permute-start(bf16[32,2048]{1,0:T(8,128)(2,1)S(1)} %get-tuple-element.104.refs_0_.refs_6_), channel_id=1, source_target_pairs={{0,8},{4,12},{8,0},{12,4},{16,24},{20,28},{24,16},{28,20},{1,9},{5... | collective-permute-start | bytes 393224 | tf_op jit(solution)/shard_map/ppermute | solution.py:27
  8.2 5.9 %collective-permute-start.1 = (bf16[2,32,512]{2,1,0:T(8,128)(2,1)S(1)}, bf16[2,32,512]{2,1,0:T(8,128)(2,1)S(1)}, u32[]{:S(2)}, u32[]{:S(2)}) collective-permute-start(bf16[2,32,512]{2,1,0:T(8,128)(2,1)S(1)} %pack_heads.1), channel_id=1, source_target_pairs={{0,2},{1,3},{2,0},{3,1},{4,6},{5,7},{6,4},{7,5},{8,10},{9,11},{10,... | collective-permute-start | bytes 196616 | tf_op jit(solution)/shard_map/ppermute | solution.py:27
  14.3 3.6 %collective-permute-start.8 = (bf16[32,2048]{1,0:T(8,128)(2,1)S(1)}, bf16[32,2048]{1,0:T(8,128)(2,1)S(1)}, u32[]{:S(2)}, u32[]{:S(2)}) collective-permute-start(bf16[32,2048]{1,0:T(8,128)(2,1)S(1)} %get-tuple-element.102.refs_0_), channel_id=1, source_target_pairs={{0,4},{4,0},{8,12},{12,8},{16,20},{20,16},{24,28},{28,24},{1,5},{5... | collective-permute-start | bytes 393224 | tf_op jit(solution)/shard_map/ppermute | solution.py:27
  14.4 9.0 %collective-permute-start.4 = (bf16[32,2048]{1,0:T(8,128)(2,1)S(1)}, bf16[32,2048]{1,0:T(8,128)(2,1)S(1)}, u32[]{:S(2)}, u32[]{:S(2)}) collective-permute-start(bf16[32,2048]{1,0:T(8,128)(2,1)S(1)} %get-tuple-element.102.refs_0_), channel_id=1, source_target_pairs={{0,24},{4,28},{8,16},{12,20},{16,8},{20,12},{24,0},{28,4},{1,25},{... | collective-permute-start | bytes 393224 | tf_op jit(solution)/shard_map/ppermute | solution.py:27
  16.9 7.1 %collective-permute-start.3 = (bf16[32,2048]{1,0:T(8,128)(2,1)S(1)}, bf16[32,2048]{1,0:T(8,128)(2,1)S(1)}, u32[]{:S(2)}, u32[]{:S(2)}) collective-permute-start(bf16[32,2048]{1,0:T(8,128)(2,1)S(1)} %get-tuple-element.102.refs_0_), channel_id=1, source_target_pairs={{0,16},{4,20},{8,24},{12,28},{16,0},{20,4},{24,8},{28,12},{1,17},{... | collective-permute-start | bytes 393224 | tf_op jit(solution)/shard_map/ppermute | solution.py:27
  17.4 6.7 %collective-permute-start.2 = (bf16[32,2048]{1,0:T(8,128)(2,1)S(1)}, bf16[32,2048]{1,0:T(8,128)(2,1)S(1)}, u32[]{:S(2)}, u32[]{:S(2)}) collective-permute-start(bf16[32,2048]{1,0:T(8,128)(2,1)S(1)} %get-tuple-element.102.refs_0_), channel_id=1, source_target_pairs={{0,8},{4,12},{8,0},{12,4},{16,24},{20,28},{24,16},{28,20},{1,9},{5... | collective-permute-start | bytes 393224 | tf_op jit(solution)/shard_map/ppermute | solution.py:27
  18.0 2.3 %collective-permute-start.9 = (bf16[128,2048]{1,0:T(8,128)(2,1)S(1)}, bf16[128,2048]{1,0:T(8,128)(2,1)S(1)}, u32[]{:S(2)}, u32[]{:S(2)}) collective-permute-start(bf16[128,2048]{1,0:T(8,128)(2,1)S(1)} %join_rows.1.refs_0_.refs_8_), channel_id=1, source_target_pairs={{0,4},{4,0},{8,12},{12,8},{16,20},{20,16},{24,28},{28,24},{1,5},{5... | collective-permute-start | bytes 1572872 | tf_op jit(solution)/shard_map/ppermute | solution.py:27
  24.1 1.3 %collective-permute-start.10 = (bf16[32,2048]{1,0:T(8,128)(2,1)S(1)}, bf16[32,2048]{1,0:T(8,128)(2,1)S(1)}, u32[]{:S(2)}, u32[]{:S(2)}) collective-permute-start(bf16[32,2048]{1,0:T(8,128)(2,1)S(1)} %collective-permute-done.2.refs_1_), channel_id=1, source_target_pairs={{0,4},{4,0},{8,12},{12,8},{16,20},{20,16},{24,28},{28,24},{1,5},{5... | collective-permute-start | bytes 393224 | tf_op jit(solution)/shard_map/ppermute | solution.py:27
  24.1 1.5 %collective-permute-start.11 = (bf16[32,2048]{1,0:T(8,128)(2,1)S(1)}, bf16[32,2048]{1,0:T(8,128)(2,1)S(1)}, u32[]{:S(2)}, u32[]{:S(2)}) collective-permute-start(bf16[32,2048]{1,0:T(8,128)(2,1)S(1)} %collective-permute-done.3.refs_2_), channel_id=1, source_target_pairs={{0,4},{4,0},{8,12},{12,8},{16,20},{20,16},{24,28},{28,24},{1,5},{5... | collective-permute-start | bytes 393224 | tf_op jit(solution)/shard_map/ppermute | solution.py:27
  24.6 1.3 %collective-permute-start.12 = (bf16[32,2048]{1,0:T(8,128)(2,1)S(1)}, bf16[32,2048]{1,0:T(8,128)(2,1)S(1)}, u32[]{:S(2)}, u32[]{:S(2)}) collective-permute-start(bf16[32,2048]{1,0:T(8,128)(2,1)S(1)} %collective-permute-done.4.refs_3_), channel_id=1, source_target_pairs={{0,4},{4,0},{8,12},{12,8},{16,20},{20,16},{24,28},{28,24},{1,5},{5... | collective-permute-start | bytes 393224 | tf_op jit(solution)/shard_map/ppermute | solution.py:27
  37.3 2.1 %collective-permute-start.13 = (bf16[136,2048]{1,0:T(8,128)(2,1)S(1)}, bf16[136,2048]{1,0:T(8,128)(2,1)S(1)}, u32[]{:S(2)}, u32[]{:S(2)}) collective-permute-start(bf16[136,2048]{1,0:T(8,128)(2,1)S(1)} %get-tuple-element.128), channel_id=1, source_target_pairs={{0,4},{4,0},{8,12},{12,8},{16,20},{20,16},{24,28},{28,24},{1,5},{5... | collective-permute-start | bytes 1671176 | tf_op jit(solution)/shard_map/ppermute | solution.py:27
  39.5 10.9 %collective-permute-start.14 = (bf16[40,2048]{1,0:T(8,128)(2,1)S(1)}, bf16[40,2048]{1,0:T(8,128)(2,1)S(1)}, u32[]{:S(2)}, u32[]{:S(2)}) collective-permute-start(bf16[40,2048]{1,0:T(8,128)(2,1)S(1)} %get-tuple-element.139), channel_id=1, source_target_pairs={{0,24},{4,28},{8,16},{12,20},{16,8},{20,12},{24,0},{28,4},{1,25},{... | collective-permute-start | bytes 491528 | tf_op jit(solution)/shard_map/ppermute | solution.py:27
  41.7 8.7 %collective-permute-start.15 = (bf16[40,2048]{1,0:T(8,128)(2,1)S(1)}, bf16[40,2048]{1,0:T(8,128)(2,1)S(1)}, u32[]{:S(2)}, u32[]{:S(2)}) collective-permute-start(bf16[40,2048]{1,0:T(8,128)(2,1)S(1)} %get-tuple-element.140), channel_id=1, source_target_pairs={{0,16},{4,20},{8,24},{12,28},{16,0},{20,4},{24,8},{28,12},{1,17},{... | collective-permute-start | bytes 491528 | tf_op jit(solution)/shard_map/ppermute | solution.py:27
  42.5 7.9 %collective-permute-start.16 = (bf16[40,2048]{1,0:T(8,128)(2,1)S(1)}, bf16[40,2048]{1,0:T(8,128)(2,1)S(1)}, u32[]{:S(2)}, u32[]{:S(2)}) collective-permute-start(bf16[40,2048]{1,0:T(8,128)(2,1)S(1)} %get-tuple-element.141), channel_id=1, source_target_pairs={{0,8},{4,12},{8,0},{12,4},{16,24},{20,28},{24,16},{28,20},{1,9},{5... | collective-permute-start | bytes 491528 | tf_op jit(solution)/shard_map/ppermute | solution.py:27
  50.7 7.3 %collective-permute-start.17 = (bf16[1,32,512]{2,1,0:T(8,128)(2,1)S(1)}, bf16[1,32,512]{2,1,0:T(8,128)(2,1)S(1)}, u32[]{:S(2)}, u32[]{:S(2)}) collective-permute-start(bf16[1,32,512]{2,1,0:T(8,128)(2,1)S(1)} %get-tuple-element.157), channel_id=1, source_target_pairs={{0,3},{1,2},{2,1},{3,0},{4,7},{5,6},{6,5},{7,4},{8,11},{9,10},{10,... | collective-permute-start | bytes 98312 | tf_op jit(solution)/shard_map/ppermute | solution.py:27
  52.8 5.2 %collective-permute-start.18 = (bf16[1,32,512]{2,1,0:T(8,128)(2,1)S(1)}, bf16[1,32,512]{2,1,0:T(8,128)(2,1)S(1)}, u32[]{:S(2)}, u32[]{:S(2)}) collective-permute-start(bf16[1,32,512]{2,1,0:T(8,128)(2,1)S(1)} %get-tuple-element.158), channel_id=1, source_target_pairs={{0,2},{1,3},{2,0},{3,1},{4,6},{5,7},{6,4},{7,5},{8,10},{9,11},{10,... | collective-permute-start | bytes 98312 | tf_op jit(solution)/shard_map/ppermute | solution.py:27
  52.8 5.2 %collective-permute-start.19 = (bf16[1,32,512]{2,1,0:T(8,128)(2,1)S(1)}, bf16[1,32,512]{2,1,0:T(8,128)(2,1)S(1)}, u32[]{:S(2)}, u32[]{:S(2)}) collective-permute-start(bf16[1,32,512]{2,1,0:T(8,128)(2,1)S(1)} %get-tuple-element.159), channel_id=1, source_target_pairs={{0,1},{1,0},{2,3},{3,2},{4,5},{5,4},{6,7},{7,6},{8,9},{9,8},{10,11... | collective-permute-start | bytes 98312 | tf_op jit(solution)/shard_map/ppermute | solution.py:27
  55.1 2.8 %collective-permute-start.20 = (f32[8,1024]{1,0:T(8,128)S(1)}, f32[8,1024]{1,0:T(8,128)S(1)}, u32[]{:S(2)}, u32[]{:S(2)}) collective-permute-start(f32[8,1024]{1,0:T(8,128)S(1)} %get-tuple-element.156.small_ref), channel_id=1, source_target_pairs={{0,4},{4,0},{8,12},{12,8},{16,20},{20,16},{24,28},{28,24},{1,5},{5... | collective-permute-start | bytes 98312 | tf_op jit(solution)/shard_map/ppermute | solution.py:27

commit v4 on v3

--- a/solution.py
+++ b/solution.py
@@ -158,7 +158,7 @@
     return tuple((d,) + pick((d, 0), lists) for d in range(1, num_tokens))
 
 
-def small_kernel(gain_hbm, router_hbm, route_hbm, down_hbm, *refs):
+def small_kernel(gain_hbm, router_in, route_hbm, down_hbm, *refs):
     gain_ref, router_ref, chosen_ref, down_ref, routes, sems, down_sem = refs
     load = pltpu.make_async_copy(down_hbm.at[0, pl.ds(0, down_ref.shape[0])], down_ref, down_sem)
     load.start()
@@ -167,13 +167,13 @@
         for i, (src, dst) in enumerate(
             [
                 (gain_hbm, gain_ref),
-                (router_hbm, router_ref),
                 (route_hbm, routes),
             ]
         )
     ]
     for copy in copies:
         copy.start()
+    router_ref[...] = router_in[...]
     for copy in copies:
         copy.wait()
     rows, experts = chosen_ref.shape
@@ -189,7 +189,7 @@
     experts, all_rows = 8, routes.shape[1]
     return pl.pallas_call(
         small_kernel,
-        in_specs=[IN_HBM] * 4,
+        in_specs=[IN_HBM, IN_VMEM, IN_HBM, IN_HBM],
         out_specs=(IN_VMEM,) * 3 + (ANYWHERE,),
         out_shape=(
             jax.ShapeDtypeStruct(gain.shape, F32),
@@ -199,13 +199,13 @@
         ),
         scratch_shapes=[
             pltpu.VMEM(routes.shape, jnp.int32),
-            pltpu.SemaphoreType.DMA((3,)),
+            pltpu.SemaphoreType.DMA((2,)),
             pltpu.SemaphoreType.DMA(()),
         ],
         compiler_params=pltpu.CompilerParams(vmem_limit_bytes=4 * MIB),
         cost_estimate=pl.CostEstimate(flops=2**36, bytes_accessed=32 * MIB, transcendentals=0),
         name="small_operands",
-    )(hbm(gain), hbm(router_rows), hbm(routes), hbm(w_down))
+    )(hbm(gain), router_rows, hbm(routes), hbm(w_down))
 
 
 def norm_kernel(places, x_ref, gain_ref, *refs):
@@ -393,8 +393,7 @@
         for i in range(size // 2):
             kept[i][:, here] = grad[i * own : (i + 1) * own]
         sent_out[:half, here] = grad[half:]
-    core = me % 2
-    sent_out[half:] = two_terms(small_out[:, head_slice(1 - core, width // 2)])
+    sent_out[half:] = wide_terms(small_out[...])
 
 
 def experts_backward(chunks, first, w_gate, w_up, back, chosen, router_rows, gain):
@@ -408,7 +407,7 @@
         out_shape=(
             jax.ShapeDtypeStruct((rows, 2 * experts * hidden), BF16),
             jax.ShapeDtypeStruct((rows, experts * hidden), BF16),
-            jax.ShapeDtypeStruct((rows // 2 + 8, width), BF16),
+            jax.ShapeDtypeStruct((rows // 2 + 16, width), BF16),
         )
         + (kept,) * (size // 2)
         + (jax.ShapeDtypeStruct((8, width), F32),),
@@ -429,33 +428,47 @@
 
 
 def two_terms(small):
-    high = small.astype(BF16)
-    low = (small - high.astype(F32)).astype(BF16)
-    return jnp.concatenate([high, low], axis=1)
-
-
-def one_term(terms):
-    half = terms.shape[1] // 2
-    return terms[:, :half].astype(F32) + terms[:, half:].astype(F32)
+    high = small.astype(BF16).astype(F32)
+    return high, small - high
+
+
+def wide_terms(small):
+    return jnp.concatenate(two_terms(small), axis=0).astype(BF16)
+
+
+def tall_terms(small):
+    half = small.shape[1] // 2
+    terms = [term[:, c : c + half] for c in (0, half) for term in two_terms(small)]
+    return jnp.concatenate(terms, axis=0).astype(BF16)
+
+
+def from_tall(terms):
+    terms = terms.astype(F32)
+    return jnp.concatenate([terms[:8] + terms[8:16], terms[16:24] + terms[24:32]], axis=1)
 
 
 def pair_kernel(count, *refs):
-    kept, (arrived_ref, small_ref), outs = refs[:count], refs[count : count + 2], refs[count + 2 :]
+    kept, (arrived_ref, small_ref) = refs[:count], refs[count : count + 2]
+    outs, total_ref = refs[count + 2 : -1], refs[-1]
     own, width = kept[0].shape
     core = lax.axis_index("dp") % 2
-    mine = small_ref[:, head_slice(core, width // 2)]
-    small = two_terms(mine + one_term(arrived_ref[count * own :]))
+    arrived = arrived_ref[count * own :].astype(F32)
+    total_ref[...] = small_ref[...] + arrived[:8] + arrived[8:]
+    small = tall_terms(total_ref[:, head_slice(core, width // 2)])
     for i in range(count):
         arrived = arrived_ref[i * own : (i + 1) * own].astype(F32)
-        outs[i][:own] = (kept[i][...].astype(F32) + arrived).astype(BF16)
-        outs[i][own:] = small
+        outs[i][:, :width] = (kept[i][...].astype(F32) + arrived).astype(BF16)
+        outs[i][:32, width:] = small
+        if own > 32:
+            outs[i][32:, width:] = jnp.zeros((own - 32, width // 4), BF16)
 
 
 def pair_sum(kept, arrived, small):
     own, width = kept[0].shape
     return pl.pallas_call(
         functools.partial(pair_kernel, len(kept)),
-        out_shape=(jax.ShapeDtypeStruct((own + 8, width), BF16),) * len(kept),
+        out_shape=(jax.ShapeDtypeStruct((own, width + width // 4), BF16),) * len(kept),
+        scratch_shapes=[pltpu.VMEM(small.shape, F32)],
         compiler_params=pltpu.CompilerParams(vmem_limit_bytes=4 * MIB),
         name="pair_sum",
     )(*kept, arrived, small)
@@ -503,7 +516,7 @@
     assemble(cot, cot_chunks)
     hidden = down_out.shape[2]
     for e in down_experts:
-        parts = 2 if e == down_experts[-1] else 1
+        parts = 2
         step = hidden // parts
         for first in range(0, hidden, step):
             columns = slice(e * hidden + first, e * hidden + first + step)
@@ -543,10 +556,10 @@
 def norm_back_kernel(count, *refs):
     parts, (summed_ref, gain_ref, cot_ref) = refs[:count], refs[count : count + 3]
     grad_ref, small_out, *sends = refs[count + 3 :]
-    own = summed_ref.shape[0]
-    grad_normed = parts[0][:own].astype(F32)
+    full = summed_ref.shape[1]
+    grad_normed = parts[0][:, :full].astype(F32)
     for part in parts[1:]:
-        grad_normed = grad_normed + part[:own].astype(F32)
+        grad_normed = grad_normed + part[:, :full].astype(F32)
     summed = summed_ref[...]
     inv_rms = lax.rsqrt(jnp.mean(summed * summed, axis=1, keepdims=True) + 1e-06)
     scaled = grad_normed * gain_ref[...]
@@ -558,7 +571,7 @@
         place = head_slice(lax.axis_index("tok") ^ (s + 1), head)
         send[0] = grad_ref[:, place].astype(BF16)
     me = lax.axis_index("dp") // 2
-    smalls = jnp.stack([one_term(part[own:]) for part in parts])
+    smalls = jnp.stack([from_tall(part[:32, full:]) for part in parts])
     small = jnp.zeros(smalls.shape[1:], F32)
     for chip in range(count):
         for i in range(count):

time: 58.9 us -> 59.7 us (1.014)
  local copies, waits for them, and re-layouts: 0 us -> 0.72 us
    unnamed x0 -> x2, local copies, waits for them, and re-layouts: none -> 0.72 us
  transfers between devices with their start and end apart: 21 -> 21, of which waited for: 6 -> 5; matrix products, arithmetic and copies ran while one was open for 0% -> 0% of each run, Pallas kernels for 35% -> 34%
where the time goes in v4:
time: 59.7 us; the launch traced here: 59.3 us
  Pallas kernels  34 us (57%)
  starting transfers between devices  21.7 us (36%)
  waiting for transfers between devices  2.1 us (4%)
  between operations  0.83 us (1%)
  local copies, waits for them, and re-layouts  0.72 us (1%)
    ppermute x21, starting transfers between devices, exchange(): return lax.ppermute(value, axis, [(i, i ^ distance) for i in range(size)])  21.7 us
    pallas_call x1, Pallas kernels, experts_backward(): pl.pallas_call(functools.partial(expert_kernel, size), in_specs=[IN_VMEM]...  11.9 us
    pallas_call x3, Pallas kernels, weight_gradients(): pl.pallas_call(functools.partial(weight_kernel, (len(normed_chunks), len(...  11.7 us
    pallas_call x1, Pallas kernels, back_hidden(): pl.pallas_call(functools.partial(back_kernel, len(chunks)), in_specs=[IN_...  3.04 us
    pallas_call x1, Pallas kernels, small_operands(): pl.pallas_call(small_kernel, in_specs=[IN_HBM, IN_VMEM, IN_HBM, IN_HBM],...  2.83 us
    pallas_call x1, Pallas kernels, load_first(): pl.pallas_call(load_kernel, in_specs=[IN_HBM] * 2, out_specs=ANYWHERE, ou...  2.24 us
    ppermute x21, waiting for transfers between devices, exchange(): return lax.ppermute(value, axis, [(i, i ^ distance) for i in range(size)])  2.1 us
  transfers between devices with their start and end apart: 21, of which 5 were waited for; matrix products, arithmetic and copies ran while one was open for 0% of the time, Pallas kernels for 34%

profile of v4, /device:TPU:0, one launch (start us, length us, event | category | flops | bytes accessed | tf_op | source)
XLA Modules:
  0.0 59.3 jit_solution(6018889177433268862)
XLA Ops:
  0.6 1.0 %split_heads.1 = (bf16[32,2048]{1,0:T(8,128)(2,1)S(1)}, bf16[32,2048]{1,0:T(8,128)(2,1)S(1)}, bf16[2,32,512]{2,1,0:T(8,128)(2,1)S(1)}, bf16[1,32,512]{2,1,0:T(8,128)(2,1)S(1)}) custom-call(bf16[1,32,2048]{2,1,0:T(8,128)(2,1)} %x_hbm.1, bf16[1,32,2048]{2,1,0:T(8,128)(2,1)} %cot_hbm.1), custom_call_target="tpu_custom_call" | custom-call | tf_op jit(solution)/shard_map/split_heads/pallas_call | solution.py:146
  1.6 3.1 %collective-permute-start = (bf16[2,32,512]{2,1,0:T(8,128)(2,1)S(1)}, bf16[2,32,512]{2,1,0:T(8,128)(2,1)S(1)}, u32[]{:S(2)}, u32[]{:S(2)}) collective-permute-start(bf16[2,32,512]{2,1,0:T(8,128)(2,1)S(1)} %get-tuple-element.91), channel_id=1, source_target_pairs={{0,1},{1,0},{2,3},{3,2},{4,5},{5,4},{6,7},{7,6},{8,9},{9,8},{10,11... | collective-permute-start | bytes 196616 | tf_op jit(solution)/shard_map/ppermute | solution.py:27
  4.7 2.4 %collective-permute-start.7 = (bf16[32,2048]{1,0:T(8,128)(2,1)S(1)}, bf16[32,2048]{1,0:T(8,128)(2,1)S(1)}, u32[]{:S(2)}, u32[]{:S(2)}) collective-permute-start(bf16[32,2048]{1,0:T(8,128)(2,1)S(1)} %get-tuple-element.104.refs_0_.refs_6_), channel_id=1, source_target_pairs={{0,24},{4,28},{8,16},{12,20},{16,8},{20,12},{24,0},{28,4},{1,25},{... | collective-permute-start | bytes 393224 | tf_op jit(solution)/shard_map/ppermute | solution.py:27
  7.7 0.5 collective-permute-start.5
  8.2 2.7 %collective-permute-start.1 = (bf16[2,32,512]{2,1,0:T(8,128)(2,1)S(1)}, bf16[2,32,512]{2,1,0:T(8,128)(2,1)S(1)}, u32[]{:S(2)}, u32[]{:S(2)}) collective-permute-start(bf16[2,32,512]{2,1,0:T(8,128)(2,1)S(1)} %pack_heads.1), channel_id=1, source_target_pairs={{0,2},{1,3},{2,0},{3,1},{4,6},{5,7},{6,4},{7,5},{8,10},{9,11},{10,... | collective-permute-start | bytes 196616 | tf_op jit(solution)/shard_map/ppermute | solution.py:27
  10.9 0.7 %copy-done = bf16[1,2048,4]{1,2,0:T(4,128)(2,1)S(1)} copy-done((bf16[1,2048,4]{1,2,0:T(4,128)(2,1)S(1)}, bf16[1,2048,4]{1,2,0:T(4,128)(2,1)}, u32[]{:S(2)}) %copy-start) | copy-done | bytes 16408
  11.6 2.8 %small_operands.1 = (f32[1,2048]{1,0:T(1,128)S(1)}, bf16[4,2048]{1,0:T(4,128)(2,1)S(1)}, f32[256,8]{1,0:T(8,128)S(1)}, bf16[3,512,2048]{2,1,0:T(8,128)(2,1)S(1)}) custom-call(f32[1,2048]{1,0:T(1,128)} %gain_hbm, bf16[4,2048]{1,0:T(4,128)(2,1)S(1)} %bitcast.9, s32[2,256]{1,0:T(2,128)} %bitcast.11, bf16[1,4,512,2048]{3,2,1,0:T(8,128)(2,1)} %refs_3_.1), custom_call_target="tpu_custom_call" | custom-call | flops 68719476736 | bytes 33554432 | tf_op jit(solution)/shard_map/small_operands/pallas_call | solution.py:190
  14.7 2.5 %collective-permute-start.4 = (bf16[32,2048]{1,0:T(8,128)(2,1)S(1)}, bf16[32,2048]{1,0:T(8,128)(2,1)S(1)}, u32[]{:S(2)}, u32[]{:S(2)}) collective-permute-start(bf16[32,2048]{1,0:T(8,128)(2,1)S(1)} %get-tuple-element.102.refs_0_), channel_id=1, source_target_pairs={{0,24},{4,28},{8,16},{12,20},{16,8},{20,12},{24,0},{28,4},{1,25},{... | collective-permute-start | bytes 393224 | tf_op jit(solution)/shard_map/ppermute | solution.py:27
  17.7 0.5 collective-permute-start.2
  18.4 2.2 %load_first.1.refs_6_ = bf16[2048,2048]{1,0:T(8,128)(2,1)S(1)} custom-call(bf16[1,4,2048,512]{3,2,1,0:T(8,128)(2,1)} %refs_9_.1, bf16[1,4,2048,512]{3,2,1,0:T(8,128)(2,1)} %refs_10_.1), custom_call_target="tpu_custom_call" | custom-call | flops 68719476736 | bytes 4194304 | tf_op jit(solution)/shard_map/load_first/pallas_call | solution.py:265
  20.6 3.0 %back_hidden.1 = (f32[4,256,512]{2,1,0:T(8,128)S(1)}, bf16[2048,2048]{1,0:T(8,128)(2,1)S(1)}) custom-call(bf16[128,2048]{1,0:T(8,128)(2,1)S(1)} %join_rows.1.refs_0_.refs_8_, bf16[128,2048]{1,0:T(8,128)(2,1)S(1)} %collective-permute-done.9.refs_1_.refs_9_, bf16[3,512,2048]{2,1,0:T(8,128)(2,1)S(1)} %get-tuple-element.111.refs_2_, ...), custom_call_target="tpu_custom_call", output_to_operand_aliasing={{1}: (6, {})} | custom-call | tf_op jit(solution)/shard_map/back_hidden/pallas_call | solution.py:303
  23.7 0.6 %collective-permute-done.3.refs_2_ = bf16[32,2048]{1,0:T(8,128)(2,1)S(1)} collective-permute-done((bf16[32,2048]{1,0:T(8,128)(2,1)S(1)}, bf16[32,2048]{1,0:T(8,128)(2,1)S(1)}, u32[]{:S(2)}, u32[]{:S(2)}) %collective-permute-start.3) | collective-permute-done | bytes 131104 | tf_op jit(solution)/shard_map/ppermute | solution.py:27
  24.4 0.5 collective-permute-start.11
  24.9 0.8 %collective-permute-done.10.refs_5_ = bf16[32,2048]{1,0:T(8,128)(2,1)S(1)} collective-permute-done((bf16[32,2048]{1,0:T(8,128)(2,1)S(1)}, bf16[32,2048]{1,0:T(8,128)(2,1)S(1)}, u32[]{:S(2)}, u32[]{:S(2)}) %collective-permute-start.10) | collective-permute-done | bytes 131104 | tf_op jit(solution)/shard_map/ppermute | solution.py:27
  26.3 11.9 %experts_backward.1 = (bf16[256,4096]{1,0:T(8,128)(2,1)S(1)}, bf16[256,2048]{1,0:T(8,128)(2,1)S(1)}, bf16[144,2048]{1,0:T(8,128)(2,1)S(1)}, bf16[32,2048]{1,0:T(...) custom-call(bf16[32,2048]{1,0:T(8,128)(2,1)S(1)} %get-tuple-element., ...), custom_call_target="tpu_custom_call" | custom-call | flops 8589934592 | bytes 24117248 | tf_op jit(solution)/shard_map/experts_backward/pallas_call | solution.py:404
  38.4 1.8 %grad_down_0.1.refs_12_ = bf16[1,4,512,2048]{3,2,1,0:T(8,128)(2,1)} custom-call(bf16[128,2048]{1,0:T(8,128)(2,1)S(1)} %join_rows.1.refs_0_.refs_8_, bf16[128,2048]{1,0:T(8,128)(2,1)S(1)} %collective-permute-done.9.refs_1_.refs_9_, bf16[256,2048]{1,0:T(8,128)(2,1)S(1)} %get-tuple-element.160.refs_2_.refs_11_), custom_call_target="tpu_custom_call" | custom-call | flops 536870912 | bytes 2097152 | tf_op jit(solution)/shard_map/grad_down_0/pallas_call | solution.py:540
  40.4 2.2 %collective-permute-start.14 = (bf16[32,2560]{1,0:T(8,128)(2,1)S(1)}, bf16[32,2560]{1,0:T(8,128)(2,1)S(1)}, u32[]{:S(2)}, u32[]{:S(2)}) collective-permute-start(bf16[32,2560]{1,0:T(8,128)(2,1)S(1)} %get-tuple-element.139), channel_id=1, source_target_pairs={{0,24},{4,28},{8,16},{12,20},{16,8},{20,12},{24,0},{28,4},{1,25},{... | collective-permute-start | bytes 491528 | tf_op jit(solution)/shard_map/ppermute | solution.py:27
  42.6 0.8 %collective-permute-start.15 = (bf16[32,2560]{1,0:T(8,128)(2,1)S(1)}, bf16[32,2560]{1,0:T(8,128)(2,1)S(1)}, u32[]{:S(2)}, u32[]{:S(2)}) collective-permute-start(bf16[32,2560]{1,0:T(8,128)(2,1)S(1)} %get-tuple-element.140), channel_id=1, source_target_pairs={{0,16},{4,20},{8,24},{12,28},{16,0},{20,4},{24,8},{28,12},{1,17},{... | collective-permute-start | bytes 491528 | tf_op jit(solution)/shard_map/ppermute | solution.py:27
  43.5 0.5 collective-permute-start.16
  44.0 7.3 %grad_gate_up.1 = (bf16[1,4,2048,512]{3,2,1,0:T(8,128)(2,1)}, bf16[1,4,2048,512]{3,2,1,0:T(8,128)(2,1)}, bf16[1,4,512,2048]{3,2,1,0:T(8,128)(2,1)}) custom-call(bf16[32,2048]{1,0:T(8,128)(2,1)S(1)} %get-tuple-element.102.refs_0_, bf16[32,2048]{1,0:T(8,128)(2,1)S(1)} %collective-permute-done.2.refs_1_, ...), custom_call_target="tpu_custom_call", output_to_operand_aliasing={{2}: (12, {})} | custom-call | flops 4831838208 | bytes 18874368 | tf_op jit(solution)/shard_map/grad_gate_up/pallas_call | solution.py:540
  51.6 1.8 %collective-permute-start.17 = (bf16[1,32,512]{2,1,0:T(8,128)(2,1)S(1)}, bf16[1,32,512]{2,1,0:T(8,128)(2,1)S(1)}, u32[]{:S(2)}, u32[]{:S(2)}) collective-permute-start(bf16[1,32,512]{2,1,0:T(8,128)(2,1)S(1)} %get-tuple-element.157), channel_id=1, source_target_pairs={{0,3},{1,2},{2,1},{3,0},{4,7},{5,6},{6,5},{7,4},{8,11},{9,10},{10,... | collective-permute-start | bytes 98312 | tf_op jit(solution)/shard_map/ppermute | solution.py:27
  53.8 2.2 %collective-permute-start.19 = (bf16[1,32,512]{2,1,0:T(8,128)(2,1)S(1)}, bf16[1,32,512]{2,1,0:T(8,128)(2,1)S(1)}, u32[]{:S(2)}, u32[]{:S(2)}) collective-permute-start(bf16[1,32,512]{2,1,0:T(8,128)(2,1)S(1)} %get-tuple-element.159), channel_id=1, source_target_pairs={{0,1},{1,0},{2,3},{3,2},{4,5},{5,4},{6,7},{7,6},{8,9},{9,8},{10,11... | collective-permute-start | bytes 98312 | tf_op jit(solution)/shard_map/ppermute | solution.py:27
  56.1 2.5 %grad_down.1 = bf16[1,4,512,2048]{3,2,1,0:T(8,128)(2,1)} custom-call(bf16[128,2048]{1,0:T(8,128)(2,1)S(1)} %join_rows.1.refs_0_.refs_8_, bf16[128,2048]{1,0:T(8,128)(2,1)S(1)} %collective-permute-done.9.refs_1_.refs_9_, bf16[256,2048]{1,0:T(8,128)(2,1)S(1)} %get-tuple-element.160.refs_2_.refs_11_, ...), custom_call_target="tpu_custom_call", output_to_operand_aliasing={{}: (3, {})} | custom-call | flops 1073741824 | bytes 4194304 | tf_op jit(solution)/shard_map/grad_down/pallas_call | solution.py:540
  58.6 0.7 %finish.1 = (bf16[1,32,2048]{2,1,0:T(8,128)(2,1)}, f32[4,2048]{1,0:T(4,128)}, f32[1,2048]{1,0:T(1,128)}) custom-call(f32[32,2048]{1,0:T(8,128)S(1)} %get-tuple-element.151.grad_ref, f32[8,1024]{1,0:T(8,128)S(1)} %get-tuple-element.156.small_ref, f32[8,1024]{1,0:T(8,128)S(1)} %collective-permute-done.20.other_ref, ...), custom_call_target="tpu_custom_call" | custom-call | tf_op jit(solution)/shard_map/finish/pallas_call | solution.py:617
  (34 shorter events, 3.1 us)
Async XLA Ops:
  1.6 6.6 %collective-permute-start = (bf16[2,32,512]{2,1,0:T(8,128)(2,1)S(1)}, bf16[2,32,512]{2,1,0:T(8,128)(2,1)S(1)}, u32[]{:S(2)}, u32[]{:S(2)}) collective-permute-start(bf16[2,32,512]{2,1,0:T(8,128)(2,1)S(1)} %get-tuple-element.91), channel_id=1, source_target_pairs={{0,1},{1,0},{2,3},{3,2},{4,5},{5,4},{6,7},{7,6},{8,9},{9,8},{10,11... | collective-permute-start | bytes 196616 | tf_op jit(solution)/shard_map/ppermute | solution.py:27
  4.7 12.5 %collective-permute-start.7 = (bf16[32,2048]{1,0:T(8,128)(2,1)S(1)}, bf16[32,2048]{1,0:T(8,128)(2,1)S(1)}, u32[]{:S(2)}, u32[]{:S(2)}) collective-permute-start(bf16[32,2048]{1,0:T(8,128)(2,1)S(1)} %get-tuple-element.104.refs_0_.refs_6_), channel_id=1, source_target_pairs={{0,24},{4,28},{8,16},{12,20},{16,8},{20,12},{24,0},{28,4},{1,25},{... | collective-permute-start | bytes 393224 | tf_op jit(solution)/shard_map/ppermute | solution.py:27
  7.2 10.5 %collective-permute-start.6 = (bf16[32,2048]{1,0:T(8,128)(2,1)S(1)}, bf16[32,2048]{1,0:T(8,128)(2,1)S(1)}, u32[]{:S(2)}, u32[]{:S(2)}) collective-permute-start(bf16[32,2048]{1,0:T(8,128)(2,1)S(1)} %get-tuple-element.104.refs_0_.refs_6_), channel_id=1, source_target_pairs={{0,16},{4,20},{8,24},{12,28},{16,0},{20,4},{24,8},{28,12},{1,17},{... | collective-permute-start | bytes 393224 | tf_op jit(solution)/shard_map/ppermute | solution.py:27
  7.7 10.6 %collective-permute-start.5 = (bf16[32,2048]{1,0:T(8,128)(2,1)S(1)}, bf16[32,2048]{1,0:T(8,128)(2,1)S(1)}, u32[]{:S(2)}, u32[]{:S(2)}) collective-permute-start(bf16[32,2048]{1,0:T(8,128)(2,1)S(1)} %get-tuple-element.104.refs_0_.refs_6_), channel_id=1, source_target_pairs={{0,8},{4,12},{8,0},{12,4},{16,24},{20,28},{24,16},{28,20},{1,9},{5... | collective-permute-start | bytes 393224 | tf_op jit(solution)/shard_map/ppermute | solution.py:27
  8.2 6.2 %collective-permute-start.1 = (bf16[2,32,512]{2,1,0:T(8,128)(2,1)S(1)}, bf16[2,32,512]{2,1,0:T(8,128)(2,1)S(1)}, u32[]{:S(2)}, u32[]{:S(2)}) collective-permute-start(bf16[2,32,512]{2,1,0:T(8,128)(2,1)S(1)} %pack_heads.1), channel_id=1, source_target_pairs={{0,2},{1,3},{2,0},{3,1},{4,6},{5,7},{6,4},{7,5},{8,10},{9,11},{10,... | collective-permute-start | bytes 196616 | tf_op jit(solution)/shard_map/ppermute | solution.py:27
  10.9 0.7 %copy-start = (bf16[1,2048,4]{1,2,0:T(4,128)(2,1)S(1)}, bf16[1,2048,4]{1,2,0:T(4,128)(2,1)}, u32[]{:S(2)}) copy-start(bf16[1,2048,4]{1,2,0:T(4,128)(2,1)} %param.11) | copy-start | bytes 49156
  14.6 3.6 %collective-permute-start.8 = (bf16[32,2048]{1,0:T(8,128)(2,1)S(1)}, bf16[32,2048]{1,0:T(8,128)(2,1)S(1)}, u32[]{:S(2)}, u32[]{:S(2)}) collective-permute-start(bf16[32,2048]{1,0:T(8,128)(2,1)S(1)} %get-tuple-element.102.refs_0_), channel_id=1, source_target_pairs={{0,4},{4,0},{8,12},{12,8},{16,20},{20,16},{24,28},{28,24},{1,5},{5... | collective-permute-start | bytes 393224 | tf_op jit(solution)/shard_map/ppermute | solution.py:27
  14.7 9.0 %collective-permute-start.4 = (bf16[32,2048]{1,0:T(8,128)(2,1)S(1)}, bf16[32,2048]{1,0:T(8,128)(2,1)S(1)}, u32[]{:S(2)}, u32[]{:S(2)}) collective-permute-start(bf16[32,2048]{1,0:T(8,128)(2,1)S(1)} %get-tuple-element.102.refs_0_), channel_id=1, source_target_pairs={{0,24},{4,28},{8,16},{12,20},{16,8},{20,12},{24,0},{28,4},{1,25},{... | collective-permute-start | bytes 393224 | tf_op jit(solution)/shard_map/ppermute | solution.py:27
  17.2 7.1 %collective-permute-start.3 = (bf16[32,2048]{1,0:T(8,128)(2,1)S(1)}, bf16[32,2048]{1,0:T(8,128)(2,1)S(1)}, u32[]{:S(2)}, u32[]{:S(2)}) collective-permute-start(bf16[32,2048]{1,0:T(8,128)(2,1)S(1)} %get-tuple-element.102.refs_0_), channel_id=1, source_target_pairs={{0,16},{4,20},{8,24},{12,28},{16,0},{20,4},{24,8},{28,12},{1,17},{... | collective-permute-start | bytes 393224 | tf_op jit(solution)/shard_map/ppermute | solution.py:27
  17.7 6.7 %collective-permute-start.2 = (bf16[32,2048]{1,0:T(8,128)(2,1)S(1)}, bf16[32,2048]{1,0:T(8,128)(2,1)S(1)}, u32[]{:S(2)}, u32[]{:S(2)}) collective-permute-start(bf16[32,2048]{1,0:T(8,128)(2,1)S(1)} %get-tuple-element.102.refs_0_), channel_id=1, source_target_pairs={{0,8},{4,12},{8,0},{12,4},{16,24},{20,28},{24,16},{28,20},{1,9},{5... | collective-permute-start | bytes 393224 | tf_op jit(solution)/shard_map/ppermute | solution.py:27
  18.3 2.3 %collective-permute-start.9 = (bf16[128,2048]{1,0:T(8,128)(2,1)S(1)}, bf16[128,2048]{1,0:T(8,128)(2,1)S(1)}, u32[]{:S(2)}, u32[]{:S(2)}) collective-permute-start(bf16[128,2048]{1,0:T(8,128)(2,1)S(1)} %join_rows.1.refs_0_.refs_8_), channel_id=1, source_target_pairs={{0,4},{4,0},{8,12},{12,8},{16,20},{20,16},{24,28},{28,24},{1,5},{5... | collective-permute-start | bytes 1572872 | tf_op jit(solution)/shard_map/ppermute | solution.py:27
  24.4 1.3 %collective-permute-start.10 = (bf16[32,2048]{1,0:T(8,128)(2,1)S(1)}, bf16[32,2048]{1,0:T(8,128)(2,1)S(1)}, u32[]{:S(2)}, u32[]{:S(2)}) collective-permute-start(bf16[32,2048]{1,0:T(8,128)(2,1)S(1)} %collective-permute-done.2.refs_1_), channel_id=1, source_target_pairs={{0,4},{4,0},{8,12},{12,8},{16,20},{20,16},{24,28},{28,24},{1,5},{5... | collective-permute-start | bytes 393224 | tf_op jit(solution)/shard_map/ppermute | solution.py:27
  24.4 1.5 %collective-permute-start.11 = (bf16[32,2048]{1,0:T(8,128)(2,1)S(1)}, bf16[32,2048]{1,0:T(8,128)(2,1)S(1)}, u32[]{:S(2)}, u32[]{:S(2)}) collective-permute-start(bf16[32,2048]{1,0:T(8,128)(2,1)S(1)} %collective-permute-done.3.refs_2_), channel_id=1, source_target_pairs={{0,4},{4,0},{8,12},{12,8},{16,20},{20,16},{24,28},{28,24},{1,5},{5... | collective-permute-start | bytes 393224 | tf_op jit(solution)/shard_map/ppermute | solution.py:27
  24.9 1.3 %collective-permute-start.12 = (bf16[32,2048]{1,0:T(8,128)(2,1)S(1)}, bf16[32,2048]{1,0:T(8,128)(2,1)S(1)}, u32[]{:S(2)}, u32[]{:S(2)}) collective-permute-start(bf16[32,2048]{1,0:T(8,128)(2,1)S(1)} %collective-permute-done.4.refs_3_), channel_id=1, source_target_pairs={{0,4},{4,0},{8,12},{12,8},{16,20},{20,16},{24,28},{28,24},{1,5},{5... | collective-permute-start | bytes 393224 | tf_op jit(solution)/shard_map/ppermute | solution.py:27
  38.2 2.1 %collective-permute-start.13 = (bf16[144,2048]{1,0:T(8,128)(2,1)S(1)}, bf16[144,2048]{1,0:T(8,128)(2,1)S(1)}, u32[]{:S(2)}, u32[]{:S(2)}) collective-permute-start(bf16[144,2048]{1,0:T(8,128)(2,1)S(1)} %get-tuple-element.128), channel_id=1, source_target_pairs={{0,4},{4,0},{8,12},{12,8},{16,20},{20,16},{24,28},{28,24},{1,5},{5... | collective-permute-start | bytes 1769480 | tf_op jit(solution)/shard_map/ppermute | solution.py:27
  40.4 10.9 %collective-permute-start.14 = (bf16[32,2560]{1,0:T(8,128)(2,1)S(1)}, bf16[32,2560]{1,0:T(8,128)(2,1)S(1)}, u32[]{:S(2)}, u32[]{:S(2)}) collective-permute-start(bf16[32,2560]{1,0:T(8,128)(2,1)S(1)} %get-tuple-element.139), channel_id=1, source_target_pairs={{0,24},{4,28},{8,16},{12,20},{16,8},{20,12},{24,0},{28,4},{1,25},{... | collective-permute-start | bytes 491528 | tf_op jit(solution)/shard_map/ppermute | solution.py:27
  42.6 8.7 %collective-permute-start.15 = (bf16[32,2560]{1,0:T(8,128)(2,1)S(1)}, bf16[32,2560]{1,0:T(8,128)(2,1)S(1)}, u32[]{:S(2)}, u32[]{:S(2)}) collective-permute-start(bf16[32,2560]{1,0:T(8,128)(2,1)S(1)} %get-tuple-element.140), channel_id=1, source_target_pairs={{0,16},{4,20},{8,24},{12,28},{16,0},{20,4},{24,8},{28,12},{1,17},{... | collective-permute-start | bytes 491528 | tf_op jit(solution)/shard_map/ppermute | solution.py:27
  43.5 7.9 %collective-permute-start.16 = (bf16[32,2560]{1,0:T(8,128)(2,1)S(1)}, bf16[32,2560]{1,0:T(8,128)(2,1)S(1)}, u32[]{:S(2)}, u32[]{:S(2)}) collective-permute-start(bf16[32,2560]{1,0:T(8,128)(2,1)S(1)} %get-tuple-element.141), channel_id=1, source_target_pairs={{0,8},{4,12},{8,0},{12,4},{16,24},{20,28},{24,16},{28,20},{1,9},{5... | collective-permute-start | bytes 491528 | tf_op jit(solution)/shard_map/ppermute | solution.py:27
  51.6 7.0 %collective-permute-start.17 = (bf16[1,32,512]{2,1,0:T(8,128)(2,1)S(1)}, bf16[1,32,512]{2,1,0:T(8,128)(2,1)S(1)}, u32[]{:S(2)}, u32[]{:S(2)}) collective-permute-start(bf16[1,32,512]{2,1,0:T(8,128)(2,1)S(1)} %get-tuple-element.157), channel_id=1, source_target_pairs={{0,3},{1,2},{2,1},{3,0},{4,7},{5,6},{6,5},{7,4},{8,11},{9,10},{10,... | collective-permute-start | bytes 98312 | tf_op jit(solution)/shard_map/ppermute | solution.py:27
  53.4 5.2 %collective-permute-start.18 = (bf16[1,32,512]{2,1,0:T(8,128)(2,1)S(1)}, bf16[1,32,512]{2,1,0:T(8,128)(2,1)S(1)}, u32[]{:S(2)}, u32[]{:S(2)}) collective-permute-start(bf16[1,32,512]{2,1,0:T(8,128)(2,1)S(1)} %get-tuple-element.158), channel_id=1, source_target_pairs={{0,2},{1,3},{2,0},{3,1},{4,6},{5,7},{6,4},{7,5},{8,10},{9,11},{10,... | collective-permute-start | bytes 98312 | tf_op jit(solution)/shard_map/ppermute | solution.py:27
  53.8 4.8 %collective-permute-start.19 = (bf16[1,32,512]{2,1,0:T(8,128)(2,1)S(1)}, bf16[1,32,512]{2,1,0:T(8,128)(2,1)S(1)}, u32[]{:S(2)}, u32[]{:S(2)}) collective-permute-start(bf16[1,32,512]{2,1,0:T(8,128)(2,1)S(1)} %get-tuple-element.159), channel_id=1, source_target_pairs={{0,1},{1,0},{2,3},{3,2},{4,5},{5,4},{6,7},{7,6},{8,9},{9,8},{10,11... | collective-permute-start | bytes 98312 | tf_op jit(solution)/shard_map/ppermute | solution.py:27
  56.1 2.6 %collective-permute-start.20 = (f32[8,1024]{1,0:T(8,128)S(1)}, f32[8,1024]{1,0:T(8,128)S(1)}, u32[]{:S(2)}, u32[]{:S(2)}) collective-permute-start(f32[8,1024]{1,0:T(8,128)S(1)} %get-tuple-element.156.small_ref), channel_id=1, source_target_pairs={{0,4},{4,0},{8,12},{12,8},{16,20},{20,16},{24,28},{28,24},{1,5},{5... | collective-permute-start | bytes 98312 | tf_op jit(solution)/shard_map/ppermute | solution.py:27
